TPU v7x, 128 devices: a whole 4x4x4 slice. The times are simulated.
128 devices in a mesh: row: 16 (over x, z_hi, core), col: 8 (over y, z_lo).
Axes of the slice: x: 4, y: 4, z: 4 (z_hi: 2, z_lo: 2; z = z_hi * 2 + z_lo), core: 2. Of those that a mesh axis runs over, the one named last changes fastest.
Arguments:
- inputs: bfloat16 [512, 8192], P('row', 'col'), may hold values from -6 to 6
- out_grad: bfloat16 [512, 8192], P('row', 'col'), may hold values from -6 to 6
- gate_weight: bfloat16 [8192, 28672], P('col', 'row'), may hold values from -0.0625 to 0.0625
- up_weight: bfloat16 [8192, 28672], P('col', 'row'), may hold values from -0.0625 to 0.0625
- down_weight: bfloat16 [28672, 8192], P('row', 'col'), may hold values from -0.03125 to 0.03125
Outputs:
- input_grad: bfloat16 [512, 8192], P('row', 'col')
- gate_weight_grad: bfloat16 [8192, 28672], P('col', 'row')
- up_weight_grad: bfloat16 [8192, 28672], P('col', 'row')
- down_weight_grad: bfloat16 [28672, 8192], P('row', 'col')
All inputs are finite; a program needn't handle non-finite values.
Results may differ from a plain program's by a relative error of at most 0.005.
Values may be sent and summed in bfloat16 or wider, within the bound.
No kernel may reach another device: no remote copies, remote signals or barrier semaphores. Data moves between devices by JAX's collectives and lax.ppermute only.
A program may use at most 128 MiB of HBM per device.

v0:
```python
import jax
import jax.numpy as jnp
from jax import lax
from jax.sharding import PartitionSpec as P


def contract_first(left, right):
    return lax.dot_general(
        left, right, (((0,), (0,)), ((), ())), preferred_element_type=jnp.float32
    )


def contract_last(left, right):
    return lax.dot_general(
        left, right, (((1,), (1,)), ((), ())), preferred_element_type=jnp.float32
    )


def swiglu_grads(gate, up, hidden_grad):
    sig = jax.nn.sigmoid(gate)
    hidden = (gate * sig * up).astype(jnp.bfloat16)
    gate_grad = (hidden_grad * up * sig * (1.0 + gate * (1.0 - sig))).astype(jnp.bfloat16)
    up_grad = (hidden_grad * gate * sig).astype(jnp.bfloat16)
    return (hidden, gate_grad, up_grad)


def per_device(inputs, out_grad, gate_weight, up_weight, down_weight):
    feat_rows, cot_rows = (
        lax.all_gather(inputs, "row", axis=0, tiled=True),
        lax.all_gather(out_grad, "row", axis=0, tiled=True),
    )
    gate_part = jnp.dot(feat_rows, gate_weight, preferred_element_type=jnp.float32)
    up_part = jnp.dot(feat_rows, up_weight, preferred_element_type=jnp.float32)
    hidden_share = lax.psum_scatter(
        contract_last(cot_rows, down_weight), "col", scatter_dimension=0, tiled=True
    )
    gate_share, up_share = (
        lax.psum_scatter(gate_part, "col", scatter_dimension=0, tiled=True),
        lax.psum_scatter(up_part, "col", scatter_dimension=0, tiled=True),
    )
    hidden, gate_grad, up_grad = swiglu_grads(gate_share, up_share, hidden_share)
    hidden, gate_grad, up_grad = (
        lax.all_gather(hidden, "col", axis=0, tiled=True),
        lax.all_gather(gate_grad, "col", axis=0, tiled=True),
        lax.all_gather(up_grad, "col", axis=0, tiled=True),
    )
    down_weight_grad = contract_first(hidden, cot_rows).astype(jnp.bfloat16)
    gate_weight_grad = contract_first(feat_rows, gate_grad).astype(jnp.bfloat16)
    up_weight_grad = contract_first(feat_rows, up_grad).astype(jnp.bfloat16)
    input_grad = lax.psum_scatter(
        contract_last(gate_grad, gate_weight) + contract_last(up_grad, up_weight),
        "row",
        scatter_dimension=0,
        tiled=True,
    ).astype(jnp.bfloat16)
    return (input_grad, gate_weight_grad, up_weight_grad, down_weight_grad)


def solution(mesh):
    return jax.shard_map(
        per_device,
        mesh=mesh,
        in_specs=(
            P("row", "col"),
            P("row", "col"),
            P("col", "row"),
            P("col", "row"),
            P("row", "col"),
        ),
        out_specs=(P("row", "col"), P("col", "row"), P("col", "row"), P("row", "col")),
        check_vma=False,
    )
```

profile of v0, /device:TPU:0, one launch (start us, length us, event | category | flops | bytes accessed | tf_op | source)
XLA Modules:
  0.0 589.2 jit_solution(10871683278324698681)
XLA Ops:
  7.2 0.0 all-gather.8.cloned.1.call-start
  7.2 0.7 all-gather.8.cloned.1.call-update
  7.9 0.0 all-gather.6.cloned.1.call-start
  7.9 0.7 all-gather.6.cloned.1.call-update
  8.6 0.0 reduce-scatter.7.cloned.1.call-start
  8.7 49.3 %all-gather.8.cloned.1.call-done = bf16[512,1024]{1,0:T(8,128)(2,1)} async-done(((bf16[32,1024]{1,0:T(8,128)(2,1)}), bf16[512,1024]{1,0:T(8,128)(2,1)}) %all-gather.8.cloned.1.call-update) | async-done | bytes 1048592 | tf_op jit(solution)/shard_map/all_gather | solution.py:29
  58.0 6.3 %fusion.3 = f32[512,1792]{1,0:T(8,128)} fusion(bf16[512,1024]{1,0:T(8,128)(2,1)} %all-gather.8.cloned.1.call-done, bf16[1024,1792]{1,0:T(8,128)(2,1)} %param.8), kind=kOutput, calls=%fused_computation.11 | convolution fusion | flops 1879048192 | bytes 8388608 | tf_op jit(solution)/shard_map/dot_general | solution.py:33
  64.2 0.0 copy-start.3
  64.2 0.0 reduce-scatter.7.cloned.1.call-update
  64.2 0.0 reduce-scatter.9.cloned.1.call-start
  64.3 1.1 copy-done.3
  65.4 5.9 %fusion.4 = f32[512,1792]{1,0:T(8,128)} fusion(bf16[512,1024]{1,0:T(8,128)(2,1)S(1)} %copy-done.3, bf16[1024,1792]{1,0:T(8,128)(2,1)} %param.7), kind=kOutput, calls=%fused_computation.12 | convolution fusion | flops 1879048192 | bytes 8388608 | tf_op jit(solution)/shard_map/dot_general | solution.py:32
  71.4 0.0 reduce-scatter.9.cloned.1.call-update
  71.4 0.0 reduce-scatter.5.cloned.1.call-start
  71.5 32.6 %all-gather.6.cloned.1.call-done = bf16[512,1024]{1,0:T(8,128)(2,1)} async-done(((bf16[32,1024]{1,0:T(8,128)(2,1)}), bf16[512,1024]{1,0:T(8,128)(2,1)}) %all-gather.6.cloned.1.call-update) | async-done | bytes 1048592 | tf_op jit(solution)/shard_map/all_gather | solution.py:30
  104.1 6.3 %fusion.2 = f32[512,1792]{1,0:T(8,128)} fusion(bf16[512,1024]{1,0:T(8,128)(2,1)} %all-gather.6.cloned.1.call-done, bf16[1792,1024]{1,0:T(8,128)(2,1)} %param.9), kind=kOutput, calls=%fused_computation.10 | convolution fusion | flops 1879048192 | bytes 8388608 | tf_op jit(solution)/shard_map/dot_general | solution.py:14
  110.4 0.0 reduce-scatter.5.cloned.1.call-update
  110.4 0.0 all-gather.10.cloned.1.call-start
  110.4 75.7 %reduce-scatter.7.cloned.1.call-done = f32[64,1792]{1,0:T(8,128)} async-done(((f32[512,1792]{1,0:T(8,128)}), f32[64,1792]{1,0:T(8,128)}) %reduce-scatter.7.cloned.1.call-update) | async-done | bytes 458768 | tf_op jit(solution)/shard_map/reduce_scatter | solution.py:39
  186.2 84.3 %reduce-scatter.9.cloned.1.call-done = f32[64,1792]{1,0:T(8,128)} async-done(((f32[512,1792]{1,0:T(8,128)}), f32[64,1792]{1,0:T(8,128)}) %reduce-scatter.9.cloned.1.call-update) | async-done | bytes 458768 | tf_op jit(solution)/shard_map/reduce_scatter | solution.py:38
  270.4 84.2 %reduce-scatter.5.cloned.1.call-done = f32[64,1792]{1,0:T(8,128)} async-done(((f32[512,1792]{1,0:T(8,128)}), f32[64,1792]{1,0:T(8,128)}) %reduce-scatter.5.cloned.1.call-update) | async-done | bytes 458768 | tf_op jit(solution)/shard_map/reduce_scatter | solution.py:34
  354.7 2.3 multiply_convert_fusion
  357.0 0.0 all-gather.10.cloned.1.call-update
  357.0 0.0 all-gather.12.cloned.1.call-start
  357.1 0.7 all-gather.12.cloned.1.call-update
  357.8 0.0 all-gather.14.cloned.1.call-start
  357.8 0.7 all-gather.14.cloned.1.call-update
  358.5 0.2 reduce-scatter.11.cloned.1.call-start
  358.8 46.6 %all-gather.10.cloned.1.call-done = bf16[512,1792]{1,0:T(8,128)(2,1)} async-done(((bf16[64,1792]{1,0:T(8,128)(2,1)}), bf16[512,1792]{1,0:T(8,128)(2,1)}) %all-gather.10.cloned.1.call-update) | async-done | bytes 1835024 | tf_op jit(solution)/shard_map/all_gather | solution.py:44
  405.4 6.0 %fusion.5 = f32[512,1024]{1,0:T(8,128)} fusion(bf16[512,1792]{1,0:T(8,128)(2,1)} %all-gather.10.cloned.1.call-done, bf16[1024,1792]{1,0:T(8,128)(2,1)} %param.7), kind=kOutput, calls=%fused_computation.13 | convolution fusion | flops 1879048192 | bytes 7602176 | tf_op jit(solution)/shard_map/dot_general | solution.py:14
  411.3 44.4 %all-gather.12.cloned.1.call-done = bf16[512,1792]{1,0:T(8,128)(2,1)} async-done(((bf16[64,1792]{1,0:T(8,128)(2,1)}), bf16[512,1792]{1,0:T(8,128)(2,1)}) %all-gather.12.cloned.1.call-update) | async-done | bytes 1835024 | tf_op jit(solution)/shard_map/all_gather | solution.py:45
  455.7 0.0 copy-start.1
  455.7 6.8 %convolution_add_fusion = f32[512,1024]{1,0:T(8,128)} fusion(f32[512,1024]{1,0:T(8,128)} %fusion.5, bf16[512,1792]{1,0:T(8,128)(2,1)} %all-gather.12.cloned.1.call-done, bf16[1024,1792]{1,0:T(8,128)(2,1)} %param.8), kind=kOutput, calls=%fused_computation.5 | convolution fusion | flops 1879572480 | bytes 9699328 | tf_op jit(solution)/shard_map/dot_general | solution.py:14
  462.5 0.0 reduce-scatter.11.cloned.1.call-update
  462.5 0.0 copy-done.1
  462.5 3.9 fusion.1
  466.5 0.0 copy-start
  466.5 6.0 %copy.10 = bf16[1024,1792]{1,0:T(8,128)(2,1)} copy(bf16[1024,1792]{0,1:T(8,128)(2,1)} %fusion.1) | data formatting | bytes 7340032
  472.5 0.0 copy-done
  472.5 3.9 fusion
  476.5 0.0 copy-start.2
  476.5 6.0 %copy.9 = bf16[1024,1792]{1,0:T(8,128)(2,1)} copy(bf16[1024,1792]{0,1:T(8,128)(2,1)} %fusion) | data formatting | bytes 7340032
  482.5 23.0 %all-gather.14.cloned.1.call-done = bf16[512,1792]{1,0:T(8,128)(2,1)} async-done(((bf16[64,1792]{1,0:T(8,128)(2,1)}), bf16[512,1792]{1,0:T(8,128)(2,1)}) %all-gather.14.cloned.1.call-update) | async-done | bytes 1835024 | tf_op jit(solution)/shard_map/all_gather | solution.py:43
  505.5 0.0 copy-done.2
  505.5 5.4 convolution_convert_fusion
  510.9 70.2 %reduce-scatter.11.cloned.1.call-done = f32[32,1024]{1,0:T(8,128)} async-done(((f32[512,1024]{1,0:T(8,128)}), f32[32,1024]{1,0:T(8,128)}) %reduce-scatter.11.cloned.1.call-update) | async-done | bytes 131088 | tf_op jit(solution)/shard_map/reduce_scatter | solution.py:50
  581.2 1.5 convert_element_type.29
Async XLA Ops:
  7.2 50.8 %all-gather.8.cloned.1.call-start = ((), (), s32[]{:S(2)}) async-start(), calls=%async_computation.6 | async-start | bytes 1114112 | tf_op jit(solution)/shard_map/all_gather | solution.py:29
  7.9 96.2 %all-gather.6.cloned.1.call-start = ((), (), s32[]{:S(2)}) async-start(), calls=%async_computation.4 | async-start | bytes 1114112 | tf_op jit(solution)/shard_map/all_gather | solution.py:30
  8.6 177.5 %reduce-scatter.7.cloned.1.call-start = ((), (), s32[]{:S(2)}) async-start(), calls=%async_computation.7 | async-start | bytes 4128768 | tf_op jit(solution)/shard_map/reduce_scatter | solution.py:39
  64.2 1.2 copy-start.3
  64.2 206.2 %reduce-scatter.9.cloned.1.call-start = ((), (), s32[]{:S(2)}) async-start(), calls=%async_computation.8 | async-start | bytes 4128768 | tf_op jit(solution)/shard_map/reduce_scatter | solution.py:38
  71.4 283.3 %reduce-scatter.5.cloned.1.call-start = ((), (), s32[]{:S(2)}) async-start(), calls=%async_computation.5 | async-start | bytes 4128768 | tf_op jit(solution)/shard_map/reduce_scatter | solution.py:34
  110.4 295.0 %all-gather.10.cloned.1.call-start = ((), (), s32[]{:S(2)}) async-start(), calls=%async_computation.9 | async-start | bytes 2064384 | tf_op jit(solution)/shard_map/all_gather | solution.py:44
  357.0 98.7 %all-gather.12.cloned.1.call-start = ((), (), s32[]{:S(2)}) async-start(), calls=%async_computation.10 | async-start | bytes 2064384 | tf_op jit(solution)/shard_map/all_gather | solution.py:45
  357.8 147.7 %all-gather.14.cloned.1.call-start = ((), (), s32[]{:S(2)}) async-start(), calls=%async_computation.12 | async-start | bytes 2064384 | tf_op jit(solution)/shard_map/all_gather | solution.py:43
  358.5 222.6 %reduce-scatter.11.cloned.1.call-start = ((), (), s32[]{:S(2)}) async-start(), calls=%async_computation.11 | async-start | bytes 2228224 | tf_op jit(solution)/shard_map/reduce_scatter | solution.py:50
  455.7 6.8 %copy-start.1 = (bf16[512,1792]{1,0:T(8,128)(2,1)S(1)}, bf16[512,1792]{1,0:T(8,128)(2,1)}, u32[]{:S(2)}) copy-start(bf16[512,1792]{1,0:T(8,128)(2,1)} %all-gather.12.cloned.1.call-done) | copy-start | bytes 5505028
  466.5 6.0 %copy-start = (bf16[512,1792]{1,0:T(8,128)(2,1)S(1)}, bf16[512,1792]{1,0:T(8,128)(2,1)}, u32[]{:S(2)}) copy-start(bf16[512,1792]{1,0:T(8,128)(2,1)} %all-gather.10.cloned.1.call-done) | copy-start | bytes 5505028
  476.5 29.0 %copy-start.2 = (bf16[512,1024]{1,0:T(8,128)(2,1)S(1)}, bf16[512,1024]{1,0:T(8,128)(2,1)}, u32[]{:S(2)}) copy-start(bf16[512,1024]{1,0:T(8,128)(2,1)} %all-gather.6.cloned.1.call-done) | copy-start | bytes 3145732
Sparse Core Ops, SparseCore 0:
  10.4 47.5 all-gather.7
  60.4 43.6 all-gather.5
  107.1 79.0 reduce-scatter.6
  189.0 81.3 reduce-scatter.8
  273.3 81.3 reduce-scatter.4
  357.2 48.1 all-gather.9
  407.6 48.0 all-gather.11
  457.3 48.0 all-gather.13
  509.4 71.6 reduce-scatter.10
where the time goes:
time: 590 us; the launch traced here: 589 us
  waiting for transfers between devices  513 us (87%)
  matrix products  44.6 us (8%)
  between operations  13.9 us (2%)
  local copies, waits for them, and re-layouts  13.2 us (2%)
    reduce_scatter x1, waiting for transfers between devices, per_device(): lax.psum_scatter(gate_part, 'col', scatter_dimension=0, tiled=True)  84.3 us
    reduce_scatter x1, waiting for transfers between devices, per_device(): lax.psum_scatter(contract_last(cot_rows, down_weight), 'col', scatter_dim...  84.2 us
    reduce_scatter x1, waiting for transfers between devices, per_device(): lax.psum_scatter(up_part, 'col', scatter_dimension=0, tiled=True)  75.7 us
    reduce_scatter x1, waiting for transfers between devices, per_device(): lax.psum_scatter(contract_last(gate_grad, gate_weight) + contract_last(up...  70.2 us
    all_gather x1, waiting for transfers between devices, per_device(): lax.all_gather(inputs, 'row', axis=0, tiled=True)  49.3 us
    all_gather x1, waiting for transfers between devices, per_device(): lax.all_gather(gate_grad, 'col', axis=0, tiled=True)  46.6 us
    all_gather x1, waiting for transfers between devices, per_device(): lax.all_gather(up_grad, 'col', axis=0, tiled=True)  44.4 us
    all_gather x1, waiting for transfers between devices, per_device(): lax.all_gather(out_grad, 'row', axis=0, tiled=True)  32.6 us
  transfers between devices with their start and end apart: 9, of which 9 were waited for; matrix products, arithmetic and copies ran while one was open for 10% of the time, Pallas kernels for 0%

commit v1 on v0

v1 whole, which is shorter than its diff:
```python
import functools

import jax
import jax.numpy as jnp
from jax import lax
from jax.experimental import pallas as pl
from jax.experimental.pallas import tpu as pltpu
from jax.sharding import PartitionSpec as P

BF16, F32 = jnp.bfloat16, jnp.float32
TILE = 256
VMEM = 48 * 1024 * 1024

COL = {"a": 2, "b": 6, "c": 1}
BIT = {"a": 4, "b": 2, "c": 1}
CORE, ZHI, XA, XB, XAB = 1, 2, 4, 12, 8


def swap(value, axis, mask):
    size = lax.axis_size(axis)
    return lax.ppermute(value, axis, [(i, i ^ mask) for i in range(size)])


def block_order(mine, dims):
    names = [
        sum(BIT[d] * ((place >> (2 - k)) & 1) for k, d in enumerate(dims))
        for place in range(8)
    ]
    return jnp.asarray(names, jnp.int32) ^ mine


def gather_rows(value):
    pair = jnp.concatenate([value, swap(value, "row", ZHI)], 0)
    half = jnp.concatenate(
        [pair] + [swap(pair, "row", mask) for mask in (XA, XB, XAB)], 0
    )
    both = jnp.concatenate([half, swap(half, "row", CORE)], 0)
    return both.reshape(8, -1, value.shape[1])


def cost(m, k, n, extra=0):
    return pl.CostEstimate(
        flops=2 * m * k * n,
        bytes_accessed=2 * (m * k + k * n + m * n) + extra,
        transcendentals=0,
    )


def reorder(order_ref, blocks_ref, out_ref):
    rows = blocks_ref.shape[1]
    for place in range(8):
        out_ref[place * rows : (place + 1) * rows, :] = blocks_ref[order_ref[place]]


def part_kernel(w_dim, order_ref, x_ref, w_ref, send_ref, keep_ref, x_scr):
    @pl.when(pl.program_id(0) == 0)
    def _():
        reorder(order_ref, x_ref, x_scr)

    part = lax.dot_general(
        x_scr[...], w_ref[...], (((1,), (w_dim,)), ((), ())), preferred_element_type=F32
    )
    half = part.shape[0] // 2
    keep_ref[...] = part[:half]
    send_ref[...] = part[half:].astype(BF16)


def partial_products(blocks, weight, w_dim, order):
    _, rows, depth = blocks.shape
    width = weight.shape[1 - w_dim]
    w_spec = (
        pl.BlockSpec((depth, TILE), lambda i, _: (0, i))
        if w_dim == 0
        else pl.BlockSpec((TILE, depth), lambda i, _: (i, 0))
    )
    half = pl.BlockSpec((4 * rows, TILE), lambda i, _: (0, i))
    return pl.pallas_call(
        functools.partial(part_kernel, w_dim),
        out_shape=(
            jax.ShapeDtypeStruct((4 * rows, width), BF16),
            jax.ShapeDtypeStruct((4 * rows, width), F32),
        ),
        grid_spec=pltpu.PrefetchScalarGridSpec(
            num_scalar_prefetch=1,
            grid=(width // TILE,),
            in_specs=[pl.BlockSpec((8, rows, depth), lambda i, _: (0, 0, 0)), w_spec],
            out_specs=(half, half),
            scratch_shapes=[pltpu.VMEM((8 * rows, depth), BF16)],
        ),
        compiler_params=pltpu.CompilerParams(vmem_limit_bytes=VMEM),
        cost_estimate=cost(8 * rows, depth, width),
    )(order, blocks, weight)


def sum_of_parts(send, keep, dims):
    far = swap(send, "col", COL[dims[0]])
    n = far.shape[0] // 4
    total = keep[: 2 * n] + far[: 2 * n].astype(F32)
    send = (keep[2 * n :] + far[2 * n :].astype(F32)).astype(BF16)
    far = swap(send, "col", COL[dims[1]])
    send = (total[n:] + far[n:].astype(F32)).astype(BF16)
    total = total[:n] + far[:n].astype(F32)
    return total + swap(send, "col", COL[dims[2]]).astype(F32)


def gather_blocks(block, dims):
    for dim in dims[:2]:
        block = jnp.concatenate([block, swap(block, "col", COL[dim])], 0)
    return block, swap(block, "col", COL[dims[2]])


def wide_kernel(near_ref, far_ref, xt_ref, out_ref):
    half = near_ref.shape[0]
    out_ref[...] = (
        jnp.dot(xt_ref[:, :half], near_ref[...], preferred_element_type=F32)
        + jnp.dot(xt_ref[:, half:], far_ref[...], preferred_element_type=F32)
    ).astype(BF16)


def wide_grad(halves, xt):
    half, width = halves[0].shape
    depth = xt.shape[0]
    return pl.pallas_call(
        wide_kernel,
        out_shape=jax.ShapeDtypeStruct((depth, width), BF16),
        grid=(width // TILE,),
        in_specs=[
            pl.BlockSpec((half, TILE), lambda i: (0, i)),
            pl.BlockSpec((half, TILE), lambda i: (0, i)),
            pl.BlockSpec(xt.shape, lambda i: (0, 0)),
        ],
        out_specs=pl.BlockSpec((depth, TILE), lambda i: (0, i)),
        compiler_params=pltpu.CompilerParams(vmem_limit_bytes=VMEM),
        cost_estimate=cost(depth, 2 * half, width),
    )(*halves, xt)


def tall_kernel(order_ref, near_ref, far_ref, g_ref, out_ref, g_scr):
    @pl.when(pl.program_id(0) == 0)
    def _():
        reorder(order_ref, g_ref, g_scr)

    half = near_ref.shape[0]
    first = (((0,), (0,)), ((), ()))
    out_ref[...] = (
        lax.dot_general(near_ref[...], g_scr[:half], first, preferred_element_type=F32)
        + lax.dot_general(far_ref[...], g_scr[half:], first, preferred_element_type=F32)
    ).astype(BF16)


def tall_grad(halves, g_blocks, order):
    half, width = halves[0].shape
    depth = g_blocks.shape[2]
    return pl.pallas_call(
        tall_kernel,
        out_shape=jax.ShapeDtypeStruct((width, depth), BF16),
        grid_spec=pltpu.PrefetchScalarGridSpec(
            num_scalar_prefetch=1,
            grid=(width // TILE,),
            in_specs=[
                pl.BlockSpec((half, TILE), lambda i, _: (0, i)),
                pl.BlockSpec((half, TILE), lambda i, _: (0, i)),
                pl.BlockSpec(g_blocks.shape, lambda i, _: (0, 0, 0)),
            ],
            out_specs=pl.BlockSpec((TILE, depth), lambda i, _: (i, 0)),
            scratch_shapes=[pltpu.VMEM((2 * half, depth), BF16)],
        ),
        compiler_params=pltpu.CompilerParams(vmem_limit_bytes=VMEM),
        cost_estimate=cost(width, 2 * half, depth),
    )(order, *halves, g_blocks)


def input_kernel(
    gate_order, up_order, gn_ref, gf_ref, un_ref, uf_ref, wg_ref, wu_ref, keep_ref, send_ref, scr
):
    last = (((1,), (1,)), ((), ()))
    rows = scr.shape[1]

    def place(order, offset, rows_ref, w_ref, add):
        part = lax.dot_general(rows_ref[...], w_ref[...], last, preferred_element_type=F32)
        for k in range(4):
            piece = part[k * rows : (k + 1) * rows]
            where = order[offset + k]
            scr[where] = scr[where] + piece if add else piece

    place(gate_order, 0, gn_ref, wg_ref, False)
    place(gate_order, 4, gf_ref, wg_ref, False)
    place(up_order, 0, un_ref, wu_ref, True)
    place(up_order, 4, uf_ref, wu_ref, True)
    keep_ref[...] = scr[:4].reshape(keep_ref.shape)
    send_ref[...] = scr[4:].reshape(send_ref.shape)


def input_parts(gate_halves, gate_order, up_halves, up_order, gate_weight, up_weight):
    half, width = gate_halves[0].shape
    depth = gate_weight.shape[0]
    whole = pl.BlockSpec((half, width), lambda i, *_: (0, 0))
    w_spec = pl.BlockSpec((TILE, width), lambda i, *_: (i, 0))
    out = pl.BlockSpec((half, TILE), lambda i, *_: (0, i))
    shape = jax.ShapeDtypeStruct((half, depth), F32)
    return pl.pallas_call(
        input_kernel,
        out_shape=(shape, shape),
        grid_spec=pltpu.PrefetchScalarGridSpec(
            num_scalar_prefetch=2,
            grid=(depth // TILE,),
            in_specs=[whole] * 4 + [w_spec] * 2,
            out_specs=(out, out),
            scratch_shapes=[pltpu.VMEM((8, half // 4, TILE), F32)],
        ),
        compiler_params=pltpu.CompilerParams(vmem_limit_bytes=VMEM),
        cost_estimate=cost(2 * half, 2 * width, depth),
    )(gate_order, up_order, *gate_halves, *up_halves, gate_weight, up_weight)


def sum_rows(keep, send):
    total = keep + swap(send, "row", CORE)
    n = total.shape[0] // 4
    parts = [total[:n]]
    for k, mask in enumerate((XA, XB, XAB), 1):
        parts.append(swap(total[k * n : (k + 1) * n].astype(BF16), "row", mask).astype(F32))
    pair = (parts[0] + parts[1]) + (parts[2] + parts[3])
    return pair[: n // 2] + swap(pair[n // 2 :], "row", ZHI)


def swiglu_grads(gate, up, hidden_grad):
    sig = jax.nn.sigmoid(gate)
    hidden = (gate * sig * up).astype(BF16)
    gate_grad = (hidden_grad * up * sig * (1.0 + gate * (1.0 - sig))).astype(BF16)
    up_grad = (hidden_grad * gate * sig).astype(BF16)
    return hidden, gate_grad, up_grad


def ordered(blocks, order):
    return jnp.concatenate(
        [lax.dynamic_index_in_dim(blocks, order[s], 0, keepdims=False) for s in range(8)], 0
    )


def per_device(inputs, out_grad, gate_weight, up_weight, down_weight):
    col = lax.axis_index("col")
    y_high, y_low = (col >> 2) & 1, (col >> 1) & 1
    mine = (y_high ^ y_low) * BIT["a"] + y_high * BIT["b"] + (col & 1) * BIT["c"]
    mine = mine.astype(jnp.int32)

    x = gather_rows(inputs)
    g = gather_rows(out_grad)

    gate = sum_of_parts(*partial_products(x, gate_weight, 0, block_order(mine, "abc")), "abc")
    up = sum_of_parts(*partial_products(x, up_weight, 0, block_order(mine, "bca")), "bca")
    hidden_grad = sum_of_parts(
        *partial_products(g, down_weight, 1, block_order(mine, "cab")), "cab"
    )
    hidden, gate_grad, up_grad = swiglu_grads(gate, up, hidden_grad)

    gate_order = block_order(mine, "cba")
    up_order = block_order(mine, "acb")
    hidden_order = block_order(mine, "bac")
    gate_halves = gather_blocks(gate_grad, "abc")
    up_halves = gather_blocks(up_grad, "bca")
    hidden_halves = gather_blocks(hidden, "cab")

    keep, send = input_parts(
        gate_halves, gate_order, up_halves, up_order, gate_weight, up_weight
    )
    input_grad = sum_rows(keep, send).astype(BF16)
    gate_weight_grad = wide_grad(gate_halves, ordered(x, gate_order).T)
    up_weight_grad = wide_grad(up_halves, ordered(x, up_order).T)
    down_weight_grad = tall_grad(hidden_halves, g, hidden_order)
    return (input_grad, gate_weight_grad, up_weight_grad, down_weight_grad)


def solution(mesh):
    return jax.shard_map(
        per_device,
        mesh=mesh,
        in_specs=(
            P("row", "col"),
            P("row", "col"),
            P("col", "row"),
            P("col", "row"),
            P("row", "col"),
        ),
        out_specs=(P("row", "col"), P("col", "row"), P("col", "row"), P("row", "col")),
        check_vma=False,
    )
```

time: 590 us -> 231 us (0.39)
  waiting for transfers between devices: 513 us -> 72.5 us
  Pallas kernels: 0 us -> 48.3 us
  matrix products: 44.6 us -> 0 us
  starting transfers between devices: 0.54 us -> 39.8 us
  local copies, waits for them, and re-layouts: 13.2 us -> 31.4 us
  between operations: 13.9 us -> 31.3 us
    reduce_scatter x4 -> x0, waiting for transfers between devices: 314 us -> none  [the longest x1 84.3 us: per_device(): lax.psum_scatter(gate_part, 'col', scatter_dimension=0, tiled=True)]
    all_gather x5 -> x0, waiting for transfers between devices: 196 us -> none  [the longest x1 49.3 us: per_device(): lax.all_gather(inputs, 'row', axis=0, tiled=True)]
    ppermute x0 -> x33, waiting for transfers between devices: none -> 72.5 us  [swap(): return lax.ppermute(value, axis, [(i, i ^ mask) for i in range(size)])]
    pallas_call x0 -> x7, Pallas kernels: none -> 48.3 us  [the longest x3 20.3 us: partial_products(): pl.pallas_call(functools.partial(part_kernel, w_dim), out_shape=(jax.Shap...]
    dot_general x8 -> x0, matrix products: 44.6 us -> none  [the longest x3 19.1 us: contract_last(): lax.dot_general(left, right, (((1,), (1,)), ((), ())), preferred_element_...]
    ppermute x0 -> x33, starting transfers between devices: none -> 39.8 us  [swap(): return lax.ppermute(value, axis, [(i, i ^ mask) for i in range(size)])]
    dynamic_slice x0 -> x17, local copies, waits for them, and re-layouts: none -> 18.3 us  [ordered(): lax.dynamic_index_in_dim(blocks, order[s], 0, keepdims=False)]
    unnamed x10 -> x34, local copies, waits for them, and re-layouts: 13.2 us -> 5.67 us
  transfers between devices with their start and end apart: 9 -> 33, of which waited for: 9 -> 17; matrix products, arithmetic and copies ran while one was open for 10% -> 15% of each run, Pallas kernels for 0% -> 21%
where the time goes in v1:
time: 231 us; the launch traced here: 229 us
  waiting for transfers between devices  72.5 us (31%)
  Pallas kernels  48.3 us (21%)
  starting transfers between devices  39.8 us (17%)
  local copies, waits for them, and re-layouts  31.4 us (14%)
  between operations  31.3 us (14%)
  other arithmetic  5.43 us (2%)
    ppermute x33, waiting for transfers between devices, swap(): return lax.ppermute(value, axis, [(i, i ^ mask) for i in range(size)])  72.5 us
    ppermute x33, starting transfers between devices, swap(): return lax.ppermute(value, axis, [(i, i ^ mask) for i in range(size)])  39.8 us
    pallas_call x3, Pallas kernels, partial_products(): pl.pallas_call(functools.partial(part_kernel, w_dim), out_shape=(jax.Shap...  20.3 us
    dynamic_slice x17, local copies, waits for them, and re-layouts, ordered(): lax.dynamic_index_in_dim(blocks, order[s], 0, keepdims=False)  18.3 us
    pallas_call x2, Pallas kernels, wide_grad(): pl.pallas_call(wide_kernel, out_shape=jax.ShapeDtypeStruct((depth, width)...  13.6 us
    pallas_call x1, Pallas kernels, input_parts(): pl.pallas_call(input_kernel, out_shape=(shape, shape), grid_spec=pltpu.Pr...  8.62 us
    pallas_call x1, Pallas kernels, tall_grad(): pl.pallas_call(tall_kernel, out_shape=jax.ShapeDtypeStruct((width, depth)...  5.73 us
    unnamed x34, local copies, waits for them, and re-layouts  5.67 us
  transfers between devices with their start and end apart: 33, of which 17 were waited for; matrix products, arithmetic and copies ran while one was open for 15% of the time, Pallas kernels for 21%

profile of v1, /device:TPU:0, one launch (start us, length us, event | category | flops | bytes accessed | tf_op | source)
XLA Modules:
  0.0 228.7 jit_solution(16363200929279558042)
XLA Ops:
  0.6 4.0 %collective-permute-start.8 = (bf16[32,1024]{1,0:T(8,128)(2,1)}, bf16[32,1024]{1,0:T(8,128)(2,1)S(1)}, u32[]{:S(2)}, u32[]{:S(2)}) collective-permute-start(bf16[32,1024]{1,0:T(8,128)(2,1)} %param.11), channel_id=1, source_target_pairs={{0,16},{8,24},{16,0},{24,8},{32,48},{40,56},{48,32},{56,40},{64,80... | collective-permute-start | bytes 196616 | tf_op jit(solution)/shard_map/ppermute | solution.py:21
  4.7 1.5 constant_dynamic-update-slice_fusion.19
  6.2 0.9 collective-permute-done.8
  7.8 1.5 collective-permute-start.9
  9.3 3.5 %collective-permute-start = (bf16[32,1024]{1,0:T(8,128)(2,1)}, bf16[32,1024]{1,0:T(8,128)(2,1)S(1)}, u32[]{:S(2)}, u32[]{:S(2)}) collective-permute-start(bf16[32,1024]{1,0:T(8,128)(2,1)} %param.12), channel_id=1, source_target_pairs={{0,16},{8,24},{16,0},{24,8},{32,48},{40,56},{48,32},{56,40},{64,80... | collective-permute-start | bytes 196616 | tf_op jit(solution)/shard_map/ppermute | solution.py:21
  12.8 2.1 collective-permute-start.10
  14.9 0.9 constant_dynamic-update-slice_fusion.6
  17.2 3.2 %collective-permute-done.10 = bf16[64,1024]{1,0:T(8,128)(2,1)S(1)} collective-permute-done((bf16[64,1024]{1,0:T(8,128)(2,1)S(1)}, bf16[64,1024]{1,0:T(8,128)(2,1)S(1)}, u32[]{:S(2)}, u32[]{:S(2)}) %collective-permute-start.10) | collective-permute-done | bytes 131104 | tf_op jit(solution)/shard_map/ppermute | solution.py:21
  21.1 1.2 collective-permute-done.11
  24.3 2.9 %collective-permute-start.3 = (bf16[64,1024]{1,0:T(8,128)(2,1)S(1)}, bf16[64,1024]{1,0:T(8,128)(2,1)S(1)}, u32[]{:S(2)}, u32[]{:S(2)}) collective-permute-start(bf16[64,1024]{1,0:T(8,128)(2,1)S(1)} %get-tuple-element.70), channel_id=1, source_target_pairs={{0,64},{8,72},{16,80},{24,88},{32,96},{40,104},{48,112},{56,120},{... | collective-permute-start | bytes 393224 | tf_op jit(solution)/shard_map/ppermute | solution.py:21
  27.2 2.2 collective-permute-done.1
  29.4 3.9 %collective-permute-done.2 = bf16[64,1024]{1,0:T(8,128)(2,1)S(1)} collective-permute-done((bf16[64,1024]{1,0:T(8,128)(2,1)S(1)}, bf16[64,1024]{1,0:T(8,128)(2,1)S(1)}, u32[]{:S(2)}, u32[]{:S(2)}) %collective-permute-start.2) | collective-permute-done | bytes 131104 | tf_op jit(solution)/shard_map/ppermute | solution.py:21
  33.4 6.7 %shard_map.139 = (bf16[256,1792]{1,0:T(8,128)(2,1)S(1)}, f32[256,1792]{1,0:T(8,128)S(1)}) custom-call(s32[8]{0:T(128)S(1)} %get-tuple-element.91.order_ref, bf16[8,64,1024]{2,1,0:T(8,128)(2,1)S(1)} %bitcast.36, bf16[1024,1792]{1,0:T(8,128)(2,1)} %wu_ref.1), custom_call_target="tpu_custom_call" | custom-call | flops 1879048192 | bytes 6553600 | tf_op jit(solution)/shard_map/pallas_call | solution.py:77
  40.2 3.1 %collective-permute-start.13 = (bf16[256,1792]{1,0:T(8,128)(2,1)S(1)}, bf16[256,1792]{1,0:T(8,128)(2,1)S(1)}, u32[]{:S(2)}, u32[]{:S(2)}) collective-permute-start(bf16[256,1792]{1,0:T(8,128)(2,1)S(1)} %get-tuple-element.15), channel_id=1, source_target_pairs={{0,6},{1,7},{2,4},{3,5},{4,2},{5,3},{6,0},{7,1},{8,14},{9,15},{10,... | collective-permute-start | bytes 2752520 | tf_op jit(solution)/shard_map/ppermute | solution.py:21
  43.4 6.7 %shard_map.140 = (bf16[256,1792]{1,0:T(8,128)(2,1)S(1)}, f32[256,1792]{1,0:T(8,128)S(1)}) custom-call(s32[8]{0:T(128)S(1)} %get-tuple-element.90.order_ref, bf16[8,64,1024]{2,1,0:T(8,128)(2,1)S(1)} %bitcast.37, bf16[1024,1792]{1,0:T(8,128)(2,1)} %wg_ref.1), custom_call_target="tpu_custom_call" | custom-call | flops 1879048192 | bytes 6553600 | tf_op jit(solution)/shard_map/pallas_call | solution.py:77
  50.4 6.9 %shard_map.138 = (bf16[256,1792]{1,0:T(8,128)(2,1)S(1)}, f32[256,1792]{1,0:T(8,128)S(1)}) custom-call(s32[8]{0:T(128)S(1)} %broadcast_xor_fusion.2.order_ref, bf16[8,64,1024]{2,1,0:T(8,128)(2,1)S(1)} %bitcast.41, bf16[1792,1024]{1,0:T(8,128)(2,1)} %w_ref.3), custom_call_target="tpu_custom_call" | custom-call | flops 1879048192 | bytes 6553600 | tf_op jit(solution)/shard_map/pallas_call | solution.py:77
  57.3 1.1 collective-permute-start.5
  58.4 4.8 %collective-permute-done.13 = bf16[256,1792]{1,0:T(8,128)(2,1)S(1)} collective-permute-done((bf16[256,1792]{1,0:T(8,128)(2,1)S(1)}, bf16[256,1792]{1,0:T(8,128)(2,1)S(1)}, u32[]{:S(2)}, u32[]{:S(2)}) %collective-permute-start.13) | collective-permute-done | bytes 917536 | tf_op jit(solution)/shard_map/ppermute | solution.py:21
  63.3 1.1 collective-permute-start.14
  64.4 8.5 %collective-permute-done.16 = bf16[256,1792]{1,0:T(8,128)(2,1)S(1)} collective-permute-done((bf16[256,1792]{1,0:T(8,128)(2,1)S(1)}, bf16[256,1792]{1,0:T(8,128)(2,1)S(1)}, u32[]{:S(2)}, u32[]{:S(2)}) %collective-permute-start.16) | collective-permute-done | bytes 917536 | tf_op jit(solution)/shard_map/ppermute | solution.py:21
  73.4 7.2 %collective-permute-done.5 = bf16[256,1792]{1,0:T(8,128)(2,1)S(1)} collective-permute-done((bf16[256,1792]{1,0:T(8,128)(2,1)S(1)}, bf16[256,1792]{1,0:T(8,128)(2,1)S(1)}, u32[]{:S(2)}, u32[]{:S(2)}) %collective-permute-start.5) | collective-permute-done | bytes 917536 | tf_op jit(solution)/shard_map/ppermute | solution.py:21
  80.7 2.0 collective-permute-start.6
  82.7 7.2 %collective-permute-done.14 = bf16[128,1792]{1,0:T(8,128)(2,1)S(1)} collective-permute-done((bf16[128,1792]{1,0:T(8,128)(2,1)S(1)}, bf16[128,1792]{1,0:T(8,128)(2,1)S(1)}, u32[]{:S(2)}, u32[]{:S(2)}) %collective-permute-start.14) | collective-permute-done | bytes 458784 | tf_op jit(solution)/shard_map/ppermute | solution.py:21
  89.9 1.8 collective-permute-start.15
  91.7 1.1 collective-permute-start.18
  93.2 4.0 %collective-permute-done.15 = bf16[64,1792]{1,0:T(8,128)(2,1)S(1)} collective-permute-done((bf16[64,1792]{1,0:T(8,128)(2,1)S(1)}, bf16[64,1792]{1,0:T(8,128)(2,1)S(1)}, u32[]{:S(2)}, u32[]{:S(2)}) %collective-permute-start.15) | collective-permute-done | bytes 229408 | tf_op jit(solution)/shard_map/ppermute | solution.py:21
  97.1 1.3 collective-permute-done.18
  98.4 2.1 collective-permute-done.7
  101.4 5.6 %collective-permute-done.19 = bf16[64,1792]{1,0:T(8,128)(2,1)S(1)} collective-permute-done((bf16[64,1792]{1,0:T(8,128)(2,1)S(1)}, bf16[64,1792]{1,0:T(8,128)(2,1)S(1)}, u32[]{:S(2)}, u32[]{:S(2)}) %collective-permute-start.19) | collective-permute-done | bytes 229408 | tf_op jit(solution)/shard_map/ppermute | solution.py:21
  107.5 1.5 collective-permute-done.22
  109.0 1.1 collective-permute-start.23
  110.1 8.1 %collective-permute-done.20 = bf16[128,1792]{1,0:T(8,128)(2,1)S(1)} collective-permute-done((bf16[128,1792]{1,0:T(8,128)(2,1)S(1)}, bf16[128,1792]{1,0:T(8,128)(2,1)S(1)}, u32[]{:S(2)}, u32[]{:S(2)}) %collective-permute-start.20) | collective-permute-done | bytes 458784 | tf_op jit(solution)/shard_map/ppermute | solution.py:21
  118.3 1.1 collective-permute-start.21
  119.4 1.1 collective-permute-start.24
  131.3 1.1 collective-permute-start.30
  132.4 7.5 %collective-permute-done.21.gf_ref.far_ref = bf16[256,1792]{1,0:T(8,128)(2,1)} collective-permute-done((bf16[256,1792]{1,0:T(8,128)(2,1)S(1)}, bf16[256,1792]{1,0:T(8,128)(2,1)}, u32[]{:S(2)}, u32[]{:S(2)}) %collective-permute-start.21) | collective-permute-done | bytes 917536 | tf_op jit(solution)/shard_map/ppermute | solution.py:21
  139.9 1.2 copy-done.3
  141.1 8.6 %shard_map.141 = (f32[256,1024]{1,0:T(8,128)S(1)}, f32[256,1024]{1,0:T(8,128)}) custom-call(s32[8]{0:T(128)S(1)} %get-tuple-element.93.gate_order, s32[8]{0:T(128)S(1)} %get-tuple-element.92.up_order, bf16[256,1792]{1,0:T(8,128)(2,1)S(1)} %copy-done.3, bf16[256,1792]{1,0:T(8,128)(2,1)} %collective-permute-done.21.gf_ref.far_ref, ...), custom_call_target="tpu_custom_call" | custom-call | flops 3758096384 | bytes 12058624 | tf_op jit(solution)/shard_map/pallas_call | solution.py:201
  150.6 2.3 collective-permute-start.31
  173.7 1.1 constant_dynamic-slice_fusion
  174.8 1.1 copy.15
  175.9 1.1 copy.16
  177.0 1.1 copy.17
  178.1 1.1 copy.18
  179.2 1.8 copy.19
  180.9 1.8 copy.20
  182.7 1.7 copy.21
  184.4 0.8 copy.22
  186.1 0.8 copy.24
  187.8 0.9 copy.26
  188.7 0.9 copy.27
  189.5 0.8 copy.28
  190.4 0.9 copy.29
  191.3 0.8 copy.30
  192.1 2.5 %concatenate.59 = bf16[512,1024]{0,1:T(8,128)(2,1)S(1)} concatenate(bf16[64,1024]{0,1:T(8,128)(2,1)S(1)} %bitcast.43, bf16[64,1024]{0,1:T(8,128)(2,1)S(1)} %bitcast.44, bf16[64,1024]{0,1:T(8,128)(2,1)S(1)} %bitcast.45, bf16[64,1024]{0,1:T(8,128)(2,1)S(1)} %bitcast.46, bf16[64,1024]{0,1:T(8,128)(2,1)} %bitcast.47, bf16[64,1024]{0,1:T(8,128)(2,1)} %bitcast.48, ...), dimensions={0} | concatenate | bytes 2097152 | tf_op jit(solution)/shard_map/concatenate | solution.py:235
  194.6 2.7 %concatenate.60 = bf16[512,1024]{0,1:T(8,128)(2,1)S(1)} concatenate(bf16[64,1024]{0,1:T(8,128)(2,1)} %bitcast.51, bf16[64,1024]{0,1:T(8,128)(2,1)} %bitcast.52, bf16[64,1024]{0,1:T(8,128)(2,1)} %bitcast.53, bf16[64,1024]{0,1:T(8,128)(2,1)} %bitcast.54, bf16[64,1024]{0,1:T(8,128)(2,1)} %bitcast.55, bf16[64,1024]{0,1:T(8,128)(2,1)} %bitcast.56, bf16[64,1024]{0,1:T(8,128)(2,1)} %bitcast.57, ...), dimensions={0} | concatenate | bytes 2097152 | tf_op jit(solution)/shard_map/concatenate | solution.py:235
  197.4 1.2 pad_maximum_fusion.2.near_ref
  199.1 6.7 %shard_map.142 = bf16[1024,1792]{1,0:T(8,128)(2,1)} custom-call(bf16[256,1792]{1,0:T(8,128)(2,1)S(1)} %copy-done.4, bf16[256,1792]{1,0:T(8,128)(2,1)} %collective-permute-done.21.gf_ref.far_ref, bf16[1024,512]{1,0:T(8,128)(2,1)S(1)} %bitcast.40), custom_call_target="tpu_custom_call" | custom-call | flops 1879048192 | bytes 6553600 | tf_op jit(solution)/shard_map/pallas_call | solution.py:123
  205.8 1.5 fusion.8
  207.4 2.9 %collective-permute-start.27 = (bf16[64,1024]{1,0:T(8,128)(2,1)S(1)}, bf16[64,1024]{1,0:T(8,128)(2,1)S(1)}, u32[]{:S(2)}, u32[]{:S(2)}) collective-permute-start(bf16[64,1024]{1,0:T(8,128)(2,1)S(1)} %get-tuple-element.49), channel_id=1, source_target_pairs={{0,96},{8,104},{16,112},{24,120},{32,64},{40,72},{48,80},{56,88},{... | collective-permute-start | bytes 393224 | tf_op jit(solution)/shard_map/ppermute | solution.py:21
  210.9 6.8 %shard_map.143 = bf16[1024,1792]{1,0:T(8,128)(2,1)} custom-call(bf16[256,1792]{1,0:T(8,128)(2,1)S(1)} %copy-done.1, bf16[256,1792]{1,0:T(8,128)(2,1)} %collective-permute-done.24.uf_ref.far_ref, bf16[1024,512]{1,0:T(8,128)(2,1)S(1)} %bitcast.39), custom_call_target="tpu_custom_call" | custom-call | flops 1879048192 | bytes 6553600 | tf_op jit(solution)/shard_map/pallas_call | solution.py:123
  217.9 1.2 collective-permute-start.29
  219.1 3.3 %collective-permute-done.32.far_ref = bf16[256,1792]{1,0:T(8,128)(2,1)S(1)} collective-permute-done((bf16[256,1792]{1,0:T(8,128)(2,1)S(1)}, bf16[256,1792]{1,0:T(8,128)(2,1)S(1)}, u32[]{:S(2)}, u32[]{:S(2)}) %collective-permute-start.32) | collective-permute-done | bytes 917536 | tf_op jit(solution)/shard_map/ppermute | solution.py:21
  222.4 5.7 %shard_map.144 = bf16[1792,1024]{1,0:T(8,128)(2,1)} custom-call(s32[8]{0:T(128)S(1)} %broadcast_xor_fusion.order_ref, bf16[256,1792]{1,0:T(8,128)(2,1)S(1)} %pad_maximum_fusion.2.near_ref, bf16[256,1792]{1,0:T(8,128)(2,1)S(1)} %collective-permute-done.32.far_ref, bf16[8,64,1024]{2,1,0:T(8,128)(2,1)S(1)} %bitcast.42), custom_call_target="tpu_custom_call" | custom-call | flops 1879048192 | bytes 6553600 | tf_op jit(solution)/shard_map/pallas_call | solution.py:154
  (90 shorter events, 13.7 us)
Async XLA Ops:
  0.6 23.7 %copy-start.10 = (s32[8]{0:T(128)S(1)}, s32[8]{0:T(128)}, u32[]{:S(2)}) copy-start(s32[8]{0:T(128)} %constant.60.clone) | copy-start | bytes 100
  0.6 6.5 %collective-permute-start.8 = (bf16[32,1024]{1,0:T(8,128)(2,1)}, bf16[32,1024]{1,0:T(8,128)(2,1)S(1)}, u32[]{:S(2)}, u32[]{:S(2)}) collective-permute-start(bf16[32,1024]{1,0:T(8,128)(2,1)} %param.11), channel_id=1, source_target_pairs={{0,16},{8,24},{16,0},{24,8},{32,48},{40,56},{48,32},{56,40},{64,80... | collective-permute-start | bytes 196616 | tf_op jit(solution)/shard_map/ppermute | solution.py:21
  7.8 8.7 %collective-permute-start.9 = (bf16[64,1024]{1,0:T(8,128)(2,1)S(1)}, bf16[64,1024]{1,0:T(8,128)(2,1)S(1)}, u32[]{:S(2)}, u32[]{:S(2)}) collective-permute-start(bf16[64,1024]{1,0:T(8,128)(2,1)S(1)} %get-tuple-element.64), channel_id=1, source_target_pairs={{0,32},{8,40},{16,48},{24,56},{32,0},{40,8},{48,16},{56,24},{64,96... | collective-permute-start | bytes 393224 | tf_op jit(solution)/shard_map/ppermute | solution.py:21
  9.3 13.7 %collective-permute-start = (bf16[32,1024]{1,0:T(8,128)(2,1)}, bf16[32,1024]{1,0:T(8,128)(2,1)S(1)}, u32[]{:S(2)}, u32[]{:S(2)}) collective-permute-start(bf16[32,1024]{1,0:T(8,128)(2,1)} %param.12), channel_id=1, source_target_pairs={{0,16},{8,24},{16,0},{24,8},{32,48},{40,56},{48,32},{56,40},{64,80... | collective-permute-start | bytes 196616 | tf_op jit(solution)/shard_map/ppermute | solution.py:21
  12.8 7.6 %collective-permute-start.10 = (bf16[64,1024]{1,0:T(8,128)(2,1)S(1)}, bf16[64,1024]{1,0:T(8,128)(2,1)S(1)}, u32[]{:S(2)}, u32[]{:S(2)}) collective-permute-start(bf16[64,1024]{1,0:T(8,128)(2,1)S(1)} %get-tuple-element.64), channel_id=1, source_target_pairs={{0,96},{8,104},{16,112},{24,120},{32,64},{40,72},{48,80},{56,88},{... | collective-permute-start | bytes 393224 | tf_op jit(solution)/shard_map/ppermute | solution.py:21
  15.8 6.6 %collective-permute-start.11 = (bf16[64,1024]{1,0:T(8,128)(2,1)S(1)}, bf16[64,1024]{1,0:T(8,128)(2,1)S(1)}, u32[]{:S(2)}, u32[]{:S(2)}) collective-permute-start(bf16[64,1024]{1,0:T(8,128)(2,1)S(1)} %get-tuple-element.64), channel_id=1, source_target_pairs={{0,64},{8,72},{16,80},{24,88},{32,96},{40,104},{48,112},{56,120},{... | collective-permute-start | bytes 393224 | tf_op jit(solution)/shard_map/ppermute | solution.py:21
  23.0 10.4 %collective-permute-start.12 = (bf16[256,1024]{1,0:T(8,128)(2,1)}, bf16[256,1024]{1,0:T(8,128)(2,1)S(1)}, u32[]{:S(2)}, u32[]{:S(2)}) collective-permute-start(bf16[256,1024]{1,0:T(8,128)(2,1)} %get-tuple-element.50), channel_id=1, source_target_pairs={{0,8},{8,0},{16,24},{24,16},{32,40},{40,32},{48,56},{56,48},{64,72... | collective-permute-start | bytes 1572872 | tf_op jit(solution)/shard_map/ppermute | solution.py:21
  23.0 6.4 %collective-permute-start.1 = (bf16[64,1024]{1,0:T(8,128)(2,1)S(1)}, bf16[64,1024]{1,0:T(8,128)(2,1)S(1)}, u32[]{:S(2)}, u32[]{:S(2)}) collective-permute-start(bf16[64,1024]{1,0:T(8,128)(2,1)S(1)} %get-tuple-element.70), channel_id=1, source_target_pairs={{0,32},{8,40},{16,48},{24,56},{32,0},{40,8},{48,16},{56,24},{64,96... | collective-permute-start | bytes 393224 | tf_op jit(solution)/shard_map/ppermute | solution.py:21
  23.7 9.6 %collective-permute-start.2 = (bf16[64,1024]{1,0:T(8,128)(2,1)S(1)}, bf16[64,1024]{1,0:T(8,128)(2,1)S(1)}, u32[]{:S(2)}, u32[]{:S(2)}) collective-permute-start(bf16[64,1024]{1,0:T(8,128)(2,1)S(1)} %get-tuple-element.70), channel_id=1, source_target_pairs={{0,96},{8,104},{16,112},{24,120},{32,64},{40,72},{48,80},{56,88},{... | collective-permute-start | bytes 393224 | tf_op jit(solution)/shard_map/ppermute | solution.py:21
  24.3 18.9 %collective-permute-start.3 = (bf16[64,1024]{1,0:T(8,128)(2,1)S(1)}, bf16[64,1024]{1,0:T(8,128)(2,1)S(1)}, u32[]{:S(2)}, u32[]{:S(2)}) collective-permute-start(bf16[64,1024]{1,0:T(8,128)(2,1)S(1)} %get-tuple-element.70), channel_id=1, source_target_pairs={{0,64},{8,72},{16,80},{24,88},{32,96},{40,104},{48,112},{56,120},{... | collective-permute-start | bytes 393224 | tf_op jit(solution)/shard_map/ppermute | solution.py:21
  40.2 23.0 %collective-permute-start.13 = (bf16[256,1792]{1,0:T(8,128)(2,1)S(1)}, bf16[256,1792]{1,0:T(8,128)(2,1)S(1)}, u32[]{:S(2)}, u32[]{:S(2)}) collective-permute-start(bf16[256,1792]{1,0:T(8,128)(2,1)S(1)} %get-tuple-element.15), channel_id=1, source_target_pairs={{0,6},{1,7},{2,4},{3,5},{4,2},{5,3},{6,0},{7,1},{8,14},{9,15},{10,... | collective-permute-start | bytes 2752520 | tf_op jit(solution)/shard_map/ppermute | solution.py:21
  43.3 7.1 %collective-permute-start.4 = (bf16[256,1024]{1,0:T(8,128)(2,1)S(1)}, bf16[256,1024]{1,0:T(8,128)(2,1)S(1)}, u32[]{:S(2)}, u32[]{:S(2)}) collective-permute-start(bf16[256,1024]{1,0:T(8,128)(2,1)S(1)} %get-tuple-element.56), channel_id=1, source_target_pairs={{0,8},{8,0},{16,24},{24,16},{32,40},{40,32},{48,56},{56,48},{64,72... | collective-permute-start | bytes 1572872 | tf_op jit(solution)/shard_map/ppermute | solution.py:21
  43.4 7.0 %copy-start.12 = (s32[8]{0:T(128)S(1)}, s32[8]{0:T(128)}, u32[]{:S(2)}) copy-start(s32[8]{0:T(128)} %constant.61.clone) | copy-start | bytes 100
  50.1 22.8 %collective-permute-start.16 = (bf16[256,1792]{1,0:T(8,128)(2,1)S(1)}, bf16[256,1792]{1,0:T(8,128)(2,1)S(1)}, u32[]{:S(2)}, u32[]{:S(2)}) collective-permute-start(bf16[256,1792]{1,0:T(8,128)(2,1)S(1)} %get-tuple-element.17), channel_id=1, source_target_pairs={{0,2},{1,3},{2,0},{3,1},{4,6},{5,7},{6,4},{7,5},{8,10},{9,11},{10,... | collective-permute-start | bytes 2752520 | tf_op jit(solution)/shard_map/ppermute | solution.py:21
  50.4 6.9 %copy-start.5 = (bf16[512,1024]{1,0:T(8,128)(2,1)}, bf16[512,1024]{1,0:T(8,128)(2,1)S(1)}, u32[]{:S(2)}) copy-start(bf16[512,1024]{1,0:T(8,128)(2,1)S(1)} %constant_dynamic-update-slice_fusion.7) | copy-start | bytes 3145732
  57.3 23.3 %collective-permute-start.5 = (bf16[256,1792]{1,0:T(8,128)(2,1)S(1)}, bf16[256,1792]{1,0:T(8,128)(2,1)S(1)}, u32[]{:S(2)}, u32[]{:S(2)}) collective-permute-start(bf16[256,1792]{1,0:T(8,128)(2,1)S(1)} %get-tuple-element.13), channel_id=1, source_target_pairs={{0,1},{1,0},{2,3},{3,2},{4,5},{5,4},{6,7},{7,6},{8,9},{9,8},{10,11... | collective-permute-start | bytes 2752520 | tf_op jit(solution)/shard_map/ppermute | solution.py:21
  63.3 26.5 %collective-permute-start.14 = (bf16[128,1792]{1,0:T(8,128)(2,1)S(1)}, bf16[128,1792]{1,0:T(8,128)(2,1)S(1)}, u32[]{:S(2)}, u32[]{:S(2)}) collective-permute-start(bf16[128,1792]{1,0:T(8,128)(2,1)S(1)} %get-tuple-element.27), channel_id=1, source_target_pairs={{0,1},{1,0},{2,3},{3,2},{4,5},{5,4},{6,7},{7,6},{8,9},{9,8},{10,11... | collective-permute-start | bytes 1376264 | tf_op jit(solution)/shard_map/ppermute | solution.py:21
  73.1 18.6 %collective-permute-start.17 = (bf16[128,1792]{1,0:T(8,128)(2,1)S(1)}, bf16[128,1792]{1,0:T(8,128)(2,1)S(1)}, u32[]{:S(2)}, u32[]{:S(2)}) collective-permute-start(bf16[128,1792]{1,0:T(8,128)(2,1)S(1)} %get-tuple-element.25), channel_id=1, source_target_pairs={{0,6},{1,7},{2,4},{3,5},{4,2},{5,3},{6,0},{7,1},{8,14},{9,15},{10,... | collective-permute-start | bytes 1376264 | tf_op jit(solution)/shard_map/ppermute | solution.py:21
  80.7 12.1 %collective-permute-start.6 = (bf16[128,1792]{1,0:T(8,128)(2,1)S(1)}, bf16[128,1792]{1,0:T(8,128)(2,1)S(1)}, u32[]{:S(2)}, u32[]{:S(2)}) collective-permute-start(bf16[128,1792]{1,0:T(8,128)(2,1)S(1)} %get-tuple-element.29), channel_id=1, source_target_pairs={{0,2},{1,3},{2,0},{3,1},{4,6},{5,7},{6,4},{7,5},{8,10},{9,11},{10,... | collective-permute-start | bytes 1376264 | tf_op jit(solution)/shard_map/ppermute | solution.py:21
  89.9 7.2 %collective-permute-start.15 = (bf16[64,1792]{1,0:T(8,128)(2,1)S(1)}, bf16[64,1792]{1,0:T(8,128)(2,1)S(1)}, u32[]{:S(2)}, u32[]{:S(2)}) collective-permute-start(bf16[64,1792]{1,0:T(8,128)(2,1)S(1)} %fusion.2), channel_id=1, source_target_pairs={{0,2},{1,3},{2,0},{3,1},{4,6},{5,7},{6,4},{7,5},{8,10},{9,11},{10,... | collective-permute-start | bytes 688136 | tf_op jit(solution)/shard_map/ppermute | solution.py:21
  91.7 6.7 %collective-permute-start.18 = (bf16[64,1792]{1,0:T(8,128)(2,1)S(1)}, bf16[64,1792]{1,0:T(8,128)(2,1)S(1)}, u32[]{:S(2)}, u32[]{:S(2)}) collective-permute-start(bf16[64,1792]{1,0:T(8,128)(2,1)S(1)} %fusion), channel_id=1, source_target_pairs={{0,1},{1,0},{2,3},{3,2},{4,5},{5,4},{6,7},{7,6},{8,9},{9,8},{10,11... | collective-permute-start | bytes 688136 | tf_op jit(solution)/shard_map/ppermute | solution.py:21
  92.9 7.6 %collective-permute-start.7 = (bf16[64,1792]{1,0:T(8,128)(2,1)S(1)}, bf16[64,1792]{1,0:T(8,128)(2,1)S(1)}, u32[]{:S(2)}, u32[]{:S(2)}) collective-permute-start(bf16[64,1792]{1,0:T(8,128)(2,1)S(1)} %fusion.4), channel_id=1, source_target_pairs={{0,6},{1,7},{2,4},{3,5},{4,2},{5,3},{6,0},{7,1},{8,14},{9,15},{10,... | collective-permute-start | bytes 688136 | tf_op jit(solution)/shard_map/ppermute | solution.py:21
  101.0 6.1 %collective-permute-start.19 = (bf16[64,1792]{1,0:T(8,128)(2,1)S(1)}, bf16[64,1792]{1,0:T(8,128)(2,1)S(1)}, u32[]{:S(2)}, u32[]{:S(2)}) collective-permute-start(bf16[64,1792]{1,0:T(8,128)(2,1)S(1)} %get-tuple-element.23), channel_id=1, source_target_pairs={{0,2},{1,3},{2,0},{3,1},{4,6},{5,7},{6,4},{7,5},{8,10},{9,11},{10,... | collective-permute-start | bytes 688136 | tf_op jit(solution)/shard_map/ppermute | solution.py:21
  101.0 7.9 %collective-permute-start.22 = (bf16[64,1792]{1,0:T(8,128)(2,1)S(1)}, bf16[64,1792]{1,0:T(8,128)(2,1)S(1)}, u32[]{:S(2)}, u32[]{:S(2)}) collective-permute-start(bf16[64,1792]{1,0:T(8,128)(2,1)S(1)} %get-tuple-element.24), channel_id=1, source_target_pairs={{0,6},{1,7},{2,4},{3,5},{4,2},{5,3},{6,0},{7,1},{8,14},{9,15},{10,... | collective-permute-start | bytes 688136 | tf_op jit(solution)/shard_map/ppermute | solution.py:21
  107.1 11.1 %collective-permute-start.20 = (bf16[128,1792]{1,0:T(8,128)(2,1)S(1)}, bf16[128,1792]{1,0:T(8,128)(2,1)S(1)}, u32[]{:S(2)}, u32[]{:S(2)}) collective-permute-start(bf16[128,1792]{1,0:T(8,128)(2,1)S(1)} %pad_maximum_fusion.3), channel_id=1, source_target_pairs={{0,6},{1,7},{2,4},{3,5},{4,2},{5,3},{6,0},{7,1},{8,14},{9,15},{10,... | collective-permute-start | bytes 1376264 | tf_op jit(solution)/shard_map/ppermute | solution.py:21
  108.9 11.6 %copy-start.8 = (s32[8]{0:T(128)S(1)}, s32[8]{0:T(128)}, u32[]{:S(2)}) copy-start(s32[8]{0:T(128)} %constant.63.clone) | copy-start | bytes 100
  109.0 11.6 %copy-start.9 = (s32[8]{0:T(128)S(1)}, s32[8]{0:T(128)}, u32[]{:S(2)}) copy-start(s32[8]{0:T(128)} %constant.62.clone) | copy-start | bytes 100
  109.0 10.4 %collective-permute-start.23 = (bf16[128,1792]{1,0:T(8,128)(2,1)S(1)}, bf16[128,1792]{1,0:T(8,128)(2,1)S(1)}, u32[]{:S(2)}, u32[]{:S(2)}) collective-permute-start(bf16[128,1792]{1,0:T(8,128)(2,1)S(1)} %pad_maximum_fusion.4), channel_id=1, source_target_pairs={{0,1},{1,0},{2,3},{3,2},{4,5},{5,4},{6,7},{7,6},{8,9},{9,8},{10,11... | collective-permute-start | bytes 1376264 | tf_op jit(solution)/shard_map/ppermute | solution.py:21
  118.3 21.7 %copy-start.2 = (bf16[256,1792]{1,0:T(8,128)(2,1)}, bf16[256,1792]{1,0:T(8,128)(2,1)S(1)}, u32[]{:S(2)}) copy-start(bf16[256,1792]{1,0:T(8,128)(2,1)S(1)} %pad_maximum_fusion.gn_ref.near_ref) | copy-start | bytes 2752516
  118.3 21.6 %collective-permute-start.21 = (bf16[256,1792]{1,0:T(8,128)(2,1)S(1)}, bf16[256,1792]{1,0:T(8,128)(2,1)}, u32[]{:S(2)}, u32[]{:S(2)}) collective-permute-start(bf16[256,1792]{1,0:T(8,128)(2,1)S(1)} %pad_maximum_fusion.gn_ref.near_ref), channel_id=1, source_target_pairs={{0,1},{1,0},{2,3},{3,2},{4,5},{5,4},{6,7},{7,6},{8,9},{9,8},{10,11... | collective-permute-start | bytes 2752520 | tf_op jit(solution)/shard_map/ppermute | solution.py:21
  119.4 30.3 %copy-start = (bf16[256,1792]{1,0:T(8,128)(2,1)}, bf16[256,1792]{1,0:T(8,128)(2,1)S(1)}, u32[]{:S(2)}) copy-start(bf16[256,1792]{1,0:T(8,128)(2,1)S(1)} %pad_maximum_fusion.1.un_ref.near_ref) | copy-start | bytes 2752516
  119.4 20.5 %collective-permute-start.24 = (bf16[256,1792]{1,0:T(8,128)(2,1)S(1)}, bf16[256,1792]{1,0:T(8,128)(2,1)}, u32[]{:S(2)}, u32[]{:S(2)}) collective-permute-start(bf16[256,1792]{1,0:T(8,128)(2,1)S(1)} %pad_maximum_fusion.1.un_ref.near_ref), channel_id=1, source_target_pairs={{0,2},{1,3},{2,0},{3,1},{4,6},{5,7},{6,4},{7,5},{8,10},{9,11},{10,... | collective-permute-start | bytes 2752520 | tf_op jit(solution)/shard_map/ppermute | solution.py:21
  131.3 18.4 %collective-permute-start.30 = (bf16[64,1792]{1,0:T(8,128)(2,1)S(1)}, bf16[64,1792]{1,0:T(8,128)(2,1)S(1)}, u32[]{:S(2)}, u32[]{:S(2)}) collective-permute-start(bf16[64,1792]{1,0:T(8,128)(2,1)S(1)} %get-tuple-element.22), channel_id=1, source_target_pairs={{0,1},{1,0},{2,3},{3,2},{4,5},{5,4},{6,7},{7,6},{8,9},{9,8},{10,11... | collective-permute-start | bytes 688136 | tf_op jit(solution)/shard_map/ppermute | solution.py:21
  139.9 1.2 copy-start.3
  141.1 32.6 %copy-start.11 = (s32[8]{0:T(128)S(1)}, s32[8]{0:T(128)}, u32[]{:S(2)}) copy-start(s32[8]{0:T(128)} %constant.64.clone) | copy-start | bytes 100
  149.7 56.1 %collective-permute-start.25 = (f32[256,1024]{1,0:T(8,128)}, f32[256,1024]{1,0:T(8,128)}, u32[]{:S(2)}, u32[]{:S(2)}) collective-permute-start(f32[256,1024]{1,0:T(8,128)} %get-tuple-element.19), channel_id=1, source_target_pairs={{0,8},{8,0},{16,24},{24,16},{32,40},{40,32},{48,56},{56,48},{64,72... | collective-permute-start | bytes 3145736 | tf_op jit(solution)/shard_map/ppermute | solution.py:21
  149.7 3.8 %copy-start.7 = (bf16[64,1792]{1,0:T(8,128)(2,1)}, bf16[64,1792]{1,0:T(8,128)(2,1)S(1)}, u32[]{:S(2)}) copy-start(bf16[64,1792]{1,0:T(8,128)(2,1)S(1)} %collective-permute-done.30) | copy-start | bytes 688132
  150.6 46.8 %collective-permute-start.31 = (bf16[128,1792]{1,0:T(8,128)(2,1)}, bf16[128,1792]{1,0:T(8,128)(2,1)}, u32[]{:S(2)}, u32[]{:S(2)}) collective-permute-start(bf16[128,1792]{1,0:T(8,128)(2,1)} %pad_maximum_fusion.5), channel_id=1, source_target_pairs={{0,2},{1,3},{2,0},{3,1},{4,6},{5,7},{6,4},{7,5},{8,10},{9,11},{10,... | collective-permute-start | bytes 1376264 | tf_op jit(solution)/shard_map/ppermute | solution.py:21
  197.4 1.7 copy-start.4
  198.6 23.8 %collective-permute-start.32 = (bf16[256,1792]{1,0:T(8,128)(2,1)S(1)}, bf16[256,1792]{1,0:T(8,128)(2,1)S(1)}, u32[]{:S(2)}, u32[]{:S(2)}) collective-permute-start(bf16[256,1792]{1,0:T(8,128)(2,1)S(1)} %pad_maximum_fusion.2.near_ref), channel_id=1, source_target_pairs={{0,6},{1,7},{2,4},{3,5},{4,2},{5,3},{6,0},{7,1},{8,14},{9,15},{10,... | collective-permute-start | bytes 2752520 | tf_op jit(solution)/shard_map/ppermute | solution.py:21
  205.8 5.1 %copy-start.1 = (bf16[256,1792]{1,0:T(8,128)(2,1)S(1)}, bf16[256,1792]{1,0:T(8,128)(2,1)}, u32[]{:S(2)}) copy-start(bf16[256,1792]{1,0:T(8,128)(2,1)} %copy-done) | copy-start | bytes 2752516
  207.4 10.4 %collective-permute-start.28 = (bf16[64,1024]{1,0:T(8,128)(2,1)S(1)}, bf16[64,1024]{1,0:T(8,128)(2,1)S(1)}, u32[]{:S(2)}, u32[]{:S(2)}) collective-permute-start(bf16[64,1024]{1,0:T(8,128)(2,1)S(1)} %get-tuple-element.48), channel_id=1, source_target_pairs={{0,64},{8,72},{16,80},{24,88},{32,96},{40,104},{48,112},{56,120},{... | collective-permute-start | bytes 393224 | tf_op jit(solution)/shard_map/ppermute | solution.py:21
  207.4 10.3 %collective-permute-start.27 = (bf16[64,1024]{1,0:T(8,128)(2,1)S(1)}, bf16[64,1024]{1,0:T(8,128)(2,1)S(1)}, u32[]{:S(2)}, u32[]{:S(2)}) collective-permute-start(bf16[64,1024]{1,0:T(8,128)(2,1)S(1)} %get-tuple-element.49), channel_id=1, source_target_pairs={{0,96},{8,104},{16,112},{24,120},{32,64},{40,72},{48,80},{56,88},{... | collective-permute-start | bytes 393224 | tf_op jit(solution)/shard_map/ppermute | solution.py:21
  210.3 7.4 %collective-permute-start.26 = (bf16[64,1024]{1,0:T(8,128)(2,1)S(1)}, bf16[64,1024]{1,0:T(8,128)(2,1)S(1)}, u32[]{:S(2)}, u32[]{:S(2)}) collective-permute-start(bf16[64,1024]{1,0:T(8,128)(2,1)S(1)} %get-tuple-element.47), channel_id=1, source_target_pairs={{0,32},{8,40},{16,48},{24,56},{32,0},{40,8},{48,16},{56,24},{64,96... | collective-permute-start | bytes 393224 | tf_op jit(solution)/shard_map/ppermute | solution.py:21
  210.9 11.4 %copy-start.6 = (bf16[512,1024]{1,0:T(8,128)(2,1)S(1)}, bf16[512,1024]{1,0:T(8,128)(2,1)}, u32[]{:S(2)}) copy-start(bf16[512,1024]{1,0:T(8,128)(2,1)} %copy-done.5) | copy-start | bytes 3145732
  217.9 10.2 %collective-permute-start.29 = (f32[32,1024]{1,0:T(8,128)S(1)}, f32[32,1024]{1,0:T(8,128)S(1)}, u32[]{:S(2)}, u32[]{:S(2)}) collective-permute-start(f32[32,1024]{1,0:T(8,128)S(1)} %slice.210), channel_id=1, source_target_pairs={{0,16},{8,24},{16,0},{24,8},{32,48},{40,56},{48,32},{56,40},{64,80... | collective-permute-start | bytes 393224 | tf_op jit(solution)/shard_map/ppermute | solution.py:21

commit v2 on v0

v2 whole, which is shorter than its diff:
```python
import functools

import jax
import jax.numpy as jnp
from jax import lax
from jax.experimental import pallas as pl
from jax.experimental.pallas import tpu as pltpu
from jax.sharding import PartitionSpec as P

BF16, F32 = jnp.bfloat16, jnp.float32
TILE = 256
CHUNKS = 2
VMEM = 20 * 1024 * 1024

COL = {"a": 2, "b": 6, "c": 1}
BIT = {"a": 4, "b": 2, "c": 1}
CORE, ZHI, XA, XB, XAB = 1, 2, 4, 12, 8

SUM_DIMS = ("abc", "bca", "cab", "abc", "bca", "cab")
GATHER_DIMS = ("bca", "cab", "cab", "bca", "acb", "cba")


def swap(value, axis, mask):
    size = lax.axis_size(axis)
    return lax.ppermute(value, axis, [(i, i ^ mask) for i in range(size)])

IN_VMEM = pl.BlockSpec(memory_space=pltpu.VMEM)
IN_SMEM = pl.BlockSpec(memory_space=pltpu.SMEM)
PARAMS = pltpu.CompilerParams(vmem_limit_bytes=VMEM)


SHORT = pl.CostEstimate(flops=1, bytes_accessed=1, transcendentals=0)


def block_at(place, mine, dims):
    name = sum(BIT[d] * ((place >> (2 - k)) & 1) for k, d in enumerate(dims))
    return name ^ mine


def place_of(block, mine, dims):
    bits = [(((block ^ mine) // BIT[d]) % 2) * (4 >> k) for k, d in enumerate(dims)]
    return bits[0] + bits[1] + bits[2]


class Order:
    def __init__(self, mine):
        self.mine = mine

    def run(self, call, *args):
        out = call(self.mine, *args)
        self.mine, out = lax.optimization_barrier((self.mine, out))
        return out


def small(kernel, shapes, count):
    return pl.pallas_call(
        lambda mine, *refs: kernel(*refs),
        out_shape=shapes,
        in_specs=[IN_SMEM] + [IN_VMEM] * count,
        out_specs=[IN_VMEM] * len(shapes),
        compiler_params=PARAMS,
        cost_estimate=SHORT,
    )


def join_kernel(plan, *refs):
    ins, outs = refs[: -len(plan)], refs[-len(plan) :]
    for out, pieces in zip(outs, plan):
        at = 0
        for which, start, size in pieces:
            out[at : at + size, :] = ins[which][start : start + size, :]
            at += size


def join(order, arrays, *plan):
    width = arrays[0].shape[1]
    shapes = [
        jax.ShapeDtypeStruct((sum(p[2] for p in pieces), width), arrays[0].dtype)
        for pieces in plan
    ]
    out = order.run(
        small(functools.partial(join_kernel, plan), shapes, len(arrays)), *arrays
    )
    return out if len(out) > 1 else out[0]


def fetch_kernel(mine_ref, w_ref, out_ref, sem):
    copy = pltpu.make_async_copy(w_ref, out_ref, sem)
    copy.start()
    copy.wait()


def fetch(order, weight):
    return order.run(
        pl.pallas_call(
            fetch_kernel,
            out_shape=jax.ShapeDtypeStruct(weight.shape, weight.dtype),
            in_specs=[IN_SMEM, pl.BlockSpec(memory_space=pltpu.HBM)],
            out_specs=IN_VMEM,
            scratch_shapes=[pltpu.SemaphoreType.DMA],
            compiler_params=PARAMS,
            cost_estimate=SHORT,
        ),
        weight,
    )


def stack_kernel(a_ref, b_ref, out_ref, sems):
    n = a_ref.shape[0]
    copies = [
        pltpu.make_async_copy(ref, out_ref.at[k * n : (k + 1) * n], sems.at[k])
        for k, ref in enumerate((a_ref, b_ref))
    ]
    for copy in copies:
        copy.start()
    for copy in copies:
        copy.wait()


def stack(a, b):
    return pl.pallas_call(
        stack_kernel,
        out_shape=jax.ShapeDtypeStruct((2 * a.shape[0], a.shape[1]), a.dtype),
        in_specs=[pl.BlockSpec(memory_space=pltpu.HBM)] * 2,
        out_specs=IN_VMEM,
        scratch_shapes=[pltpu.SemaphoreType.DMA((2,))],
        compiler_params=PARAMS,
        cost_estimate=SHORT,
    )(a, b)


def part_kernel(w_dim, dims, first, cols, mine_ref, x_ref, w_ref, out_ref, x_scr):
    rows = x_ref.shape[1]
    for k in range(4):
        x_scr[k * rows : (k + 1) * rows, :] = x_ref[block_at(first + k, mine_ref[0], dims)]
    w = w_ref[:, cols] if w_dim == 0 else w_ref[cols, :]
    out_ref[...] = lax.dot_general(
        x_scr[...], w, (((1,), (w_dim,)), ((), ())), preferred_element_type=F32
    ).astype(out_ref.dtype)


def partial_product(order, blocks, weight, w_dim, dims, first, cols, dtype):
    _, rows, depth = blocks.shape
    width = cols.stop - cols.start
    call = pl.pallas_call(
        functools.partial(part_kernel, w_dim, dims, first, cols),
        out_shape=jax.ShapeDtypeStruct((4 * rows, width), dtype),
        in_specs=[IN_SMEM, IN_VMEM, IN_VMEM],
        out_specs=IN_VMEM,
        scratch_shapes=[pltpu.VMEM((4 * rows, depth), BF16)],
        compiler_params=PARAMS,
        cost_estimate=SHORT,
    )
    return order.run(call, blocks, weight)


def halve_kernel(keep_ref, far_ref, send_ref, total_ref):
    n = send_ref.shape[0]
    send_ref[...] = (keep_ref[n:, :] + far_ref[n:, :].astype(F32)).astype(BF16)
    total_ref[...] = keep_ref[:n, :] + far_ref[:n, :].astype(F32)


def halve(order, keep, far):
    shape = (far.shape[0] // 2, far.shape[1])
    shapes = [jax.ShapeDtypeStruct(shape, BF16), jax.ShapeDtypeStruct(shape, F32)]
    return order.run(small(halve_kernel, shapes, 2), keep, far)


def swiglu_kernel(*refs):
    gate, up, hidden_grad = (
        refs[2 * k][...] + refs[2 * k + 1][...].astype(F32) for k in range(3)
    )
    for ref, value in zip(refs[6:], swiglu_grads(gate, up, hidden_grad)):
        ref[...] = value


def swiglu(order, totals, fars):
    shape = jax.ShapeDtypeStruct(totals[0].shape, BF16)
    args = [a for pair in zip(totals, fars) for a in pair]
    return order.run(small(swiglu_kernel, [shape] * 3, 6), *args)


def reorder(dims, mine_ref, blocks_ref, out_ref):
    rows = blocks_ref.shape[1]
    for place in range(8):
        out_ref[place * rows : (place + 1) * rows, :] = blocks_ref[
            block_at(place, mine_ref[0], dims)
        ]


FIRST = (((0,), (0,)), ((), ()))
LAST = (((1,), (1,)), ((), ()))


def grad_pieces(out_ref, out_scr, sems, rows_at, cols, pieces):
    copies = []
    for k, (rows, value) in enumerate(pieces):
        out_scr[rows, :] = value().astype(BF16)
        there = slice(rows_at + rows.start, rows_at + rows.stop)
        copies.append(
            pltpu.make_async_copy(out_scr.at[rows], out_ref.at[there, cols], sems.at[k])
        )
        copies[-1].start()
    for copy in copies:
        copy.wait()


def wide_kernel(dims, cols, mine_ref, x_ref, grad_ref, *rest):
    out_ref, x_scr, out_scr, sems = rest[-4:]
    reorder(dims, mine_ref, x_ref, x_scr)
    half = out_scr.shape[0] // 2

    def product(rows):
        return lambda: lax.dot_general(
            x_scr[:, rows], grad_ref[...], FIRST, preferred_element_type=F32
        )

    parts = (slice(0, half), slice(half, 2 * half))
    grad_pieces(out_ref, out_scr, sems, 0, cols, [(rows, product(rows)) for rows in parts])


def tall_kernel(dims, at, mine_ref, g_ref, hidden_ref, *rest):
    out_ref, g_scr, out_scr, sems = rest[-4:]
    reorder(dims, mine_ref, g_ref, g_scr)
    width = out_scr.shape[0]
    half = -(-width // 256) * 128

    def product(rows):
        return lambda: lax.dot_general(
            hidden_ref[:, rows], g_scr[...], FIRST, preferred_element_type=F32
        )

    parts = (slice(0, half), slice(half, width))
    grad_pieces(
        out_ref, out_scr, sems, at, slice(None), [(rows, product(rows)) for rows in parts]
    )


def weight_grad(order, kernel, shape, piece, blocks, grad, before):
    _, rows, depth = blocks.shape
    tokens, width = grad.shape
    more = [] if before is None else [before]
    call = pl.pallas_call(
        kernel,
        out_shape=jax.ShapeDtypeStruct(shape, BF16),
        in_specs=[IN_SMEM, IN_VMEM, IN_VMEM] + [pl.BlockSpec(memory_space=pltpu.HBM)] * len(more),
        out_specs=pl.BlockSpec(memory_space=pl.ANY),
        scratch_shapes=[
            pltpu.VMEM((tokens, depth), BF16),
            pltpu.VMEM(piece, BF16),
            pltpu.SemaphoreType.DMA((2,)),
        ],
        input_output_aliases={3: 0} if more else {},
        compiler_params=PARAMS,
        cost_estimate=SHORT,
    )
    return order.run(call, blocks, grad, *more)


def input_kernel(first, gate_dims, up_dims, cols, mine_ref, gg_ref, ug_ref, wg_ref, wu_ref, *rest):
    out_ref, gg_scr, ug_scr = rest[-3:]
    mine = mine_ref[0]
    rows = gg_ref.shape[1]
    for k in range(4):
        here = slice(k * rows, (k + 1) * rows)
        gg_scr[here, :] = gg_ref[place_of(first + k, mine, gate_dims)]
        ug_scr[here, :] = ug_ref[place_of(first + k, mine, up_dims)]
    for i in range(0, out_ref.shape[1], TILE):
        here = slice(i, i + TILE)
        part = lax.dot_general(
            gg_scr[...], wg_ref[here, cols], LAST, preferred_element_type=F32
        ) + lax.dot_general(ug_scr[...], wu_ref[here, cols], LAST, preferred_element_type=F32)
        out_ref[:, here] = part + rest[0][:, here] if len(rest) == 4 else part


def input_part(order, first, grads, dims, weights, cols, before):
    tokens, width = grads[0].shape
    depth = weights[0].shape[0]
    half = pltpu.VMEM((tokens // 2, width), BF16)
    blocked = (8, tokens // 8, width)
    more = [] if before is None else [before]
    call = pl.pallas_call(
        functools.partial(input_kernel, first, *dims, cols),
        out_shape=jax.ShapeDtypeStruct((tokens // 2, depth), F32),
        in_specs=[IN_SMEM] + [IN_VMEM] * (4 + len(more)),
        out_specs=IN_VMEM,
        scratch_shapes=[half, half],
        compiler_params=PARAMS,
        cost_estimate=SHORT,
    )
    return order.run(call, *(v.reshape(blocked) for v in grads), *weights, *more)


def core_kernel(keep_ref, far_ref, own_ref, *send_refs):
    n = own_ref.shape[0]
    own_ref[...] = keep_ref[:n, :] + far_ref[:n, :]
    for k, ref in enumerate(send_refs, 1):
        here = slice(k * n, (k + 1) * n)
        ref[...] = (keep_ref[here, :] + far_ref[here, :]).astype(BF16)


def ring_kernel(own_ref, a_ref, b_ref, c_ref, keep_ref, send_ref):
    total = (own_ref[...] + a_ref[...].astype(F32)) + (
        b_ref[...].astype(F32) + c_ref[...].astype(F32)
    )
    n = keep_ref.shape[0]
    keep_ref[...] = total[:n]
    send_ref[...] = total[n:]


def swiglu_grads(gate, up, hidden_grad):
    sig = jax.nn.sigmoid(gate)
    hidden = (gate * sig * up).astype(BF16)
    gate_grad = (hidden_grad * up * sig * (1.0 + gate * (1.0 - sig))).astype(BF16)
    up_grad = (hidden_grad * gate * sig).astype(BF16)
    return hidden, gate_grad, up_grad


def per_device(inputs, out_grad, gate_weight, up_weight, down_weight):
    col = lax.axis_index("col")
    y_high, y_low = (col >> 2) & 1, (col >> 1) & 1
    mine = (y_high ^ y_low) * BIT["a"] + y_high * BIT["b"] + (col & 1) * BIT["c"]
    mine = mine.astype(jnp.int32).reshape(1)

    order = Order(mine)
    depth, width = gate_weight.shape
    size = width // CHUNKS
    chunks = [slice(k * size, (k + 1) * size) for k in range(CHUNKS)]
    n = inputs.shape[0]
    own = stack(inputs, out_grad)
    far = swap(own, "row", ZHI)
    weights = [fetch(order, gate_weight)]
    x, g = join(order, (own, far), ((0, 0, n), (1, 0, n)), ((0, n, n), (1, n, n)))
    far_x, far_g = swap(x, "row", XA), swap(g, "row", XB)
    weights.append(fetch(order, up_weight))
    n = 2 * n
    x, g = join(order, (x, far_x, g, far_g), ((0, 0, n), (1, 0, n)), ((2, 0, n), (3, 0, n)))
    far_x, far_g = swap(x, "row", XB), swap(g, "row", XA)
    weights.append(fetch(order, down_weight))
    x, g = join(
        order,
        (x, far_x, g, far_g),
        ((0, 0, 2 * n), (1, 0, 2 * n)),
        ((2, 0, n), (3, 0, n), (2, n, n), (3, n, n)),
    )
    far_x, far_g = swap(x, "row", CORE), swap(g, "row", CORE)
    x = join(order, (x, far_x), ((0, 0, 4 * n), (1, 0, 4 * n))).reshape(8, n, -1)

    w_dims = (0, 0, 1)
    items = [(c, k) for c in range(CHUNKS) for k in range(3)]
    totals, fars = [None] * len(items), [None] * len(items)
    lefts = [x, x, None]

    def part(i, first, dtype):
        c, k = items[i]
        return partial_product(
            order, lefts[k], weights[k], w_dims[k], SUM_DIMS[i], first, chunks[c], dtype
        )

    for i, (_, k) in enumerate(items):
        if lefts[k] is None:
            lefts[k] = join(order, (g, far_g), ((0, 0, 4 * n), (1, 0, 4 * n))).reshape(x.shape)
        fars[i] = swap(part(i, 4, BF16), "col", COL[SUM_DIMS[i][0]])
    for step in (1, 2):
        for i, dims in enumerate(SUM_DIMS):
            if step == 1:
                totals[i] = part(i, 0, F32)
            send, totals[i] = halve(order, totals[i], fars[i])
            fars[i] = swap(send, "col", COL[dims[step]])

    grads = [None] * len(items)
    for c in range(CHUNKS):
        these = slice(3 * c, 3 * c + 3)
        hidden, gate_grad, up_grad = swiglu(order, totals[these], fars[these])
        grads[these] = gate_grad, up_grad, hidden
        for i in (3 * c, 3 * c + 1):
            fars[i] = swap(grads[i], "col", COL[GATHER_DIMS[i][0]])

    def grow(i, step):
        if step:
            n = fars[i].shape[0]
            grads[i] = join(order, (grads[i], fars[i]), ((0, 0, n), (1, 0, n)))
        if step < 3:
            fars[i] = swap(grads[i], "col", COL[GATHER_DIMS[i][step]])

    out = [None] * 3
    shapes = (((depth, width), (depth, size)),) * 2 + (((width, depth), (size, depth)),)

    def weight_step(i):
        c, k = items[i]
        place = GATHER_DIMS[i][::-1]
        kernel = (
            functools.partial(wide_kernel, place, chunks[c])
            if k < 2
            else functools.partial(tall_kernel, place, chunks[c].start)
        )
        out[k] = weight_grad(order, kernel, *shapes[k], lefts[k], grads[i], out[k])

    def input_step(c, first, before):
        these = slice(3 * c, 3 * c + 2)
        places = [dims[::-1] for dims in GATHER_DIMS[these]]
        return input_part(order, first, grads[these], places, weights[:2], chunks[c], before)

    for step in (1, 2):
        for i in (0, 1, 3, 4):
            grow(i, step)
    grow(2, 0)
    grow(5, 0)
    grow(0, 3)
    grow(1, 3)
    send, keep = input_step(0, 4, None), input_step(0, 0, None)
    grow(2, 1)
    grow(5, 1)
    weight_step(0)
    weight_step(1)
    grow(3, 3)
    grow(4, 3)
    send = input_step(1, 4, send)
    far = swap(send, "row", CORE)
    keep = input_step(1, 0, keep)

    n = x.shape[1]
    shape = (n, depth)
    own, *sends = order.run(
        small(
            core_kernel,
            [jax.ShapeDtypeStruct(shape, F32)] + [jax.ShapeDtypeStruct(shape, BF16)] * 3,
            2,
        ),
        keep,
        far,
    )
    rings = [swap(v, "row", mask) for v, mask in zip(sends, (XA, XB, XAB))]
    grow(2, 2)
    grow(5, 2)
    weight_step(3)
    shape = jax.ShapeDtypeStruct((n // 2, depth), F32)
    keep, send = order.run(small(ring_kernel, [shape, shape], 4), own, *rings)
    far = swap(send, "row", ZHI)
    weight_step(4)
    for i in (2, 5):
        grow(i, 3)
        weight_step(i)
    input_grad = (keep + far).astype(BF16)
    return (input_grad, *out)


def solution(mesh):
    return jax.shard_map(
        per_device,
        mesh=mesh,
        in_specs=(
            P("row", "col"),
            P("row", "col"),
            P("col", "row"),
            P("col", "row"),
            P("row", "col"),
        ),
        out_specs=(P("row", "col"), P("col", "row"), P("col", "row"), P("row", "col")),
        check_vma=False,
    )
```

time: 590 us -> 140 us (0.24)
  waiting for transfers between devices: 513 us -> 38.9 us
  starting transfers between devices: 0.54 us -> 64.6 us
  matrix products: 44.6 us -> 0 us
  Pallas kernels: 0 us -> 30 us
  between operations: 13.9 us -> 1.44 us
  local copies, waits for them, and re-layouts: 13.2 us -> 3.72 us
    reduce_scatter x4 -> x0, waiting for transfers between devices: 314 us -> none  [the longest x1 84.3 us: per_device(): lax.psum_scatter(gate_part, 'col', scatter_dimension=0, tiled=True)]
    all_gather x5 -> x0, waiting for transfers between devices: 196 us -> none  [the longest x1 49.3 us: per_device(): lax.all_gather(inputs, 'row', axis=0, tiled=True)]
    ppermute x0 -> x48, starting transfers between devices: none -> 64.6 us  [swap(): return lax.ppermute(value, axis, [(i, i ^ mask) for i in range(size)])]
    dot_general x8 -> x0, matrix products: 44.6 us -> none  [the longest x3 19.1 us: contract_last(): lax.dot_general(left, right, (((1,), (1,)), ((), ())), preferred_element_...]
    ppermute x0 -> x48, waiting for transfers between devices: none -> 38.9 us  [swap(): return lax.ppermute(value, axis, [(i, i ^ mask) for i in range(size)])]
    pallas_call x0 -> x65, Pallas kernels: none -> 30 us  [the longest x64 29.9 us: run(): out = call(self.mine, *args)]
    unnamed x10, local copies, waits for them, and re-layouts: 13.2 us -> 3.72 us
  transfers between devices with their start and end apart: 9 -> 48, of which waited for: 9 -> 22; matrix products, arithmetic and copies ran while one was open for 10% -> 0% of each run, Pallas kernels for 0% -> 19%
where the time goes in v2:
time: 140 us; the launch traced here: 139 us
  starting transfers between devices  64.6 us (46%)
  waiting for transfers between devices  38.9 us (28%)
  Pallas kernels  30 us (21%)
  local copies, waits for them, and re-layouts  3.72 us (3%)
  between operations  1.44 us (1%)
    ppermute x48, starting transfers between devices, swap(): return lax.ppermute(value, axis, [(i, i ^ mask) for i in range(size)])  64.6 us
    ppermute x48, waiting for transfers between devices, swap(): return lax.ppermute(value, axis, [(i, i ^ mask) for i in range(size)])  38.9 us
    pallas_call x64, Pallas kernels, run(): out = call(self.mine, *args)  29.9 us
    unnamed x10, local copies, waits for them, and re-layouts  3.72 us
  transfers between devices with their start and end apart: 48, of which 22 were waited for; matrix products, arithmetic and copies ran while one was open for 0% of the time, Pallas kernels for 19%

profile of v2, /device:TPU:0, one launch (start us, length us, event | category | flops | bytes accessed | tf_op | source)
XLA Modules:
  0.0 139.4 jit_solution(16367221604332345486)
XLA Ops:
  0.6 0.8 copy-done.3
  1.5 0.8 copy-done.4
  2.5 4.0 %collective-permute-start = (bf16[64,1024]{1,0:T(8,128)(2,1)S(1)}, bf16[64,1024]{1,0:T(8,128)(2,1)S(1)}, u32[]{:S(2)}, u32[]{:S(2)}) collective-permute-start(bf16[64,1024]{1,0:T(8,128)(2,1)S(1)} %shard_map.85.refs_0_), channel_id=1, source_target_pairs={{0,16},{8,24},{16,0},{24,8},{32,48},{40,56},{48,32},{56,40},{64,80... | collective-permute-start | bytes 393224 | tf_op jit(solution)/shard_map/ppermute | solution.py:25
  6.5 2.0 %copy-done = bf16[1024,1792]{1,0:T(8,128)(2,1)S(1)} copy-done((bf16[1024,1792]{1,0:T(8,128)(2,1)S(1)}, bf16[1024,1792]{1,0:T(8,128)(2,1)}, u32[]{:S(2)}) %copy-start) | copy-done | bytes 3670040
  8.8 1.2 collective-permute-done.refs_1_
  10.0 1.6 %collective-permute-start.1 = (bf16[64,1024]{1,0:T(8,128)(2,1)S(1)}, bf16[64,1024]{1,0:T(8,128)(2,1)S(1)}, u32[]{:S(2)}, u32[]{:S(2)}) collective-permute-start(bf16[64,1024]{1,0:T(8,128)(2,1)S(1)} %get-tuple-element.201.refs_0_), channel_id=1, source_target_pairs={{0,32},{8,40},{16,48},{24,56},{32,0},{40,8},{48,16},{56,24},{64,96... | collective-permute-start | bytes 393224 | tf_op jit(solution)/shard_map/ppermute | solution.py:25
  11.6 2.1 %collective-permute-start.2 = (bf16[64,1024]{1,0:T(8,128)(2,1)S(1)}, bf16[64,1024]{1,0:T(8,128)(2,1)S(1)}, u32[]{:S(2)}, u32[]{:S(2)}) collective-permute-start(bf16[64,1024]{1,0:T(8,128)(2,1)S(1)} %get-tuple-element.202.refs_2_), channel_id=1, source_target_pairs={{0,96},{8,104},{16,112},{24,120},{32,64},{40,72},{48,80},{56,88},{... | collective-permute-start | bytes 393224 | tf_op jit(solution)/shard_map/ppermute | solution.py:25
  14.0 1.1 collective-permute-done.1.refs_1_
  15.1 2.7 %collective-permute-done.2.refs_3_ = bf16[64,1024]{1,0:T(8,128)(2,1)S(1)} collective-permute-done((bf16[64,1024]{1,0:T(8,128)(2,1)S(1)}, bf16[64,1024]{1,0:T(8,128)(2,1)S(1)}, u32[]{:S(2)}, u32[]{:S(2)}) %collective-permute-start.2) | collective-permute-done | bytes 131104 | tf_op jit(solution)/shard_map/ppermute | solution.py:25
  17.8 2.2 %collective-permute-start.3 = (bf16[128,1024]{1,0:T(8,128)(2,1)S(1)}, bf16[128,1024]{1,0:T(8,128)(2,1)S(1)}, u32[]{:S(2)}, u32[]{:S(2)}) collective-permute-start(bf16[128,1024]{1,0:T(8,128)(2,1)S(1)} %get-tuple-element.207.refs_0_), channel_id=1, source_target_pairs={{0,96},{8,104},{16,112},{24,120},{32,64},{40,72},{48,80},{56,88},{... | collective-permute-start | bytes 786440 | tf_op jit(solution)/shard_map/ppermute | solution.py:25
  20.3 5.2 %collective-permute-done.3.refs_1_ = bf16[128,1024]{1,0:T(8,128)(2,1)S(1)} collective-permute-done((bf16[128,1024]{1,0:T(8,128)(2,1)S(1)}, bf16[128,1024]{1,0:T(8,128)(2,1)S(1)}, u32[]{:S(2)}, u32[]{:S(2)}) %collective-permute-start.3) | collective-permute-done | bytes 262176 | tf_op jit(solution)/shard_map/ppermute | solution.py:25
  25.5 0.9 collective-permute-done.4.refs_3_
  27.0 1.4 %collective-permute-done.5.refs_1_ = bf16[256,1024]{1,0:T(8,128)(2,1)S(1)} collective-permute-done((bf16[256,1024]{1,0:T(8,128)(2,1)S(1)}, bf16[256,1024]{1,0:T(8,128)(2,1)S(1)}, u32[]{:S(2)}, u32[]{:S(2)}) %collective-permute-start.5) | collective-permute-done | bytes 524320 | tf_op jit(solution)/shard_map/ppermute | solution.py:25
  29.2 1.7 %collective-permute-start.7 = (bf16[256,896]{1,0:T(8,128)(2,1)S(1)}, bf16[256,896]{1,0:T(8,128)(2,1)S(1)}, u32[]{:S(2)}, u32[]{:S(2)}) collective-permute-start(bf16[256,896]{1,0:T(8,128)(2,1)S(1)} %shard_map.92), channel_id=1, source_target_pairs={{0,2},{1,3},{2,0},{3,1},{4,6},{5,7},{6,4},{7,5},{8,10},{9,11},{10,... | collective-permute-start | bytes 1376264 | tf_op jit(solution)/shard_map/ppermute | solution.py:25
  31.6 2.3 %collective-permute-start.8 = (bf16[256,896]{1,0:T(8,128)(2,1)S(1)}, bf16[256,896]{1,0:T(8,128)(2,1)S(1)}, u32[]{:S(2)}, u32[]{:S(2)}) collective-permute-start(bf16[256,896]{1,0:T(8,128)(2,1)S(1)} %shard_map.93), channel_id=1, source_target_pairs={{0,6},{1,7},{2,4},{3,5},{4,2},{5,3},{6,0},{7,1},{8,14},{9,15},{10,... | collective-permute-start | bytes 1376264 | tf_op jit(solution)/shard_map/ppermute | solution.py:25
  34.7 1.4 collective-permute-start.9
  39.7 3.0 %collective-permute-done.7.refs_1_ = bf16[256,896]{1,0:T(8,128)(2,1)S(1)} collective-permute-done((bf16[256,896]{1,0:T(8,128)(2,1)S(1)}, bf16[256,896]{1,0:T(8,128)(2,1)S(1)}, u32[]{:S(2)}, u32[]{:S(2)}) %collective-permute-start.7) | collective-permute-done | bytes 458784 | tf_op jit(solution)/shard_map/ppermute | solution.py:25
  42.7 1.3 collective-permute-start.12
  44.8 1.5 %collective-permute-done.8.refs_1_ = bf16[256,896]{1,0:T(8,128)(2,1)S(1)} collective-permute-done((bf16[256,896]{1,0:T(8,128)(2,1)S(1)}, bf16[256,896]{1,0:T(8,128)(2,1)S(1)}, u32[]{:S(2)}, u32[]{:S(2)}) %collective-permute-start.8) | collective-permute-done | bytes 458784 | tf_op jit(solution)/shard_map/ppermute | solution.py:25
  46.3 2.2 %collective-permute-start.13 = (bf16[128,896]{1,0:T(8,128)(2,1)S(1)}, bf16[128,896]{1,0:T(8,128)(2,1)S(1)}, u32[]{:S(2)}, u32[]{:S(2)}) collective-permute-start(bf16[128,896]{1,0:T(8,128)(2,1)S(1)} %get-tuple-element.264), channel_id=1, source_target_pairs={{0,6},{1,7},{2,4},{3,5},{4,2},{5,3},{6,0},{7,1},{8,14},{9,15},{10,... | collective-permute-start | bytes 688136 | tf_op jit(solution)/shard_map/ppermute | solution.py:25
  50.0 1.4 collective-permute-start.14
  52.2 1.1 collective-permute-start.15
  53.4 2.8 %collective-permute-done.11.refs_1_ = bf16[256,896]{1,0:T(8,128)(2,1)S(1)} collective-permute-done((bf16[256,896]{1,0:T(8,128)(2,1)S(1)}, bf16[256,896]{1,0:T(8,128)(2,1)S(1)}, u32[]{:S(2)}, u32[]{:S(2)}) %collective-permute-start.11) | collective-permute-done | bytes 458784 | tf_op jit(solution)/shard_map/ppermute | solution.py:25
  56.1 2.2 %collective-permute-start.16 = (bf16[128,896]{1,0:T(8,128)(2,1)S(1)}, bf16[128,896]{1,0:T(8,128)(2,1)S(1)}, u32[]{:S(2)}, u32[]{:S(2)}) collective-permute-start(bf16[128,896]{1,0:T(8,128)(2,1)S(1)} %get-tuple-element.279), channel_id=1, source_target_pairs={{0,6},{1,7},{2,4},{3,5},{4,2},{5,3},{6,0},{7,1},{8,14},{9,15},{10,... | collective-permute-start | bytes 688136 | tf_op jit(solution)/shard_map/ppermute | solution.py:25
  59.9 1.4 collective-permute-start.17
  61.5 1.4 collective-permute-done.14.refs_1_
  63.0 1.4 collective-permute-start.19
  64.3 0.8 collective-permute-start.20
  65.1 1.9 %collective-permute-start.21 = (bf16[64,896]{1,0:T(8,128)(2,1)S(1)}, bf16[64,896]{1,0:T(8,128)(2,1)S(1)}, u32[]{:S(2)}, u32[]{:S(2)}) collective-permute-start(bf16[64,896]{1,0:T(8,128)(2,1)S(1)} %get-tuple-element.298), channel_id=1, source_target_pairs={{0,6},{1,7},{2,4},{3,5},{4,2},{5,3},{6,0},{7,1},{8,14},{9,15},{10,... | collective-permute-start | bytes 344072 | tf_op jit(solution)/shard_map/ppermute | solution.py:25
  67.8 1.4 collective-permute-start.22
  69.8 1.7 %collective-permute-start.24 = (bf16[64,896]{1,0:T(8,128)(2,1)S(1)}, bf16[64,896]{1,0:T(8,128)(2,1)S(1)}, u32[]{:S(2)}, u32[]{:S(2)}) collective-permute-start(bf16[64,896]{1,0:T(8,128)(2,1)S(1)} %get-tuple-element.308), channel_id=1, source_target_pairs={{0,6},{1,7},{2,4},{3,5},{4,2},{5,3},{6,0},{7,1},{8,14},{9,15},{10,... | collective-permute-start | bytes 344072 | tf_op jit(solution)/shard_map/ppermute | solution.py:25
  71.7 2.8 %collective-permute-start.25 = (bf16[64,896]{1,0:T(8,128)(2,1)S(1)}, bf16[64,896]{1,0:T(8,128)(2,1)S(1)}, u32[]{:S(2)}, u32[]{:S(2)}) collective-permute-start(bf16[64,896]{1,0:T(8,128)(2,1)S(1)} %get-tuple-element.313.refs_0_), channel_id=1, source_target_pairs={{0,6},{1,7},{2,4},{3,5},{4,2},{5,3},{6,0},{7,1},{8,14},{9,15},{10,... | collective-permute-start | bytes 344072 | tf_op jit(solution)/shard_map/ppermute | solution.py:25
  74.5 1.3 collective-permute-start.26
  76.0 1.8 %collective-permute-done.25.refs_1_ = bf16[64,896]{1,0:T(8,128)(2,1)S(1)} collective-permute-done((bf16[64,896]{1,0:T(8,128)(2,1)S(1)}, bf16[64,896]{1,0:T(8,128)(2,1)S(1)}, u32[]{:S(2)}, u32[]{:S(2)}) %collective-permute-start.25) | collective-permute-done | bytes 114720 | tf_op jit(solution)/shard_map/ppermute | solution.py:25
  77.8 1.1 collective-permute-start.29
  78.9 3.1 %collective-permute-start.27 = (bf16[64,896]{1,0:T(8,128)(2,1)S(1)}, bf16[64,896]{1,0:T(8,128)(2,1)S(1)}, u32[]{:S(2)}, u32[]{:S(2)}) collective-permute-start(bf16[64,896]{1,0:T(8,128)(2,1)S(1)} %get-tuple-element.317.refs_0_), channel_id=1, source_target_pairs={{0,6},{1,7},{2,4},{3,5},{4,2},{5,3},{6,0},{7,1},{8,14},{9,15},{10,... | collective-permute-start | bytes 344072 | tf_op jit(solution)/shard_map/ppermute | solution.py:25
  82.0 2.1 %collective-permute-start.30 = (bf16[128,896]{1,0:T(8,128)(2,1)S(1)}, bf16[128,896]{1,0:T(8,128)(2,1)S(1)}, u32[]{:S(2)}, u32[]{:S(2)}) collective-permute-start(bf16[128,896]{1,0:T(8,128)(2,1)S(1)} %shard_map.120.refs_0_), channel_id=1, source_target_pairs={{0,2},{1,3},{2,0},{3,1},{4,6},{5,7},{6,4},{7,5},{8,10},{9,11},{10,... | collective-permute-start | bytes 688136 | tf_op jit(solution)/shard_map/ppermute | solution.py:25
  84.1 0.8 collective-permute-done.27.refs_1_
  84.9 1.1 collective-permute-start.31
  86.0 2.0 %collective-permute-done.28.refs_1_ = bf16[64,896]{1,0:T(8,128)(2,1)S(1)} collective-permute-done((bf16[64,896]{1,0:T(8,128)(2,1)S(1)}, bf16[64,896]{1,0:T(8,128)(2,1)S(1)}, u32[]{:S(2)}, u32[]{:S(2)}) %collective-permute-start.28) | collective-permute-done | bytes 114720 | tf_op jit(solution)/shard_map/ppermute | solution.py:25
  88.8 4.1 %collective-permute-done.30.refs_1_ = bf16[128,896]{1,0:T(8,128)(2,1)S(1)} collective-permute-done((bf16[128,896]{1,0:T(8,128)(2,1)S(1)}, bf16[128,896]{1,0:T(8,128)(2,1)S(1)}, u32[]{:S(2)}, u32[]{:S(2)}) %collective-permute-start.30) | collective-permute-done | bytes 229408 | tf_op jit(solution)/shard_map/ppermute | solution.py:25
  93.2 0.9 collective-permute-done.32.refs_1_
  94.2 4.1 %collective-permute-start.38 = (bf16[256,896]{1,0:T(8,128)(2,1)S(1)}, bf16[256,896]{1,0:T(8,128)(2,1)S(1)}, u32[]{:S(2)}, u32[]{:S(2)}) collective-permute-start(bf16[256,896]{1,0:T(8,128)(2,1)S(1)} %shard_map.126.refs_0_), channel_id=1, source_target_pairs={{0,6},{1,7},{2,4},{3,5},{4,2},{5,3},{6,0},{7,1},{8,14},{9,15},{10,... | collective-permute-start | bytes 1376264 | tf_op jit(solution)/shard_map/ppermute | solution.py:25
  98.3 1.0 collective-permute-start.35
  99.3 3.3 %collective-permute-done.33.refs_1_ = bf16[256,896]{1,0:T(8,128)(2,1)S(1)} collective-permute-done((bf16[256,896]{1,0:T(8,128)(2,1)S(1)}, bf16[256,896]{1,0:T(8,128)(2,1)S(1)}, u32[]{:S(2)}, u32[]{:S(2)}) %collective-permute-start.33) | collective-permute-done | bytes 458784 | tf_op jit(solution)/shard_map/ppermute | solution.py:25
  102.6 1.2 collective-permute-start.36
  103.9 1.3 shard_map.129.rest_0_
  105.2 1.3 shard_map.130.rest_0_
  106.5 0.8 collective-permute-done.36.refs_1_
  107.4 2.2 %shard_map.133.rest_0_ = bf16[1024,1792]{1,0:T(8,128)(2,1)} custom-call(s32[1]{0:T(128)} %bitcast.mine_ref.mine, bf16[8,64,1024]{2,1,0:T(8,128)(2,1)S(1)} %bitcast.15, bf16[512,896]{1,0:T(8,128)(2,1)S(1)} %shard_map.127.grad_ref), custom_call_target="tpu_custom_call" | custom-call | flops 1 | bytes 1 | tf_op jit(solution)/shard_map/pallas_call | solution.py:50
  109.6 2.2 %shard_map.134.rest_0_ = bf16[1024,1792]{1,0:T(8,128)(2,1)} custom-call(s32[1]{0:T(128)} %bitcast.mine_ref.mine, bf16[8,64,1024]{2,1,0:T(8,128)(2,1)S(1)} %bitcast.16, bf16[512,896]{1,0:T(8,128)(2,1)S(1)} %shard_map.128.grad_ref), custom_call_target="tpu_custom_call" | custom-call | flops 1 | bytes 1 | tf_op jit(solution)/shard_map/pallas_call | solution.py:50
  112.1 1.3 shard_map.137
  113.7 1.1 collective-permute-start.41
  114.9 1.3 shard_map.138.refs_0_
  116.4 1.3 collective-permute-start.43
  117.7 2.8 %collective-permute-start.44 = (bf16[64,1024]{1,0:T(8,128)(2,1)S(1)}, bf16[64,1024]{1,0:T(8,128)(2,1)S(1)}, u32[]{:S(2)}, u32[]{:S(2)}) collective-permute-start(bf16[64,1024]{1,0:T(8,128)(2,1)S(1)} %get-tuple-element.369), channel_id=1, source_target_pairs={{0,64},{8,72},{16,80},{24,88},{32,96},{40,104},{48,112},{56,120},{... | collective-permute-start | bytes 393224 | tf_op jit(solution)/shard_map/ppermute | solution.py:25
  120.5 1.0 collective-permute-done.40.refs_1_
  121.5 1.3 collective-permute-start.46
  123.5 2.2 %shard_map.142 = bf16[1024,1792]{1,0:T(8,128)(2,1)} custom-call(s32[1]{0:T(128)} %bitcast.mine_ref.mine, bf16[8,64,1024]{2,1,0:T(8,128)(2,1)S(1)} %bitcast.17, bf16[512,896]{1,0:T(8,128)(2,1)S(1)} %shard_map.135.grad_ref, bf16[1024,1792]{1,0:T(8,128)(2,1)} %shard_map.133.rest_0_), custom_call_target="tpu_custom_call", output_to_operand_aliasing={{}: (3, {})} | custom-call | flops 1 | bytes 1 | tf_op jit(solution)/shard_map/pallas_call | solution.py:50
  126.0 3.9 %collective-permute-start.45 = (f32[32,1024]{1,0:T(8,128)S(1)}, f32[32,1024]{1,0:T(8,128)S(1)}, u32[]{:S(2)}, u32[]{:S(2)}) collective-permute-start(f32[32,1024]{1,0:T(8,128)S(1)} %get-tuple-element.373), channel_id=1, source_target_pairs={{0,16},{8,24},{16,0},{24,8},{32,48},{40,56},{48,32},{56,40},{64,80... | collective-permute-start | bytes 393224 | tf_op jit(solution)/shard_map/ppermute | solution.py:25
  129.9 2.2 %shard_map.144 = bf16[1024,1792]{1,0:T(8,128)(2,1)} custom-call(s32[1]{0:T(128)} %bitcast.mine_ref.mine, bf16[8,64,1024]{2,1,0:T(8,128)(2,1)S(1)} %bitcast.18, bf16[512,896]{1,0:T(8,128)(2,1)S(1)} %shard_map.136.grad_ref, bf16[1024,1792]{1,0:T(8,128)(2,1)} %shard_map.134.rest_0_), custom_call_target="tpu_custom_call", output_to_operand_aliasing={{}: (3, {})} | custom-call | flops 1 | bytes 1 | tf_op jit(solution)/shard_map/pallas_call | solution.py:50
  133.5 1.4 collective-permute-done.46.refs_1_
  135.0 2.0 %shard_map.146.rest_0_ = bf16[1792,1024]{1,0:T(8,128)(2,1)} custom-call(s32[1]{0:T(128)} %bitcast.mine_ref.mine, bf16[8,64,1024]{2,1,0:T(8,128)(2,1)S(1)} %bitcast.23, bf16[512,896]{1,0:T(8,128)(2,1)S(1)} %shard_map.145.hidden_ref), custom_call_target="tpu_custom_call" | custom-call | flops 1 | bytes 1 | tf_op jit(solution)/shard_map/pallas_call | solution.py:50
  137.1 2.1 %shard_map.148 = bf16[1792,1024]{1,0:T(8,128)(2,1)} custom-call(s32[1]{0:T(128)} %bitcast.mine_ref.mine, bf16[8,64,1024]{2,1,0:T(8,128)(2,1)S(1)} %bitcast.24, bf16[512,896]{1,0:T(8,128)(2,1)S(1)} %shard_map.147.hidden_ref, bf16[1792,1024]{1,0:T(8,128)(2,1)} %shard_map.146.rest_0_), custom_call_target="tpu_custom_call", output_to_operand_aliasing={{}: (3, {})} | custom-call | flops 1 | bytes 1 | tf_op jit(solution)/shard_map/pallas_call | solution.py:50
  (108 shorter events, 18.8 us)
Async XLA Ops:
  0.6 0.8 copy-start.3
  1.5 0.8 copy-start.4
  2.5 7.5 %collective-permute-start = (bf16[64,1024]{1,0:T(8,128)(2,1)S(1)}, bf16[64,1024]{1,0:T(8,128)(2,1)S(1)}, u32[]{:S(2)}, u32[]{:S(2)}) collective-permute-start(bf16[64,1024]{1,0:T(8,128)(2,1)S(1)} %shard_map.85.refs_0_), channel_id=1, source_target_pairs={{0,16},{8,24},{16,0},{24,8},{32,48},{40,56},{48,32},{56,40},{64,80... | collective-permute-start | bytes 393224 | tf_op jit(solution)/shard_map/ppermute | solution.py:25
  6.5 2.0 %copy-start = (bf16[1024,1792]{1,0:T(8,128)(2,1)S(1)}, bf16[1024,1792]{1,0:T(8,128)(2,1)}, u32[]{:S(2)}) copy-start(bf16[1024,1792]{1,0:T(8,128)(2,1)} %w_ref.3) | copy-start | bytes 11010052
  8.6 5.2 %copy-start.1 = (bf16[1024,1792]{1,0:T(8,128)(2,1)S(1)}, bf16[1024,1792]{1,0:T(8,128)(2,1)}, u32[]{:S(2)}) copy-start(bf16[1024,1792]{1,0:T(8,128)(2,1)} %w_ref.4) | copy-start | bytes 11010052
  10.0 10.0 %copy-start.2 = (bf16[1792,1024]{1,0:T(8,128)(2,1)S(1)}, bf16[1792,1024]{1,0:T(8,128)(2,1)}, u32[]{:S(2)}) copy-start(bf16[1792,1024]{1,0:T(8,128)(2,1)} %w_ref.5) | copy-start | bytes 11010052
  10.0 5.0 %collective-permute-start.1 = (bf16[64,1024]{1,0:T(8,128)(2,1)S(1)}, bf16[64,1024]{1,0:T(8,128)(2,1)S(1)}, u32[]{:S(2)}, u32[]{:S(2)}) collective-permute-start(bf16[64,1024]{1,0:T(8,128)(2,1)S(1)} %get-tuple-element.201.refs_0_), channel_id=1, source_target_pairs={{0,32},{8,40},{16,48},{24,56},{32,0},{40,8},{48,16},{56,24},{64,96... | collective-permute-start | bytes 393224 | tf_op jit(solution)/shard_map/ppermute | solution.py:25
  11.6 6.2 %collective-permute-start.2 = (bf16[64,1024]{1,0:T(8,128)(2,1)S(1)}, bf16[64,1024]{1,0:T(8,128)(2,1)S(1)}, u32[]{:S(2)}, u32[]{:S(2)}) collective-permute-start(bf16[64,1024]{1,0:T(8,128)(2,1)S(1)} %get-tuple-element.202.refs_2_), channel_id=1, source_target_pairs={{0,96},{8,104},{16,112},{24,120},{32,64},{40,72},{48,80},{56,88},{... | collective-permute-start | bytes 393224 | tf_op jit(solution)/shard_map/ppermute | solution.py:25
  17.8 7.7 %collective-permute-start.3 = (bf16[128,1024]{1,0:T(8,128)(2,1)S(1)}, bf16[128,1024]{1,0:T(8,128)(2,1)S(1)}, u32[]{:S(2)}, u32[]{:S(2)}) collective-permute-start(bf16[128,1024]{1,0:T(8,128)(2,1)S(1)} %get-tuple-element.207.refs_0_), channel_id=1, source_target_pairs={{0,96},{8,104},{16,112},{24,120},{32,64},{40,72},{48,80},{56,88},{... | collective-permute-start | bytes 786440 | tf_op jit(solution)/shard_map/ppermute | solution.py:25
  20.0 6.4 %collective-permute-start.4 = (bf16[128,1024]{1,0:T(8,128)(2,1)S(1)}, bf16[128,1024]{1,0:T(8,128)(2,1)S(1)}, u32[]{:S(2)}, u32[]{:S(2)}) collective-permute-start(bf16[128,1024]{1,0:T(8,128)(2,1)S(1)} %get-tuple-element.208.refs_2_), channel_id=1, source_target_pairs={{0,32},{8,40},{16,48},{24,56},{32,0},{40,8},{48,16},{56,24},{64,96... | collective-permute-start | bytes 786440 | tf_op jit(solution)/shard_map/ppermute | solution.py:25
  26.5 2.0 %collective-permute-start.5 = (bf16[256,1024]{1,0:T(8,128)(2,1)S(1)}, bf16[256,1024]{1,0:T(8,128)(2,1)S(1)}, u32[]{:S(2)}, u32[]{:S(2)}) collective-permute-start(bf16[256,1024]{1,0:T(8,128)(2,1)S(1)} %get-tuple-element.212.refs_0_), channel_id=1, source_target_pairs={{0,8},{8,0},{16,24},{24,16},{32,40},{40,32},{48,56},{56,48},{64,72... | collective-permute-start | bytes 1572872 | tf_op jit(solution)/shard_map/ppermute | solution.py:25
  26.5 7.3 %collective-permute-start.6 = (bf16[256,1024]{1,0:T(8,128)(2,1)S(1)}, bf16[256,1024]{1,0:T(8,128)(2,1)S(1)}, u32[]{:S(2)}, u32[]{:S(2)}) collective-permute-start(bf16[256,1024]{1,0:T(8,128)(2,1)S(1)} %get-tuple-element.219.refs_0_), channel_id=1, source_target_pairs={{0,8},{8,0},{16,24},{24,16},{32,40},{40,32},{48,56},{56,48},{64,72... | collective-permute-start | bytes 1572872 | tf_op jit(solution)/shard_map/ppermute | solution.py:25
  29.2 13.4 %collective-permute-start.7 = (bf16[256,896]{1,0:T(8,128)(2,1)S(1)}, bf16[256,896]{1,0:T(8,128)(2,1)S(1)}, u32[]{:S(2)}, u32[]{:S(2)}) collective-permute-start(bf16[256,896]{1,0:T(8,128)(2,1)S(1)} %shard_map.92), channel_id=1, source_target_pairs={{0,2},{1,3},{2,0},{3,1},{4,6},{5,7},{6,4},{7,5},{8,10},{9,11},{10,... | collective-permute-start | bytes 1376264 | tf_op jit(solution)/shard_map/ppermute | solution.py:25
  31.6 14.7 %collective-permute-start.8 = (bf16[256,896]{1,0:T(8,128)(2,1)S(1)}, bf16[256,896]{1,0:T(8,128)(2,1)S(1)}, u32[]{:S(2)}, u32[]{:S(2)}) collective-permute-start(bf16[256,896]{1,0:T(8,128)(2,1)S(1)} %shard_map.93), channel_id=1, source_target_pairs={{0,6},{1,7},{2,4},{3,5},{4,2},{5,3},{6,0},{7,1},{8,14},{9,15},{10,... | collective-permute-start | bytes 1376264 | tf_op jit(solution)/shard_map/ppermute | solution.py:25
  34.7 15.3 %collective-permute-start.9 = (bf16[256,896]{1,0:T(8,128)(2,1)S(1)}, bf16[256,896]{1,0:T(8,128)(2,1)S(1)}, u32[]{:S(2)}, u32[]{:S(2)}) collective-permute-start(bf16[256,896]{1,0:T(8,128)(2,1)S(1)} %shard_map.95), channel_id=1, source_target_pairs={{0,1},{1,0},{2,3},{3,2},{4,5},{5,4},{6,7},{7,6},{8,9},{9,8},{10,11... | collective-permute-start | bytes 1376264 | tf_op jit(solution)/shard_map/ppermute | solution.py:25
  36.8 15.4 %collective-permute-start.10 = (bf16[256,896]{1,0:T(8,128)(2,1)S(1)}, bf16[256,896]{1,0:T(8,128)(2,1)S(1)}, u32[]{:S(2)}, u32[]{:S(2)}) collective-permute-start(bf16[256,896]{1,0:T(8,128)(2,1)S(1)} %shard_map.96), channel_id=1, source_target_pairs={{0,2},{1,3},{2,0},{3,1},{4,6},{5,7},{6,4},{7,5},{8,10},{9,11},{10,... | collective-permute-start | bytes 1376264 | tf_op jit(solution)/shard_map/ppermute | solution.py:25
  38.3 17.9 %collective-permute-start.11 = (bf16[256,896]{1,0:T(8,128)(2,1)S(1)}, bf16[256,896]{1,0:T(8,128)(2,1)S(1)}, u32[]{:S(2)}, u32[]{:S(2)}) collective-permute-start(bf16[256,896]{1,0:T(8,128)(2,1)S(1)} %shard_map.97), channel_id=1, source_target_pairs={{0,6},{1,7},{2,4},{3,5},{4,2},{5,3},{6,0},{7,1},{8,14},{9,15},{10,... | collective-permute-start | bytes 1376264 | tf_op jit(solution)/shard_map/ppermute | solution.py:25
  42.7 17.2 %collective-permute-start.12 = (bf16[256,896]{1,0:T(8,128)(2,1)S(1)}, bf16[256,896]{1,0:T(8,128)(2,1)S(1)}, u32[]{:S(2)}, u32[]{:S(2)}) collective-permute-start(bf16[256,896]{1,0:T(8,128)(2,1)S(1)} %shard_map.98), channel_id=1, source_target_pairs={{0,1},{1,0},{2,3},{3,2},{4,5},{5,4},{6,7},{7,6},{8,9},{9,8},{10,11... | collective-permute-start | bytes 1376264 | tf_op jit(solution)/shard_map/ppermute | solution.py:25
  46.3 15.0 %collective-permute-start.13 = (bf16[128,896]{1,0:T(8,128)(2,1)S(1)}, bf16[128,896]{1,0:T(8,128)(2,1)S(1)}, u32[]{:S(2)}, u32[]{:S(2)}) collective-permute-start(bf16[128,896]{1,0:T(8,128)(2,1)S(1)} %get-tuple-element.264), channel_id=1, source_target_pairs={{0,6},{1,7},{2,4},{3,5},{4,2},{5,3},{6,0},{7,1},{8,14},{9,15},{10,... | collective-permute-start | bytes 688136 | tf_op jit(solution)/shard_map/ppermute | solution.py:25
  50.0 12.8 %collective-permute-start.14 = (bf16[128,896]{1,0:T(8,128)(2,1)S(1)}, bf16[128,896]{1,0:T(8,128)(2,1)S(1)}, u32[]{:S(2)}, u32[]{:S(2)}) collective-permute-start(bf16[128,896]{1,0:T(8,128)(2,1)S(1)} %get-tuple-element.269), channel_id=1, source_target_pairs={{0,1},{1,0},{2,3},{3,2},{4,5},{5,4},{6,7},{7,6},{8,9},{9,8},{10,11... | collective-permute-start | bytes 688136 | tf_op jit(solution)/shard_map/ppermute | solution.py:25
  52.2 10.7 %collective-permute-start.15 = (bf16[128,896]{1,0:T(8,128)(2,1)S(1)}, bf16[128,896]{1,0:T(8,128)(2,1)S(1)}, u32[]{:S(2)}, u32[]{:S(2)}) collective-permute-start(bf16[128,896]{1,0:T(8,128)(2,1)S(1)} %get-tuple-element.274), channel_id=1, source_target_pairs={{0,2},{1,3},{2,0},{3,1},{4,6},{5,7},{6,4},{7,5},{8,10},{9,11},{10,... | collective-permute-start | bytes 688136 | tf_op jit(solution)/shard_map/ppermute | solution.py:25
  56.1 9.0 %collective-permute-start.16 = (bf16[128,896]{1,0:T(8,128)(2,1)S(1)}, bf16[128,896]{1,0:T(8,128)(2,1)S(1)}, u32[]{:S(2)}, u32[]{:S(2)}) collective-permute-start(bf16[128,896]{1,0:T(8,128)(2,1)S(1)} %get-tuple-element.279), channel_id=1, source_target_pairs={{0,6},{1,7},{2,4},{3,5},{4,2},{5,3},{6,0},{7,1},{8,14},{9,15},{10,... | collective-permute-start | bytes 688136 | tf_op jit(solution)/shard_map/ppermute | solution.py:25
  59.9 7.8 %collective-permute-start.17 = (bf16[128,896]{1,0:T(8,128)(2,1)S(1)}, bf16[128,896]{1,0:T(8,128)(2,1)S(1)}, u32[]{:S(2)}, u32[]{:S(2)}) collective-permute-start(bf16[128,896]{1,0:T(8,128)(2,1)S(1)} %get-tuple-element.284), channel_id=1, source_target_pairs={{0,1},{1,0},{2,3},{3,2},{4,5},{5,4},{6,7},{7,6},{8,9},{9,8},{10,11... | collective-permute-start | bytes 688136 | tf_op jit(solution)/shard_map/ppermute | solution.py:25
  61.3 6.4 %collective-permute-start.18 = (bf16[128,896]{1,0:T(8,128)(2,1)S(1)}, bf16[128,896]{1,0:T(8,128)(2,1)S(1)}, u32[]{:S(2)}, u32[]{:S(2)}) collective-permute-start(bf16[128,896]{1,0:T(8,128)(2,1)S(1)} %get-tuple-element.289), channel_id=1, source_target_pairs={{0,2},{1,3},{2,0},{3,1},{4,6},{5,7},{6,4},{7,5},{8,10},{9,11},{10,... | collective-permute-start | bytes 688136 | tf_op jit(solution)/shard_map/ppermute | solution.py:25
  63.0 6.9 %collective-permute-start.19 = (bf16[64,896]{1,0:T(8,128)(2,1)S(1)}, bf16[64,896]{1,0:T(8,128)(2,1)S(1)}, u32[]{:S(2)}, u32[]{:S(2)}) collective-permute-start(bf16[64,896]{1,0:T(8,128)(2,1)S(1)} %get-tuple-element.294), channel_id=1, source_target_pairs={{0,1},{1,0},{2,3},{3,2},{4,5},{5,4},{6,7},{7,6},{8,9},{9,8},{10,11... | collective-permute-start | bytes 344072 | tf_op jit(solution)/shard_map/ppermute | solution.py:25
  64.3 7.2 %collective-permute-start.20 = (bf16[64,896]{1,0:T(8,128)(2,1)S(1)}, bf16[64,896]{1,0:T(8,128)(2,1)S(1)}, u32[]{:S(2)}, u32[]{:S(2)}) collective-permute-start(bf16[64,896]{1,0:T(8,128)(2,1)S(1)} %get-tuple-element.296), channel_id=1, source_target_pairs={{0,2},{1,3},{2,0},{3,1},{4,6},{5,7},{6,4},{7,5},{8,10},{9,11},{10,... | collective-permute-start | bytes 344072 | tf_op jit(solution)/shard_map/ppermute | solution.py:25
  65.1 6.4 %collective-permute-start.21 = (bf16[64,896]{1,0:T(8,128)(2,1)S(1)}, bf16[64,896]{1,0:T(8,128)(2,1)S(1)}, u32[]{:S(2)}, u32[]{:S(2)}) collective-permute-start(bf16[64,896]{1,0:T(8,128)(2,1)S(1)} %get-tuple-element.298), channel_id=1, source_target_pairs={{0,6},{1,7},{2,4},{3,5},{4,2},{5,3},{6,0},{7,1},{8,14},{9,15},{10,... | collective-permute-start | bytes 344072 | tf_op jit(solution)/shard_map/ppermute | solution.py:25
  67.8 8.0 %collective-permute-start.22 = (bf16[64,896]{1,0:T(8,128)(2,1)S(1)}, bf16[64,896]{1,0:T(8,128)(2,1)S(1)}, u32[]{:S(2)}, u32[]{:S(2)}) collective-permute-start(bf16[64,896]{1,0:T(8,128)(2,1)S(1)} %get-tuple-element.304), channel_id=1, source_target_pairs={{0,1},{1,0},{2,3},{3,2},{4,5},{5,4},{6,7},{7,6},{8,9},{9,8},{10,11... | collective-permute-start | bytes 344072 | tf_op jit(solution)/shard_map/ppermute | solution.py:25
  69.1 6.7 %collective-permute-start.23 = (bf16[64,896]{1,0:T(8,128)(2,1)S(1)}, bf16[64,896]{1,0:T(8,128)(2,1)S(1)}, u32[]{:S(2)}, u32[]{:S(2)}) collective-permute-start(bf16[64,896]{1,0:T(8,128)(2,1)S(1)} %get-tuple-element.306), channel_id=1, source_target_pairs={{0,2},{1,3},{2,0},{3,1},{4,6},{5,7},{6,4},{7,5},{8,10},{9,11},{10,... | collective-permute-start | bytes 344072 | tf_op jit(solution)/shard_map/ppermute | solution.py:25
  69.8 6.0 %collective-permute-start.24 = (bf16[64,896]{1,0:T(8,128)(2,1)S(1)}, bf16[64,896]{1,0:T(8,128)(2,1)S(1)}, u32[]{:S(2)}, u32[]{:S(2)}) collective-permute-start(bf16[64,896]{1,0:T(8,128)(2,1)S(1)} %get-tuple-element.308), channel_id=1, source_target_pairs={{0,6},{1,7},{2,4},{3,5},{4,2},{5,3},{6,0},{7,1},{8,14},{9,15},{10,... | collective-permute-start | bytes 344072 | tf_op jit(solution)/shard_map/ppermute | solution.py:25
  71.7 6.1 %collective-permute-start.25 = (bf16[64,896]{1,0:T(8,128)(2,1)S(1)}, bf16[64,896]{1,0:T(8,128)(2,1)S(1)}, u32[]{:S(2)}, u32[]{:S(2)}) collective-permute-start(bf16[64,896]{1,0:T(8,128)(2,1)S(1)} %get-tuple-element.313.refs_0_), channel_id=1, source_target_pairs={{0,6},{1,7},{2,4},{3,5},{4,2},{5,3},{6,0},{7,1},{8,14},{9,15},{10,... | collective-permute-start | bytes 344072 | tf_op jit(solution)/shard_map/ppermute | solution.py:25
  74.5 7.5 %collective-permute-start.26 = (bf16[64,896]{1,0:T(8,128)(2,1)S(1)}, bf16[64,896]{1,0:T(8,128)(2,1)S(1)}, u32[]{:S(2)}, u32[]{:S(2)}) collective-permute-start(bf16[64,896]{1,0:T(8,128)(2,1)S(1)} %get-tuple-element.315.refs_0_), channel_id=1, source_target_pairs={{0,1},{1,0},{2,3},{3,2},{4,5},{5,4},{6,7},{7,6},{8,9},{9,8},{10,11... | collective-permute-start | bytes 344072 | tf_op jit(solution)/shard_map/ppermute | solution.py:25
  77.8 10.9 %collective-permute-start.29 = (bf16[128,896]{1,0:T(8,128)(2,1)S(1)}, bf16[128,896]{1,0:T(8,128)(2,1)S(1)}, u32[]{:S(2)}, u32[]{:S(2)}) collective-permute-start(bf16[128,896]{1,0:T(8,128)(2,1)S(1)} %shard_map.119.refs_0_), channel_id=1, source_target_pairs={{0,1},{1,0},{2,3},{3,2},{4,5},{5,4},{6,7},{7,6},{8,9},{9,8},{10,11... | collective-permute-start | bytes 688136 | tf_op jit(solution)/shard_map/ppermute | solution.py:25
  78.9 6.0 %collective-permute-start.27 = (bf16[64,896]{1,0:T(8,128)(2,1)S(1)}, bf16[64,896]{1,0:T(8,128)(2,1)S(1)}, u32[]{:S(2)}, u32[]{:S(2)}) collective-permute-start(bf16[64,896]{1,0:T(8,128)(2,1)S(1)} %get-tuple-element.317.refs_0_), channel_id=1, source_target_pairs={{0,6},{1,7},{2,4},{3,5},{4,2},{5,3},{6,0},{7,1},{8,14},{9,15},{10,... | collective-permute-start | bytes 344072 | tf_op jit(solution)/shard_map/ppermute | solution.py:25
  82.0 6.1 %collective-permute-start.28 = (bf16[64,896]{1,0:T(8,128)(2,1)S(1)}, bf16[64,896]{1,0:T(8,128)(2,1)S(1)}, u32[]{:S(2)}, u32[]{:S(2)}) collective-permute-start(bf16[64,896]{1,0:T(8,128)(2,1)S(1)} %get-tuple-element.319.refs_0_), channel_id=1, source_target_pairs={{0,2},{1,3},{2,0},{3,1},{4,6},{5,7},{6,4},{7,5},{8,10},{9,11},{10,... | collective-permute-start | bytes 344072 | tf_op jit(solution)/shard_map/ppermute | solution.py:25
  82.0 11.0 %collective-permute-start.30 = (bf16[128,896]{1,0:T(8,128)(2,1)S(1)}, bf16[128,896]{1,0:T(8,128)(2,1)S(1)}, u32[]{:S(2)}, u32[]{:S(2)}) collective-permute-start(bf16[128,896]{1,0:T(8,128)(2,1)S(1)} %shard_map.120.refs_0_), channel_id=1, source_target_pairs={{0,2},{1,3},{2,0},{3,1},{4,6},{5,7},{6,4},{7,5},{8,10},{9,11},{10,... | collective-permute-start | bytes 688136 | tf_op jit(solution)/shard_map/ppermute | solution.py:25
  84.9 8.2 %collective-permute-start.31 = (bf16[128,896]{1,0:T(8,128)(2,1)S(1)}, bf16[128,896]{1,0:T(8,128)(2,1)S(1)}, u32[]{:S(2)}, u32[]{:S(2)}) collective-permute-start(bf16[128,896]{1,0:T(8,128)(2,1)S(1)} %shard_map.121.refs_0_), channel_id=1, source_target_pairs={{0,1},{1,0},{2,3},{3,2},{4,5},{5,4},{6,7},{7,6},{8,9},{9,8},{10,11... | collective-permute-start | bytes 688136 | tf_op jit(solution)/shard_map/ppermute | solution.py:25
  88.1 6.1 %collective-permute-start.32 = (bf16[128,896]{1,0:T(8,128)(2,1)S(1)}, bf16[128,896]{1,0:T(8,128)(2,1)S(1)}, u32[]{:S(2)}, u32[]{:S(2)}) collective-permute-start(bf16[128,896]{1,0:T(8,128)(2,1)S(1)} %shard_map.122.refs_0_), channel_id=1, source_target_pairs={{0,1},{1,0},{2,3},{3,2},{4,5},{5,4},{6,7},{7,6},{8,9},{9,8},{10,11... | collective-permute-start | bytes 688136 | tf_op jit(solution)/shard_map/ppermute | solution.py:25
  88.7 13.8 %collective-permute-start.33 = (bf16[256,896]{1,0:T(8,128)(2,1)S(1)}, bf16[256,896]{1,0:T(8,128)(2,1)S(1)}, u32[]{:S(2)}, u32[]{:S(2)}) collective-permute-start(bf16[256,896]{1,0:T(8,128)(2,1)S(1)} %shard_map.123.refs_0_), channel_id=1, source_target_pairs={{0,2},{1,3},{2,0},{3,1},{4,6},{5,7},{6,4},{7,5},{8,10},{9,11},{10,... | collective-permute-start | bytes 1376264 | tf_op jit(solution)/shard_map/ppermute | solution.py:25
  93.0 10.8 %collective-permute-start.34 = (bf16[256,896]{1,0:T(8,128)(2,1)S(1)}, bf16[256,896]{1,0:T(8,128)(2,1)S(1)}, u32[]{:S(2)}, u32[]{:S(2)}) collective-permute-start(bf16[256,896]{1,0:T(8,128)(2,1)S(1)} %shard_map.124.refs_0_), channel_id=1, source_target_pairs={{0,6},{1,7},{2,4},{3,5},{4,2},{5,3},{6,0},{7,1},{8,14},{9,15},{10,... | collective-permute-start | bytes 1376264 | tf_op jit(solution)/shard_map/ppermute | solution.py:25
  93.1 18.8 %collective-permute-start.37 = (bf16[256,896]{1,0:T(8,128)(2,1)S(1)}, bf16[256,896]{1,0:T(8,128)(2,1)S(1)}, u32[]{:S(2)}, u32[]{:S(2)}) collective-permute-start(bf16[256,896]{1,0:T(8,128)(2,1)S(1)} %shard_map.125.refs_0_), channel_id=1, source_target_pairs={{0,2},{1,3},{2,0},{3,1},{4,6},{5,7},{6,4},{7,5},{8,10},{9,11},{10,... | collective-permute-start | bytes 1376264 | tf_op jit(solution)/shard_map/ppermute | solution.py:25
  94.2 17.8 %collective-permute-start.38 = (bf16[256,896]{1,0:T(8,128)(2,1)S(1)}, bf16[256,896]{1,0:T(8,128)(2,1)S(1)}, u32[]{:S(2)}, u32[]{:S(2)}) collective-permute-start(bf16[256,896]{1,0:T(8,128)(2,1)S(1)} %shard_map.126.refs_0_), channel_id=1, source_target_pairs={{0,6},{1,7},{2,4},{3,5},{4,2},{5,3},{6,0},{7,1},{8,14},{9,15},{10,... | collective-permute-start | bytes 1376264 | tf_op jit(solution)/shard_map/ppermute | solution.py:25
  98.3 8.2 %collective-permute-start.35 = (bf16[64,896]{1,0:T(8,128)(2,1)S(1)}, bf16[64,896]{1,0:T(8,128)(2,1)S(1)}, u32[]{:S(2)}, u32[]{:S(2)}) collective-permute-start(bf16[64,896]{1,0:T(8,128)(2,1)S(1)} %get-tuple-element.337.refs_0_), channel_id=1, source_target_pairs={{0,1},{1,0},{2,3},{3,2},{4,5},{5,4},{6,7},{7,6},{8,9},{9,8},{10,11... | collective-permute-start | bytes 344072 | tf_op jit(solution)/shard_map/ppermute | solution.py:25
  102.6 4.8 %collective-permute-start.36 = (bf16[64,896]{1,0:T(8,128)(2,1)S(1)}, bf16[64,896]{1,0:T(8,128)(2,1)S(1)}, u32[]{:S(2)}, u32[]{:S(2)}) collective-permute-start(bf16[64,896]{1,0:T(8,128)(2,1)S(1)} %get-tuple-element.339.refs_0_), channel_id=1, source_target_pairs={{0,1},{1,0},{2,3},{3,2},{4,5},{5,4},{6,7},{7,6},{8,9},{9,8},{10,11... | collective-permute-start | bytes 344072 | tf_op jit(solution)/shard_map/ppermute | solution.py:25
  113.4 2.8 %collective-permute-start.39 = (f32[256,1024]{1,0:T(8,128)S(1)}, f32[256,1024]{1,0:T(8,128)S(1)}, u32[]{:S(2)}, u32[]{:S(2)}) collective-permute-start(f32[256,1024]{1,0:T(8,128)S(1)} %shard_map.137), channel_id=1, source_target_pairs={{0,8},{8,0},{16,24},{24,16},{32,40},{40,32},{48,56},{56,48},{64,72... | collective-permute-start | bytes 3145736 | tf_op jit(solution)/shard_map/ppermute | solution.py:25
  113.5 8.0 %collective-permute-start.40 = (bf16[128,896]{1,0:T(8,128)(2,1)S(1)}, bf16[128,896]{1,0:T(8,128)(2,1)S(1)}, u32[]{:S(2)}, u32[]{:S(2)}) collective-permute-start(bf16[128,896]{1,0:T(8,128)(2,1)S(1)} %shard_map.131.refs_0_), channel_id=1, source_target_pairs={{0,2},{1,3},{2,0},{3,1},{4,6},{5,7},{6,4},{7,5},{8,10},{9,11},{10,... | collective-permute-start | bytes 688136 | tf_op jit(solution)/shard_map/ppermute | solution.py:25
  113.7 9.1 %collective-permute-start.41 = (bf16[128,896]{1,0:T(8,128)(2,1)S(1)}, bf16[128,896]{1,0:T(8,128)(2,1)S(1)}, u32[]{:S(2)}, u32[]{:S(2)}) collective-permute-start(bf16[128,896]{1,0:T(8,128)(2,1)S(1)} %shard_map.132.refs_0_), channel_id=1, source_target_pairs={{0,6},{1,7},{2,4},{3,5},{4,2},{5,3},{6,0},{7,1},{8,14},{9,15},{10,... | collective-permute-start | bytes 688136 | tf_op jit(solution)/shard_map/ppermute | solution.py:25
  116.3 9.4 %collective-permute-start.42 = (bf16[64,1024]{1,0:T(8,128)(2,1)S(1)}, bf16[64,1024]{1,0:T(8,128)(2,1)S(1)}, u32[]{:S(2)}, u32[]{:S(2)}) collective-permute-start(bf16[64,1024]{1,0:T(8,128)(2,1)S(1)} %get-tuple-element.367), channel_id=1, source_target_pairs={{0,32},{8,40},{16,48},{24,56},{32,0},{40,8},{48,16},{56,24},{64,96... | collective-permute-start | bytes 393224 | tf_op jit(solution)/shard_map/ppermute | solution.py:25
  116.4 9.6 %collective-permute-start.43 = (bf16[64,1024]{1,0:T(8,128)(2,1)S(1)}, bf16[64,1024]{1,0:T(8,128)(2,1)S(1)}, u32[]{:S(2)}, u32[]{:S(2)}) collective-permute-start(bf16[64,1024]{1,0:T(8,128)(2,1)S(1)} %get-tuple-element.368), channel_id=1, source_target_pairs={{0,96},{8,104},{16,112},{24,120},{32,64},{40,72},{48,80},{56,88},{... | collective-permute-start | bytes 393224 | tf_op jit(solution)/shard_map/ppermute | solution.py:25
  117.7 8.3 %collective-permute-start.44 = (bf16[64,1024]{1,0:T(8,128)(2,1)S(1)}, bf16[64,1024]{1,0:T(8,128)(2,1)S(1)}, u32[]{:S(2)}, u32[]{:S(2)}) collective-permute-start(bf16[64,1024]{1,0:T(8,128)(2,1)S(1)} %get-tuple-element.369), channel_id=1, source_target_pairs={{0,64},{8,72},{16,80},{24,88},{32,96},{40,104},{48,112},{56,120},{... | collective-permute-start | bytes 393224 | tf_op jit(solution)/shard_map/ppermute | solution.py:25
  121.5 13.4 %collective-permute-start.46 = (bf16[256,896]{1,0:T(8,128)(2,1)S(1)}, bf16[256,896]{1,0:T(8,128)(2,1)S(1)}, u32[]{:S(2)}, u32[]{:S(2)}) collective-permute-start(bf16[256,896]{1,0:T(8,128)(2,1)S(1)} %shard_map.140.refs_0_), channel_id=1, source_target_pairs={{0,6},{1,7},{2,4},{3,5},{4,2},{5,3},{6,0},{7,1},{8,14},{9,15},{10,... | collective-permute-start | bytes 1376264 | tf_op jit(solution)/shard_map/ppermute | solution.py:25
  122.9 14.2 %collective-permute-start.47 = (bf16[256,896]{1,0:T(8,128)(2,1)S(1)}, bf16[256,896]{1,0:T(8,128)(2,1)S(1)}, u32[]{:S(2)}, u32[]{:S(2)}) collective-permute-start(bf16[256,896]{1,0:T(8,128)(2,1)S(1)} %shard_map.141.refs_0_), channel_id=1, source_target_pairs={{0,2},{1,3},{2,0},{3,1},{4,6},{5,7},{6,4},{7,5},{8,10},{9,11},{10,... | collective-permute-start | bytes 1376264 | tf_op jit(solution)/shard_map/ppermute | solution.py:25
  126.0 6.9 %collective-permute-start.45 = (f32[32,1024]{1,0:T(8,128)S(1)}, f32[32,1024]{1,0:T(8,128)S(1)}, u32[]{:S(2)}, u32[]{:S(2)}) collective-permute-start(f32[32,1024]{1,0:T(8,128)S(1)} %get-tuple-element.373), channel_id=1, source_target_pairs={{0,16},{8,24},{16,0},{24,8},{32,48},{40,56},{48,32},{56,40},{64,80... | collective-permute-start | bytes 393224 | tf_op jit(solution)/shard_map/ppermute | solution.py:25

commit v3 on v2

--- a/solution.py
+++ b/solution.py
@@ -105,30 +105,6 @@
     )
 
 
-def stack_kernel(a_ref, b_ref, out_ref, sems):
-    n = a_ref.shape[0]
-    copies = [
-        pltpu.make_async_copy(ref, out_ref.at[k * n : (k + 1) * n], sems.at[k])
-        for k, ref in enumerate((a_ref, b_ref))
-    ]
-    for copy in copies:
-        copy.start()
-    for copy in copies:
-        copy.wait()
-
-
-def stack(a, b):
-    return pl.pallas_call(
-        stack_kernel,
-        out_shape=jax.ShapeDtypeStruct((2 * a.shape[0], a.shape[1]), a.dtype),
-        in_specs=[pl.BlockSpec(memory_space=pltpu.HBM)] * 2,
-        out_specs=IN_VMEM,
-        scratch_shapes=[pltpu.SemaphoreType.DMA((2,))],
-        compiler_params=PARAMS,
-        cost_estimate=SHORT,
-    )(a, b)
-
-
 def part_kernel(w_dim, dims, first, cols, mine_ref, x_ref, w_ref, out_ref, x_scr):
     rows = x_ref.shape[1]
     for k in range(4):
@@ -180,6 +156,30 @@
     return order.run(small(swiglu_kernel, [shape] * 3, 6), *args)
 
 
+def beside_kernel(a_ref, b_ref, out_ref):
+    width = a_ref.shape[1]
+    out_ref[:, :width] = a_ref[...]
+    out_ref[:, width:] = b_ref[...]
+
+
+def beside(order, a, b):
+    shape = jax.ShapeDtypeStruct((a.shape[0], a.shape[1] + b.shape[1]), a.dtype)
+    return order.run(small(beside_kernel, [shape], 2), a, b)[0]
+
+
+def split_kernel(near_ref, far_ref, *out_refs):
+    rows, width = near_ref.shape[0], out_refs[0].shape[1]
+    for k, ref in enumerate(out_refs):
+        here = slice(k * width, (k + 1) * width)
+        ref[:rows, :] = near_ref[:, here]
+        ref[rows:, :] = far_ref[:, here]
+
+
+def split(order, near, far, count):
+    shape = jax.ShapeDtypeStruct((2 * near.shape[0], near.shape[1] // count), near.dtype)
+    return order.run(small(split_kernel, [shape] * count, 2), near, far)
+
+
 def reorder(dims, mine_ref, blocks_ref, out_ref):
     rows = blocks_ref.shape[1]
     for place in range(8):
@@ -192,69 +192,60 @@
 LAST = (((1,), (1,)), ((), ()))
 
 
-def grad_pieces(out_ref, out_scr, sems, rows_at, cols, pieces):
+def grads_kernel(jobs, mine_ref, *refs):
+    count = len(jobs)
+    lefts, grads = refs[:count], refs[count : 2 * count]
+    kinds = sorted({kind for kind, _, _ in jobs})
+    out_refs, (scrs, out_scrs, sems) = refs[-len(kinds) - 3 : -3], refs[-3:]
     copies = []
-    for k, (rows, value) in enumerate(pieces):
-        out_scr[rows, :] = value().astype(BF16)
-        there = slice(rows_at + rows.start, rows_at + rows.stop)
-        copies.append(
-            pltpu.make_async_copy(out_scr.at[rows], out_ref.at[there, cols], sems.at[k])
-        )
-        copies[-1].start()
+    for k, (kind, dims, cols) in enumerate(jobs):
+        left_scr, out_scr, out_ref = scrs[k], out_scrs[k], out_refs[kinds.index(kind)]
+        reorder(dims, mine_ref, lefts[k], left_scr)
+        size = out_scr.shape[0]
+        half = -(-size // 256) * 128
+        for rows in (slice(0, half), slice(half, size)):
+            if kind < 2:
+                a, b = left_scr[:, rows], grads[k][...]
+                there = out_ref.at[rows, cols]
+            else:
+                a, b = grads[k][:, rows], left_scr[...]
+                there = out_ref.at[cols.start + rows.start : cols.start + rows.stop]
+            out_scr[rows, :] = lax.dot_general(
+                a, b, FIRST, preferred_element_type=F32
+            ).astype(BF16)
+            copies.append(pltpu.make_async_copy(out_scr.at[rows], there, sems.at[len(copies)]))
+            copies[-1].start()
     for copy in copies:
         copy.wait()
 
 
-def wide_kernel(dims, cols, mine_ref, x_ref, grad_ref, *rest):
-    out_ref, x_scr, out_scr, sems = rest[-4:]
-    reorder(dims, mine_ref, x_ref, x_scr)
-    half = out_scr.shape[0] // 2
-
-    def product(rows):
-        return lambda: lax.dot_general(
-            x_scr[:, rows], grad_ref[...], FIRST, preferred_element_type=F32
-        )
-
-    parts = (slice(0, half), slice(half, 2 * half))
-    grad_pieces(out_ref, out_scr, sems, 0, cols, [(rows, product(rows)) for rows in parts])
-
-
-def tall_kernel(dims, at, mine_ref, g_ref, hidden_ref, *rest):
-    out_ref, g_scr, out_scr, sems = rest[-4:]
-    reorder(dims, mine_ref, g_ref, g_scr)
-    width = out_scr.shape[0]
-    half = -(-width // 256) * 128
-
-    def product(rows):
-        return lambda: lax.dot_general(
-            hidden_ref[:, rows], g_scr[...], FIRST, preferred_element_type=F32
-        )
-
-    parts = (slice(0, half), slice(half, width))
-    grad_pieces(
-        out_ref, out_scr, sems, at, slice(None), [(rows, product(rows)) for rows in parts]
-    )
-
-
-def weight_grad(order, kernel, shape, piece, blocks, grad, before):
-    _, rows, depth = blocks.shape
-    tokens, width = grad.shape
-    more = [] if before is None else [before]
+def weight_grads(order, jobs, lefts, grads, shapes, befores):
+    kinds = sorted({kind for kind, _, _ in jobs})
+    in_hbm = pl.BlockSpec(memory_space=pltpu.HBM)
+    known = [(at, befores[k]) for at, k in enumerate(kinds) if befores[k] is not None]
+    sizes = [
+        (shapes[kind][0], cols.stop - cols.start)
+        if kind < 2
+        else (cols.stop - cols.start, shapes[kind][1])
+        for kind, _, cols in jobs
+    ]
+    flat = [(v.shape[0] * v.shape[1], v.shape[2]) for v in lefts]
+    first = 1 + 2 * len(jobs)
     call = pl.pallas_call(
-        kernel,
-        out_shape=jax.ShapeDtypeStruct(shape, BF16),
-        in_specs=[IN_SMEM, IN_VMEM, IN_VMEM] + [pl.BlockSpec(memory_space=pltpu.HBM)] * len(more),
-        out_specs=pl.BlockSpec(memory_space=pl.ANY),
+        functools.partial(grads_kernel, jobs),
+        out_shape=[jax.ShapeDtypeStruct(shapes[k], BF16) for k in kinds],
+        in_specs=[IN_SMEM] + [IN_VMEM] * (2 * len(jobs)) + [in_hbm] * len(known),
+        out_specs=[pl.BlockSpec(memory_space=pl.ANY)] * len(kinds),
         scratch_shapes=[
-            pltpu.VMEM((tokens, depth), BF16),
-            pltpu.VMEM(piece, BF16),
-            pltpu.SemaphoreType.DMA((2,)),
+            [pltpu.VMEM(shape, BF16) for shape in flat],
+            [pltpu.VMEM(size, BF16) for size in sizes],
+            pltpu.SemaphoreType.DMA((2 * len(jobs),)),
         ],
-        input_output_aliases={3: 0} if more else {},
+        input_output_aliases={first + at: k for at, (k, _) in enumerate(known)},
         compiler_params=PARAMS,
         cost_estimate=SHORT,
     )
-    return order.run(call, blocks, grad, *more)
+    return order.run(call, *lefts, *grads, *(b for _, b in known))
 
 
 def input_kernel(first, gate_dims, up_dims, cols, mine_ref, gg_ref, ug_ref, wg_ref, wu_ref, *rest):
@@ -327,23 +318,20 @@
     size = width // CHUNKS
     chunks = [slice(k * size, (k + 1) * size) for k in range(CHUNKS)]
     n = inputs.shape[0]
-    own = stack(inputs, out_grad)
-    far = swap(own, "row", ZHI)
+    far_x, far_g = swap(inputs, "row", ZHI), swap(out_grad, "row", ZHI)
     weights = [fetch(order, gate_weight)]
-    x, g = join(order, (own, far), ((0, 0, n), (1, 0, n)), ((0, n, n), (1, n, n)))
-    far_x, far_g = swap(x, "row", XA), swap(g, "row", XB)
+    both = join(order, (inputs, far_x, out_grad, far_g), tuple((k, 0, n) for k in range(4)))
+    n = 2 * n
+    fars = [swap(both, "row", mask) for mask in (XA, XB, XAB)]
     weights.append(fetch(order, up_weight))
-    n = 2 * n
-    x, g = join(order, (x, far_x, g, far_g), ((0, 0, n), (1, 0, n)), ((2, 0, n), (3, 0, n)))
-    far_x, far_g = swap(x, "row", XB), swap(g, "row", XA)
-    weights.append(fetch(order, down_weight))
     x, g = join(
         order,
-        (x, far_x, g, far_g),
-        ((0, 0, 2 * n), (1, 0, 2 * n)),
-        ((2, 0, n), (3, 0, n), (2, n, n), (3, n, n)),
+        (both, *fars),
+        tuple((k, 0, n) for k in range(4)),
+        tuple((k, n, n) for k in range(4)),
     )
     far_x, far_g = swap(x, "row", CORE), swap(g, "row", CORE)
+    weights.append(fetch(order, down_weight))
     x = join(order, (x, far_x), ((0, 0, 4 * n), (1, 0, 4 * n))).reshape(8, n, -1)
 
     w_dims = (0, 0, 1)
@@ -357,19 +345,22 @@
             order, lefts[k], weights[k], w_dims[k], SUM_DIMS[i], first, chunks[c], dtype
         )
 
-    for i, (_, k) in enumerate(items):
+    grads = [None] * len(items)
+
+    def send_step(i):
+        k = items[i][1]
         if lefts[k] is None:
             lefts[k] = join(order, (g, far_g), ((0, 0, 4 * n), (1, 0, 4 * n))).reshape(x.shape)
         fars[i] = swap(part(i, 4, BF16), "col", COL[SUM_DIMS[i][0]])
-    for step in (1, 2):
-        for i, dims in enumerate(SUM_DIMS):
-            if step == 1:
-                totals[i] = part(i, 0, F32)
-            send, totals[i] = halve(order, totals[i], fars[i])
-            fars[i] = swap(send, "col", COL[dims[step]])
-
-    grads = [None] * len(items)
-    for c in range(CHUNKS):
+
+    def keep_step(i):
+        totals[i] = part(i, 0, F32)
+
+    def halve_step(step, i):
+        send, totals[i] = halve(order, totals[i], fars[i])
+        fars[i] = swap(send, "col", COL[SUM_DIMS[i][step]])
+
+    def swiglu_step(c):
         these = slice(3 * c, 3 * c + 3)
         hidden, gate_grad, up_grad = swiglu(order, totals[these], fars[these])
         grads[these] = gate_grad, up_grad, hidden
@@ -384,35 +375,69 @@
             fars[i] = swap(grads[i], "col", COL[GATHER_DIMS[i][step]])
 
     out = [None] * 3
-    shapes = (((depth, width), (depth, size)),) * 2 + (((width, depth), (size, depth)),)
-
-    def weight_step(i):
-        c, k = items[i]
-        place = GATHER_DIMS[i][::-1]
-        kernel = (
-            functools.partial(wide_kernel, place, chunks[c])
-            if k < 2
-            else functools.partial(tall_kernel, place, chunks[c].start)
+    shapes = ((depth, width), (depth, width), (width, depth))
+
+    def weight_step(*parts):
+        kinds = [items[i][1] for i in parts]
+        jobs = [(k, GATHER_DIMS[i][::-1], chunks[items[i][0]]) for i, k in zip(parts, kinds)]
+        results = weight_grads(
+            order,
+            jobs,
+            [lefts[k] for k in kinds],
+            [grads[i] for i in parts],
+            shapes,
+            out,
         )
-        out[k] = weight_grad(order, kernel, *shapes[k], lefts[k], grads[i], out[k])
+        for k, result in zip(sorted(set(kinds)), results):
+            out[k] = result
 
     def input_step(c, first, before):
         these = slice(3 * c, 3 * c + 2)
         places = [dims[::-1] for dims in GATHER_DIMS[these]]
         return input_part(order, first, grads[these], places, weights[:2], chunks[c], before)
 
-    for step in (1, 2):
-        for i in (0, 1, 3, 4):
-            grow(i, step)
-    grow(2, 0)
-    grow(5, 0)
+    send_step(0)
+    send_step(1)
+    send_step(2)
+    send_step(3)
+    send_step(4)
+    keep_step(0)
+    keep_step(1)
+    keep_step(2)
+    keep_step(3)
+    send_step(5)
+    halve_step(1, 0)
+    halve_step(1, 1)
+    halve_step(1, 2)
+    halve_step(1, 3)
+    keep_step(4)
+    halve_step(1, 4)
+    keep_step(5)
+    halve_step(1, 5)
+    halve_step(2, 0)
+    halve_step(2, 1)
+    halve_step(2, 2)
+    halve_step(2, 3)
+    halve_step(2, 4)
+    halve_step(2, 5)
+    swiglu_step(0)
+    swiglu_step(1)
+    grow(0, 1)
+    grow(1, 1)
+    both = beside(order, grads[2], grads[5])
+    far = swap(both, "col", COL[GATHER_DIMS[2][0]])
+    grow(3, 1)
+    grow(4, 1)
+    grow(0, 2)
+    grow(1, 2)
+    grow(3, 2)
+    grow(4, 2)
+    grads[2], grads[5] = split(order, both, far, CHUNKS)
+    for i in (2, 5):
+        fars[i] = swap(grads[i], "col", COL[GATHER_DIMS[i][1]])
     grow(0, 3)
     grow(1, 3)
     send, keep = input_step(0, 4, None), input_step(0, 0, None)
-    grow(2, 1)
-    grow(5, 1)
-    weight_step(0)
-    weight_step(1)
     grow(3, 3)
     grow(4, 3)
     send = input_step(1, 4, send)
@@ -433,14 +458,14 @@
     rings = [swap(v, "row", mask) for v, mask in zip(sends, (XA, XB, XAB))]
     grow(2, 2)
     grow(5, 2)
-    weight_step(3)
+    weight_step(0, 1)
     shape = jax.ShapeDtypeStruct((n // 2, depth), F32)
     keep, send = order.run(small(ring_kernel, [shape, shape], 4), own, *rings)
     far = swap(send, "row", ZHI)
-    weight_step(4)
-    for i in (2, 5):
-        grow(i, 3)
-        weight_step(i)
+    weight_step(3, 4)
+    grow(2, 3)
+    grow(5, 3)
+    weight_step(2, 5)
     input_grad = (keep + far).astype(BF16)
     return (input_grad, *out)
 

time: 140 us -> 134 us (0.957)
  starting transfers between devices: 64.6 us -> 56.9 us
  waiting for transfers between devices: 38.9 us -> 46 us
  Pallas kernels: 30 us -> 26.5 us
  local copies, waits for them, and re-layouts: 3.72 us -> 2.06 us
    ppermute x48 -> x47, starting transfers between devices: 64.6 us -> 56.9 us  [swap(): return lax.ppermute(value, axis, [(i, i ^ mask) for i in range(size)])]
    ppermute x48 -> x47, waiting for transfers between devices: 38.9 us -> 46 us  [swap(): return lax.ppermute(value, axis, [(i, i ^ mask) for i in range(size)])]
    pallas_call x64 -> x60, Pallas kernels: 29.9 us -> 26.5 us  [run(): out = call(self.mine, *args)]
    unnamed x10, local copies, waits for them, and re-layouts: 3.72 us -> 2.06 us
  transfers between devices with their start and end apart: 48 -> 47, of which waited for: 22 -> 29; matrix products, arithmetic and copies ran while one was open for 0% -> 0% of each run, Pallas kernels for 19% -> 16%
where the time goes in v3:
time: 134 us; the launch traced here: 133 us
  starting transfers between devices  56.9 us (42%)
  waiting for transfers between devices  46 us (34%)
  Pallas kernels  26.5 us (20%)
  local copies, waits for them, and re-layouts  2.06 us (2%)
    ppermute x47, starting transfers between devices, swap(): return lax.ppermute(value, axis, [(i, i ^ mask) for i in range(size)])  56.9 us
    ppermute x47, waiting for transfers between devices, swap(): return lax.ppermute(value, axis, [(i, i ^ mask) for i in range(size)])  46 us
    pallas_call x60, Pallas kernels, run(): out = call(self.mine, *args)  26.5 us
  transfers between devices with their start and end apart: 47, of which 29 were waited for; matrix products, arithmetic and copies ran while one was open for 0% of the time, Pallas kernels for 16%

profile of v3, /device:TPU:0, one launch (start us, length us, event | category | flops | bytes accessed | tf_op | source)
XLA Modules:
  0.0 133.5 jit_solution(7383682288380481970)
XLA Ops:
  0.6 4.0 %collective-permute-start = (bf16[32,1024]{1,0:T(8,128)(2,1)}, bf16[32,1024]{1,0:T(8,128)(2,1)S(1)}, u32[]{:S(2)}, u32[]{:S(2)}) collective-permute-start(bf16[32,1024]{1,0:T(8,128)(2,1)} %refs_0_.1), channel_id=1, source_target_pairs={{0,16},{8,24},{16,0},{24,8},{32,48},{40,56},{48,32},{56,40},{64,80... | collective-permute-start | bytes 196616 | tf_op jit(solution)/shard_map/ppermute | solution.py:25
  4.8 2.0 %copy-done = bf16[1024,1792]{1,0:T(8,128)(2,1)S(1)} copy-done((bf16[1024,1792]{1,0:T(8,128)(2,1)S(1)}, bf16[1024,1792]{1,0:T(8,128)(2,1)}, u32[]{:S(2)}) %copy-start) | copy-done | bytes 3670040
  7.1 3.5 %collective-permute-done.1.refs_3_ = bf16[32,1024]{1,0:T(8,128)(2,1)S(1)} collective-permute-done((bf16[32,1024]{1,0:T(8,128)(2,1)}, bf16[32,1024]{1,0:T(8,128)(2,1)S(1)}, u32[]{:S(2)}, u32[]{:S(2)}) %collective-permute-start.1) | collective-permute-done | bytes 65568 | tf_op jit(solution)/shard_map/ppermute | solution.py:25
  10.7 1.6 %collective-permute-start.2 = (bf16[128,1024]{1,0:T(8,128)(2,1)S(1)}, bf16[128,1024]{1,0:T(8,128)(2,1)S(1)}, u32[]{:S(2)}, u32[]{:S(2)}) collective-permute-start(bf16[128,1024]{1,0:T(8,128)(2,1)S(1)} %shard_map.85.refs_0_), channel_id=1, source_target_pairs={{0,32},{8,40},{16,48},{24,56},{32,0},{40,8},{48,16},{56,24},{64,96... | collective-permute-start | bytes 786440 | tf_op jit(solution)/shard_map/ppermute | solution.py:25
  12.3 2.1 %collective-permute-start.3 = (bf16[128,1024]{1,0:T(8,128)(2,1)S(1)}, bf16[128,1024]{1,0:T(8,128)(2,1)S(1)}, u32[]{:S(2)}, u32[]{:S(2)}) collective-permute-start(bf16[128,1024]{1,0:T(8,128)(2,1)S(1)} %shard_map.85.refs_0_), channel_id=1, source_target_pairs={{0,96},{8,104},{16,112},{24,120},{32,64},{40,72},{48,80},{56,88},{... | collective-permute-start | bytes 786440 | tf_op jit(solution)/shard_map/ppermute | solution.py:25
  15.3 4.7 %collective-permute-done.2.refs_1_ = bf16[128,1024]{1,0:T(8,128)(2,1)S(1)} collective-permute-done((bf16[128,1024]{1,0:T(8,128)(2,1)S(1)}, bf16[128,1024]{1,0:T(8,128)(2,1)S(1)}, u32[]{:S(2)}, u32[]{:S(2)}) %collective-permute-start.2) | collective-permute-done | bytes 262176 | tf_op jit(solution)/shard_map/ppermute | solution.py:25
  20.0 5.4 %collective-permute-done.3.refs_2_ = bf16[128,1024]{1,0:T(8,128)(2,1)S(1)} collective-permute-done((bf16[128,1024]{1,0:T(8,128)(2,1)S(1)}, bf16[128,1024]{1,0:T(8,128)(2,1)S(1)}, u32[]{:S(2)}, u32[]{:S(2)}) %collective-permute-start.3) | collective-permute-done | bytes 262176 | tf_op jit(solution)/shard_map/ppermute | solution.py:25
  26.4 1.1 collective-permute-done.5.refs_1_
  28.3 1.7 %collective-permute-start.7 = (bf16[256,896]{1,0:T(8,128)(2,1)S(1)}, bf16[256,896]{1,0:T(8,128)(2,1)S(1)}, u32[]{:S(2)}, u32[]{:S(2)}) collective-permute-start(bf16[256,896]{1,0:T(8,128)(2,1)S(1)} %shard_map.90), channel_id=1, source_target_pairs={{0,2},{1,3},{2,0},{3,1},{4,6},{5,7},{6,4},{7,5},{8,10},{9,11},{10,... | collective-permute-start | bytes 1376264 | tf_op jit(solution)/shard_map/ppermute | solution.py:25
  30.7 2.3 %collective-permute-start.8 = (bf16[256,896]{1,0:T(8,128)(2,1)S(1)}, bf16[256,896]{1,0:T(8,128)(2,1)S(1)}, u32[]{:S(2)}, u32[]{:S(2)}) collective-permute-start(bf16[256,896]{1,0:T(8,128)(2,1)S(1)} %shard_map.91), channel_id=1, source_target_pairs={{0,6},{1,7},{2,4},{3,5},{4,2},{5,3},{6,0},{7,1},{8,14},{9,15},{10,... | collective-permute-start | bytes 1376264 | tf_op jit(solution)/shard_map/ppermute | solution.py:25
  33.0 0.7 shard_map.93
  33.8 1.1 collective-permute-start.9
  35.6 0.8 collective-permute-start.10
  39.2 0.7 shard_map.98.refs_0_
  40.7 0.7 shard_map.100
  41.7 1.0 collective-permute-start.12
  42.8 2.5 %collective-permute-done.8.refs_1_ = bf16[256,896]{1,0:T(8,128)(2,1)S(1)} collective-permute-done((bf16[256,896]{1,0:T(8,128)(2,1)S(1)}, bf16[256,896]{1,0:T(8,128)(2,1)S(1)}, u32[]{:S(2)}, u32[]{:S(2)}) %collective-permute-start.8) | collective-permute-done | bytes 458784 | tf_op jit(solution)/shard_map/ppermute | solution.py:25
  45.4 2.2 %collective-permute-start.13 = (bf16[128,896]{1,0:T(8,128)(2,1)S(1)}, bf16[128,896]{1,0:T(8,128)(2,1)S(1)}, u32[]{:S(2)}, u32[]{:S(2)}) collective-permute-start(bf16[128,896]{1,0:T(8,128)(2,1)S(1)} %get-tuple-element.251), channel_id=1, source_target_pairs={{0,6},{1,7},{2,4},{3,5},{4,2},{5,3},{6,0},{7,1},{8,14},{9,15},{10,... | collective-permute-start | bytes 688136 | tf_op jit(solution)/shard_map/ppermute | solution.py:25
  47.6 1.1 collective-permute-start.14
  48.8 2.0 %collective-permute-done.10.refs_1_ = bf16[256,896]{1,0:T(8,128)(2,1)S(1)} collective-permute-done((bf16[256,896]{1,0:T(8,128)(2,1)S(1)}, bf16[256,896]{1,0:T(8,128)(2,1)S(1)}, u32[]{:S(2)}, u32[]{:S(2)}) %collective-permute-start.10) | collective-permute-done | bytes 458784 | tf_op jit(solution)/shard_map/ppermute | solution.py:25
  50.8 1.6 %collective-permute-start.15 = (bf16[128,896]{1,0:T(8,128)(2,1)S(1)}, bf16[128,896]{1,0:T(8,128)(2,1)S(1)}, u32[]{:S(2)}, u32[]{:S(2)}) collective-permute-start(bf16[128,896]{1,0:T(8,128)(2,1)S(1)} %get-tuple-element.261), channel_id=1, source_target_pairs={{0,2},{1,3},{2,0},{3,1},{4,6},{5,7},{6,4},{7,5},{8,10},{9,11},{10,... | collective-permute-start | bytes 688136 | tf_op jit(solution)/shard_map/ppermute | solution.py:25
  53.1 2.1 %collective-permute-done.11.refs_1_ = bf16[256,896]{1,0:T(8,128)(2,1)S(1)} collective-permute-done((bf16[256,896]{1,0:T(8,128)(2,1)S(1)}, bf16[256,896]{1,0:T(8,128)(2,1)S(1)}, u32[]{:S(2)}, u32[]{:S(2)}) %collective-permute-start.11) | collective-permute-done | bytes 458784 | tf_op jit(solution)/shard_map/ppermute | solution.py:25
  55.2 2.2 %collective-permute-start.16 = (bf16[128,896]{1,0:T(8,128)(2,1)S(1)}, bf16[128,896]{1,0:T(8,128)(2,1)S(1)}, u32[]{:S(2)}, u32[]{:S(2)}) collective-permute-start(bf16[128,896]{1,0:T(8,128)(2,1)S(1)} %get-tuple-element.266), channel_id=1, source_target_pairs={{0,6},{1,7},{2,4},{3,5},{4,2},{5,3},{6,0},{7,1},{8,14},{9,15},{10,... | collective-permute-start | bytes 688136 | tf_op jit(solution)/shard_map/ppermute | solution.py:25
  57.4 0.7 shard_map.107.refs_0_
  58.2 1.1 collective-permute-start.17
  60.2 1.9 %collective-permute-done.14.refs_1_ = bf16[128,896]{1,0:T(8,128)(2,1)S(1)} collective-permute-done((bf16[128,896]{1,0:T(8,128)(2,1)S(1)}, bf16[128,896]{1,0:T(8,128)(2,1)S(1)}, u32[]{:S(2)}, u32[]{:S(2)}) %collective-permute-start.14) | collective-permute-done | bytes 229408 | tf_op jit(solution)/shard_map/ppermute | solution.py:25
  62.1 1.2 collective-permute-start.21
  63.3 1.2 collective-permute-done.16.refs_1_
  64.7 1.0 collective-permute-start.19
  65.8 0.8 collective-permute-done.18.refs_1_
  66.6 2.2 %collective-permute-start.24 = (bf16[64,896]{1,0:T(8,128)(2,1)S(1)}, bf16[64,896]{1,0:T(8,128)(2,1)S(1)}, u32[]{:S(2)}, u32[]{:S(2)}) collective-permute-start(bf16[64,896]{1,0:T(8,128)(2,1)S(1)} %get-tuple-element.295), channel_id=1, source_target_pairs={{0,6},{1,7},{2,4},{3,5},{4,2},{5,3},{6,0},{7,1},{8,14},{9,15},{10,... | collective-permute-start | bytes 344072 | tf_op jit(solution)/shard_map/ppermute | solution.py:25
  68.9 1.1 collective-permute-start.23
  69.9 1.0 collective-permute-start.22
  71.1 1.9 %collective-permute-start.25 = (bf16[64,896]{1,0:T(8,128)(2,1)S(1)}, bf16[64,896]{1,0:T(8,128)(2,1)S(1)}, u32[]{:S(2)}, u32[]{:S(2)}) collective-permute-start(bf16[64,896]{1,0:T(8,128)(2,1)S(1)} %get-tuple-element.300.refs_0_), channel_id=1, source_target_pairs={{0,6},{1,7},{2,4},{3,5},{4,2},{5,3},{6,0},{7,1},{8,14},{9,15},{10,... | collective-permute-start | bytes 344072 | tf_op jit(solution)/shard_map/ppermute | solution.py:25
  73.1 1.0 collective-permute-start.26
  74.9 1.3 collective-permute-start.27
  76.4 0.8 collective-permute-done.25.refs_1_
  77.2 1.1 collective-permute-start.29
  79.0 1.1 collective-permute-start.30
  80.2 0.9 collective-permute-done.27.refs_1_
  81.0 1.1 collective-permute-start.31
  82.1 1.1 collective-permute-start.32
  83.2 2.6 %collective-permute-done.29.refs_1_ = bf16[128,896]{1,0:T(8,128)(2,1)S(1)} collective-permute-done((bf16[128,896]{1,0:T(8,128)(2,1)S(1)}, bf16[128,896]{1,0:T(8,128)(2,1)S(1)}, u32[]{:S(2)}, u32[]{:S(2)}) %collective-permute-start.29) | collective-permute-done | bytes 229408 | tf_op jit(solution)/shard_map/ppermute | solution.py:25
  85.9 1.1 collective-permute-start.34
  87.2 1.9 %collective-permute-start.35 = (bf16[256,896]{1,0:T(8,128)(2,1)S(1)}, bf16[256,896]{1,0:T(8,128)(2,1)S(1)}, u32[]{:S(2)}, u32[]{:S(2)}) collective-permute-start(bf16[256,896]{1,0:T(8,128)(2,1)S(1)} %shard_map.123.refs_0_), channel_id=1, source_target_pairs={{0,6},{1,7},{2,4},{3,5},{4,2},{5,3},{6,0},{7,1},{8,14},{9,15},{10,... | collective-permute-start | bytes 1376264 | tf_op jit(solution)/shard_map/ppermute | solution.py:25
  89.2 1.0 collective-permute-done.31.refs_1_
  90.4 2.2 %collective-permute-done.32.refs_1_ = bf16[128,896]{1,0:T(8,128)(2,1)S(1)} collective-permute-done((bf16[128,896]{1,0:T(8,128)(2,1)S(1)}, bf16[128,896]{1,0:T(8,128)(2,1)S(1)}, u32[]{:S(2)}, u32[]{:S(2)}) %collective-permute-start.32) | collective-permute-done | bytes 229408 | tf_op jit(solution)/shard_map/ppermute | solution.py:25
  92.6 1.5 %collective-permute-start.37 = (bf16[256,896]{1,0:T(8,128)(2,1)S(1)}, bf16[256,896]{1,0:T(8,128)(2,1)S(1)}, u32[]{:S(2)}, u32[]{:S(2)}) collective-permute-start(bf16[256,896]{1,0:T(8,128)(2,1)S(1)} %shard_map.125.refs_0_), channel_id=1, source_target_pairs={{0,6},{1,7},{2,4},{3,5},{4,2},{5,3},{6,0},{7,1},{8,14},{9,15},{10,... | collective-permute-start | bytes 1376264 | tf_op jit(solution)/shard_map/ppermute | solution.py:25
  94.1 1.0 collective-permute-start.33
  95.1 5.0 %collective-permute-done.33.refs_1_ = bf16[64,1792]{1,0:T(8,128)(2,1)S(1)} collective-permute-done((bf16[64,1792]{1,0:T(8,128)(2,1)S(1)}, bf16[64,1792]{1,0:T(8,128)(2,1)S(1)}, u32[]{:S(2)}, u32[]{:S(2)}) %collective-permute-start.33) | collective-permute-done | bytes 229408 | tf_op jit(solution)/shard_map/ppermute | solution.py:25
  100.5 1.3 shard_map.129.rest_0_
  101.8 1.3 shard_map.130.rest_0_
  103.1 1.7 %collective-permute-done.36.refs_1_ = bf16[256,896]{1,0:T(8,128)(2,1)S(1)} collective-permute-done((bf16[256,896]{1,0:T(8,128)(2,1)S(1)}, bf16[256,896]{1,0:T(8,128)(2,1)S(1)}, u32[]{:S(2)}, u32[]{:S(2)}) %collective-permute-start.36) | collective-permute-done | bytes 458784 | tf_op jit(solution)/shard_map/ppermute | solution.py:25
  104.9 2.0 %collective-permute-done.37.refs_1_ = bf16[256,896]{1,0:T(8,128)(2,1)S(1)} collective-permute-done((bf16[256,896]{1,0:T(8,128)(2,1)S(1)}, bf16[256,896]{1,0:T(8,128)(2,1)S(1)}, u32[]{:S(2)}, u32[]{:S(2)}) %collective-permute-start.37) | collective-permute-done | bytes 458784 | tf_op jit(solution)/shard_map/ppermute | solution.py:25
  106.9 1.3 shard_map.133
  108.4 2.1 %collective-permute-start.40 = (bf16[128,896]{1,0:T(8,128)(2,1)S(1)}, bf16[128,896]{1,0:T(8,128)(2,1)S(1)}, u32[]{:S(2)}, u32[]{:S(2)}) collective-permute-start(bf16[128,896]{1,0:T(8,128)(2,1)S(1)} %get-tuple-element.350.refs_0_), channel_id=1, source_target_pairs={{0,6},{1,7},{2,4},{3,5},{4,2},{5,3},{6,0},{7,1},{8,14},{9,15},{10,... | collective-permute-start | bytes 688136 | tf_op jit(solution)/shard_map/ppermute | solution.py:25
  110.6 1.3 shard_map.134.refs_0_
  112.1 2.2 %collective-permute-start.42 = (bf16[64,1024]{1,0:T(8,128)(2,1)S(1)}, bf16[64,1024]{1,0:T(8,128)(2,1)S(1)}, u32[]{:S(2)}, u32[]{:S(2)}) collective-permute-start(bf16[64,1024]{1,0:T(8,128)(2,1)S(1)} %get-tuple-element.357), channel_id=1, source_target_pairs={{0,96},{8,104},{16,112},{24,120},{32,64},{40,72},{48,80},{56,88},{... | collective-permute-start | bytes 393224 | tf_op jit(solution)/shard_map/ppermute | solution.py:25
  114.2 1.9 %collective-permute-start.43 = (bf16[64,1024]{1,0:T(8,128)(2,1)S(1)}, bf16[64,1024]{1,0:T(8,128)(2,1)S(1)}, u32[]{:S(2)}, u32[]{:S(2)}) collective-permute-start(bf16[64,1024]{1,0:T(8,128)(2,1)S(1)} %get-tuple-element.358), channel_id=1, source_target_pairs={{0,64},{8,72},{16,80},{24,88},{32,96},{40,104},{48,112},{56,120},{... | collective-permute-start | bytes 393224 | tf_op jit(solution)/shard_map/ppermute | solution.py:25
  116.4 1.9 %collective-permute-start.45 = (bf16[256,896]{1,0:T(8,128)(2,1)S(1)}, bf16[256,896]{1,0:T(8,128)(2,1)S(1)}, u32[]{:S(2)}, u32[]{:S(2)}) collective-permute-start(bf16[256,896]{1,0:T(8,128)(2,1)S(1)} %shard_map.136.refs_0_), channel_id=1, source_target_pairs={{0,6},{1,7},{2,4},{3,5},{4,2},{5,3},{6,0},{7,1},{8,14},{9,15},{10,... | collective-permute-start | bytes 1376264 | tf_op jit(solution)/shard_map/ppermute | solution.py:25
  118.4 3.4 %shard_map.138 = (bf16[1024,1792]{1,0:T(8,128)(2,1)}, bf16[1024,1792]{1,0:T(8,128)(2,1)}) custom-call(s32[1]{0:T(128)} %bitcast.mine_ref.mine, bf16[8,64,1024]{2,1,0:T(8,128)(2,1)S(1)} %bitcast.15, bf16[8,64,1024]{2,1,0:T(8,128)(2,1)S(1)} %bitcast.16, bf16[512,896]{1,0:T(8,128)(2,1)S(1)} %shard_map.127.refs_2_, bf16[512,896]{1,0:T(8,128)(2,1)S(1)} %shard_map.128.refs_3_), custom_call_target="tpu_custom_call" | custom-call | flops 1 | bytes 1 | tf_op jit(solution)/shard_map/pallas_call | solution.py:50
  121.9 2.5 %collective-permute-start.44 = (f32[32,1024]{1,0:T(8,128)S(1)}, f32[32,1024]{1,0:T(8,128)S(1)}, u32[]{:S(2)}, u32[]{:S(2)}) collective-permute-start(f32[32,1024]{1,0:T(8,128)S(1)} %get-tuple-element.362), channel_id=1, source_target_pairs={{0,16},{8,24},{16,0},{24,8},{32,48},{40,56},{48,32},{56,40},{64,80... | collective-permute-start | bytes 393224 | tf_op jit(solution)/shard_map/ppermute | solution.py:25
  124.4 3.3 %shard_map.140 = (bf16[1024,1792]{1,0:T(8,128)(2,1)}, bf16[1024,1792]{1,0:T(8,128)(2,1)}) custom-call(s32[1]{0:T(128)} %bitcast.mine_ref.mine, bf16[8,64,1024]{2,1,0:T(8,128)(2,1)S(1)} %bitcast.17, bf16[8,64,1024]{2,1,0:T(8,128)(2,1)S(1)} %bitcast.18, bf16[512,896]{1,0:T(8,128)(2,1)S(1)} %shard_map.131.refs_2_, ...), custom_call_target="tpu_custom_call", output_to_operand_aliasing={{0}: (5, {}), {1}: (6, {})} | custom-call | flops 1 | bytes 1 | tf_op jit(solution)/shard_map/pallas_call | solution.py:50
  130.3 3.0 %shard_map.143 = bf16[1792,1024]{1,0:T(8,128)(2,1)} custom-call(s32[1]{0:T(128)} %bitcast.mine_ref.mine, bf16[8,64,1024]{2,1,0:T(8,128)(2,1)S(1)} %bitcast.23, bf16[8,64,1024]{2,1,0:T(8,128)(2,1)S(1)} %bitcast.24, bf16[512,896]{1,0:T(8,128)(2,1)S(1)} %shard_map.141.refs_2_, bf16[512,896]{1,0:T(8,128)(2,1)S(1)} %shard_map.142.refs_3_), custom_call_target="tpu_custom_call" | custom-call | flops 1 | bytes 1 | tf_op jit(solution)/shard_map/pallas_call | solution.py:50
  (101 shorter events, 16.9 us)
Async XLA Ops:
  0.6 6.5 %collective-permute-start = (bf16[32,1024]{1,0:T(8,128)(2,1)}, bf16[32,1024]{1,0:T(8,128)(2,1)S(1)}, u32[]{:S(2)}, u32[]{:S(2)}) collective-permute-start(bf16[32,1024]{1,0:T(8,128)(2,1)} %refs_0_.1), channel_id=1, source_target_pairs={{0,16},{8,24},{16,0},{24,8},{32,48},{40,56},{48,32},{56,40},{64,80... | collective-permute-start | bytes 196616 | tf_op jit(solution)/shard_map/ppermute | solution.py:25
  4.7 6.0 %collective-permute-start.1 = (bf16[32,1024]{1,0:T(8,128)(2,1)}, bf16[32,1024]{1,0:T(8,128)(2,1)S(1)}, u32[]{:S(2)}, u32[]{:S(2)}) collective-permute-start(bf16[32,1024]{1,0:T(8,128)(2,1)} %refs_2_.1), channel_id=1, source_target_pairs={{0,16},{8,24},{16,0},{24,8},{32,48},{40,56},{48,32},{56,40},{64,80... | collective-permute-start | bytes 196616 | tf_op jit(solution)/shard_map/ppermute | solution.py:25
  4.8 2.0 %copy-start = (bf16[1024,1792]{1,0:T(8,128)(2,1)S(1)}, bf16[1024,1792]{1,0:T(8,128)(2,1)}, u32[]{:S(2)}) copy-start(bf16[1024,1792]{1,0:T(8,128)(2,1)} %w_ref.3) | copy-start | bytes 11010052
  6.8 3.9 %copy-start.3 = (bf16[32,1024]{1,0:T(8,128)(2,1)S(1)}, bf16[32,1024]{1,0:T(8,128)(2,1)}, u32[]{:S(2)}) copy-start(bf16[32,1024]{1,0:T(8,128)(2,1)} %refs_0_.1) | copy-start | bytes 196612
  6.8 3.9 %copy-start.4 = (bf16[32,1024]{1,0:T(8,128)(2,1)S(1)}, bf16[32,1024]{1,0:T(8,128)(2,1)}, u32[]{:S(2)}) copy-start(bf16[32,1024]{1,0:T(8,128)(2,1)} %refs_2_.1) | copy-start | bytes 196612
  6.8 8.2 %copy-start.1 = (bf16[1024,1792]{1,0:T(8,128)(2,1)S(1)}, bf16[1024,1792]{1,0:T(8,128)(2,1)}, u32[]{:S(2)}) copy-start(bf16[1024,1792]{1,0:T(8,128)(2,1)} %w_ref.4) | copy-start | bytes 11010052
  10.7 15.4 %copy-start.2 = (bf16[1792,1024]{1,0:T(8,128)(2,1)S(1)}, bf16[1792,1024]{1,0:T(8,128)(2,1)}, u32[]{:S(2)}) copy-start(bf16[1792,1024]{1,0:T(8,128)(2,1)} %w_ref.5) | copy-start | bytes 11010052
  10.7 9.3 %collective-permute-start.2 = (bf16[128,1024]{1,0:T(8,128)(2,1)S(1)}, bf16[128,1024]{1,0:T(8,128)(2,1)S(1)}, u32[]{:S(2)}, u32[]{:S(2)}) collective-permute-start(bf16[128,1024]{1,0:T(8,128)(2,1)S(1)} %shard_map.85.refs_0_), channel_id=1, source_target_pairs={{0,32},{8,40},{16,48},{24,56},{32,0},{40,8},{48,16},{56,24},{64,96... | collective-permute-start | bytes 786440 | tf_op jit(solution)/shard_map/ppermute | solution.py:25
  12.3 13.2 %collective-permute-start.3 = (bf16[128,1024]{1,0:T(8,128)(2,1)S(1)}, bf16[128,1024]{1,0:T(8,128)(2,1)S(1)}, u32[]{:S(2)}, u32[]{:S(2)}) collective-permute-start(bf16[128,1024]{1,0:T(8,128)(2,1)S(1)} %shard_map.85.refs_0_), channel_id=1, source_target_pairs={{0,96},{8,104},{16,112},{24,120},{32,64},{40,72},{48,80},{56,88},{... | collective-permute-start | bytes 786440 | tf_op jit(solution)/shard_map/ppermute | solution.py:25
  14.4 11.1 %collective-permute-start.4 = (bf16[128,1024]{1,0:T(8,128)(2,1)S(1)}, bf16[128,1024]{1,0:T(8,128)(2,1)S(1)}, u32[]{:S(2)}, u32[]{:S(2)}) collective-permute-start(bf16[128,1024]{1,0:T(8,128)(2,1)S(1)} %shard_map.85.refs_0_), channel_id=1, source_target_pairs={{0,64},{8,72},{16,80},{24,88},{32,96},{40,104},{48,112},{56,120},{... | collective-permute-start | bytes 786440 | tf_op jit(solution)/shard_map/ppermute | solution.py:25
  25.5 2.0 %collective-permute-start.5 = (bf16[256,1024]{1,0:T(8,128)(2,1)S(1)}, bf16[256,1024]{1,0:T(8,128)(2,1)S(1)}, u32[]{:S(2)}, u32[]{:S(2)}) collective-permute-start(bf16[256,1024]{1,0:T(8,128)(2,1)S(1)} %get-tuple-element.199.refs_0_), channel_id=1, source_target_pairs={{0,8},{8,0},{16,24},{24,16},{32,40},{40,32},{48,56},{56,48},{64,72... | collective-permute-start | bytes 1572872 | tf_op jit(solution)/shard_map/ppermute | solution.py:25
  25.6 7.3 %collective-permute-start.6 = (bf16[256,1024]{1,0:T(8,128)(2,1)S(1)}, bf16[256,1024]{1,0:T(8,128)(2,1)S(1)}, u32[]{:S(2)}, u32[]{:S(2)}) collective-permute-start(bf16[256,1024]{1,0:T(8,128)(2,1)S(1)} %get-tuple-element.206.refs_0_), channel_id=1, source_target_pairs={{0,8},{8,0},{16,24},{24,16},{32,40},{40,32},{48,56},{56,48},{64,72... | collective-permute-start | bytes 1572872 | tf_op jit(solution)/shard_map/ppermute | solution.py:25
  28.3 13.4 %collective-permute-start.7 = (bf16[256,896]{1,0:T(8,128)(2,1)S(1)}, bf16[256,896]{1,0:T(8,128)(2,1)S(1)}, u32[]{:S(2)}, u32[]{:S(2)}) collective-permute-start(bf16[256,896]{1,0:T(8,128)(2,1)S(1)} %shard_map.90), channel_id=1, source_target_pairs={{0,2},{1,3},{2,0},{3,1},{4,6},{5,7},{6,4},{7,5},{8,10},{9,11},{10,... | collective-permute-start | bytes 1376264 | tf_op jit(solution)/shard_map/ppermute | solution.py:25
  30.7 14.7 %collective-permute-start.8 = (bf16[256,896]{1,0:T(8,128)(2,1)S(1)}, bf16[256,896]{1,0:T(8,128)(2,1)S(1)}, u32[]{:S(2)}, u32[]{:S(2)}) collective-permute-start(bf16[256,896]{1,0:T(8,128)(2,1)S(1)} %shard_map.91), channel_id=1, source_target_pairs={{0,6},{1,7},{2,4},{3,5},{4,2},{5,3},{6,0},{7,1},{8,14},{9,15},{10,... | collective-permute-start | bytes 1376264 | tf_op jit(solution)/shard_map/ppermute | solution.py:25
  33.8 13.9 %collective-permute-start.9 = (bf16[256,896]{1,0:T(8,128)(2,1)S(1)}, bf16[256,896]{1,0:T(8,128)(2,1)S(1)}, u32[]{:S(2)}, u32[]{:S(2)}) collective-permute-start(bf16[256,896]{1,0:T(8,128)(2,1)S(1)} %shard_map.93), channel_id=1, source_target_pairs={{0,1},{1,0},{2,3},{3,2},{4,5},{5,4},{6,7},{7,6},{8,9},{9,8},{10,11... | collective-permute-start | bytes 1376264 | tf_op jit(solution)/shard_map/ppermute | solution.py:25
  35.6 15.2 %collective-permute-start.10 = (bf16[256,896]{1,0:T(8,128)(2,1)S(1)}, bf16[256,896]{1,0:T(8,128)(2,1)S(1)}, u32[]{:S(2)}, u32[]{:S(2)}) collective-permute-start(bf16[256,896]{1,0:T(8,128)(2,1)S(1)} %shard_map.94), channel_id=1, source_target_pairs={{0,2},{1,3},{2,0},{3,1},{4,6},{5,7},{6,4},{7,5},{8,10},{9,11},{10,... | collective-permute-start | bytes 1376264 | tf_op jit(solution)/shard_map/ppermute | solution.py:25
  38.5 16.7 %collective-permute-start.11 = (bf16[256,896]{1,0:T(8,128)(2,1)S(1)}, bf16[256,896]{1,0:T(8,128)(2,1)S(1)}, u32[]{:S(2)}, u32[]{:S(2)}) collective-permute-start(bf16[256,896]{1,0:T(8,128)(2,1)S(1)} %shard_map.95), channel_id=1, source_target_pairs={{0,6},{1,7},{2,4},{3,5},{4,2},{5,3},{6,0},{7,1},{8,14},{9,15},{10,... | collective-permute-start | bytes 1376264 | tf_op jit(solution)/shard_map/ppermute | solution.py:25
  41.7 16.5 %collective-permute-start.12 = (bf16[256,896]{1,0:T(8,128)(2,1)S(1)}, bf16[256,896]{1,0:T(8,128)(2,1)S(1)}, u32[]{:S(2)}, u32[]{:S(2)}) collective-permute-start(bf16[256,896]{1,0:T(8,128)(2,1)S(1)} %shard_map.100), channel_id=1, source_target_pairs={{0,1},{1,0},{2,3},{3,2},{4,5},{5,4},{6,7},{7,6},{8,9},{9,8},{10,11... | collective-permute-start | bytes 1376264 | tf_op jit(solution)/shard_map/ppermute | solution.py:25
  45.4 14.7 %collective-permute-start.13 = (bf16[128,896]{1,0:T(8,128)(2,1)S(1)}, bf16[128,896]{1,0:T(8,128)(2,1)S(1)}, u32[]{:S(2)}, u32[]{:S(2)}) collective-permute-start(bf16[128,896]{1,0:T(8,128)(2,1)S(1)} %get-tuple-element.251), channel_id=1, source_target_pairs={{0,6},{1,7},{2,4},{3,5},{4,2},{5,3},{6,0},{7,1},{8,14},{9,15},{10,... | collective-permute-start | bytes 688136 | tf_op jit(solution)/shard_map/ppermute | solution.py:25
  47.6 14.4 %collective-permute-start.14 = (bf16[128,896]{1,0:T(8,128)(2,1)S(1)}, bf16[128,896]{1,0:T(8,128)(2,1)S(1)}, u32[]{:S(2)}, u32[]{:S(2)}) collective-permute-start(bf16[128,896]{1,0:T(8,128)(2,1)S(1)} %get-tuple-element.256), channel_id=1, source_target_pairs={{0,1},{1,0},{2,3},{3,2},{4,5},{5,4},{6,7},{7,6},{8,9},{9,8},{10,11... | collective-permute-start | bytes 688136 | tf_op jit(solution)/shard_map/ppermute | solution.py:25
  50.8 11.3 %collective-permute-start.15 = (bf16[128,896]{1,0:T(8,128)(2,1)S(1)}, bf16[128,896]{1,0:T(8,128)(2,1)S(1)}, u32[]{:S(2)}, u32[]{:S(2)}) collective-permute-start(bf16[128,896]{1,0:T(8,128)(2,1)S(1)} %get-tuple-element.261), channel_id=1, source_target_pairs={{0,2},{1,3},{2,0},{3,1},{4,6},{5,7},{6,4},{7,5},{8,10},{9,11},{10,... | collective-permute-start | bytes 688136 | tf_op jit(solution)/shard_map/ppermute | solution.py:25
  55.2 9.3 %collective-permute-start.16 = (bf16[128,896]{1,0:T(8,128)(2,1)S(1)}, bf16[128,896]{1,0:T(8,128)(2,1)S(1)}, u32[]{:S(2)}, u32[]{:S(2)}) collective-permute-start(bf16[128,896]{1,0:T(8,128)(2,1)S(1)} %get-tuple-element.266), channel_id=1, source_target_pairs={{0,6},{1,7},{2,4},{3,5},{4,2},{5,3},{6,0},{7,1},{8,14},{9,15},{10,... | collective-permute-start | bytes 688136 | tf_op jit(solution)/shard_map/ppermute | solution.py:25
  58.2 7.5 %collective-permute-start.17 = (bf16[128,896]{1,0:T(8,128)(2,1)S(1)}, bf16[128,896]{1,0:T(8,128)(2,1)S(1)}, u32[]{:S(2)}, u32[]{:S(2)}) collective-permute-start(bf16[128,896]{1,0:T(8,128)(2,1)S(1)} %get-tuple-element.271), channel_id=1, source_target_pairs={{0,1},{1,0},{2,3},{3,2},{4,5},{5,4},{6,7},{7,6},{8,9},{9,8},{10,11... | collective-permute-start | bytes 688136 | tf_op jit(solution)/shard_map/ppermute | solution.py:25
  60.1 6.5 %collective-permute-start.18 = (bf16[128,896]{1,0:T(8,128)(2,1)S(1)}, bf16[128,896]{1,0:T(8,128)(2,1)S(1)}, u32[]{:S(2)}, u32[]{:S(2)}) collective-permute-start(bf16[128,896]{1,0:T(8,128)(2,1)S(1)} %get-tuple-element.276), channel_id=1, source_target_pairs={{0,2},{1,3},{2,0},{3,1},{4,6},{5,7},{6,4},{7,5},{8,10},{9,11},{10,... | collective-permute-start | bytes 688136 | tf_op jit(solution)/shard_map/ppermute | solution.py:25
  62.1 7.8 %collective-permute-start.21 = (bf16[64,896]{1,0:T(8,128)(2,1)S(1)}, bf16[64,896]{1,0:T(8,128)(2,1)S(1)}, u32[]{:S(2)}, u32[]{:S(2)}) collective-permute-start(bf16[64,896]{1,0:T(8,128)(2,1)S(1)} %get-tuple-element.285), channel_id=1, source_target_pairs={{0,6},{1,7},{2,4},{3,5},{4,2},{5,3},{6,0},{7,1},{8,14},{9,15},{10,... | collective-permute-start | bytes 344072 | tf_op jit(solution)/shard_map/ppermute | solution.py:25
  64.5 6.4 %collective-permute-start.20 = (bf16[64,896]{1,0:T(8,128)(2,1)S(1)}, bf16[64,896]{1,0:T(8,128)(2,1)S(1)}, u32[]{:S(2)}, u32[]{:S(2)}) collective-permute-start(bf16[64,896]{1,0:T(8,128)(2,1)S(1)} %get-tuple-element.283), channel_id=1, source_target_pairs={{0,2},{1,3},{2,0},{3,1},{4,6},{5,7},{6,4},{7,5},{8,10},{9,11},{10,... | collective-permute-start | bytes 344072 | tf_op jit(solution)/shard_map/ppermute | solution.py:25
  64.7 6.2 %collective-permute-start.19 = (bf16[64,896]{1,0:T(8,128)(2,1)S(1)}, bf16[64,896]{1,0:T(8,128)(2,1)S(1)}, u32[]{:S(2)}, u32[]{:S(2)}) collective-permute-start(bf16[64,896]{1,0:T(8,128)(2,1)S(1)} %get-tuple-element.281), channel_id=1, source_target_pairs={{0,1},{1,0},{2,3},{3,2},{4,5},{5,4},{6,7},{7,6},{8,9},{9,8},{10,11... | collective-permute-start | bytes 344072 | tf_op jit(solution)/shard_map/ppermute | solution.py:25
  66.6 7.4 %collective-permute-start.24 = (bf16[64,896]{1,0:T(8,128)(2,1)S(1)}, bf16[64,896]{1,0:T(8,128)(2,1)S(1)}, u32[]{:S(2)}, u32[]{:S(2)}) collective-permute-start(bf16[64,896]{1,0:T(8,128)(2,1)S(1)} %get-tuple-element.295), channel_id=1, source_target_pairs={{0,6},{1,7},{2,4},{3,5},{4,2},{5,3},{6,0},{7,1},{8,14},{9,15},{10,... | collective-permute-start | bytes 344072 | tf_op jit(solution)/shard_map/ppermute | solution.py:25
  68.9 5.2 %collective-permute-start.23 = (bf16[64,896]{1,0:T(8,128)(2,1)S(1)}, bf16[64,896]{1,0:T(8,128)(2,1)S(1)}, u32[]{:S(2)}, u32[]{:S(2)}) collective-permute-start(bf16[64,896]{1,0:T(8,128)(2,1)S(1)} %get-tuple-element.293), channel_id=1, source_target_pairs={{0,2},{1,3},{2,0},{3,1},{4,6},{5,7},{6,4},{7,5},{8,10},{9,11},{10,... | collective-permute-start | bytes 344072 | tf_op jit(solution)/shard_map/ppermute | solution.py:25
  69.9 4.8 %collective-permute-start.22 = (bf16[64,896]{1,0:T(8,128)(2,1)S(1)}, bf16[64,896]{1,0:T(8,128)(2,1)S(1)}, u32[]{:S(2)}, u32[]{:S(2)}) collective-permute-start(bf16[64,896]{1,0:T(8,128)(2,1)S(1)} %get-tuple-element.291), channel_id=1, source_target_pairs={{0,1},{1,0},{2,3},{3,2},{4,5},{5,4},{6,7},{7,6},{8,9},{9,8},{10,11... | collective-permute-start | bytes 344072 | tf_op jit(solution)/shard_map/ppermute | solution.py:25
  71.1 6.1 %collective-permute-start.25 = (bf16[64,896]{1,0:T(8,128)(2,1)S(1)}, bf16[64,896]{1,0:T(8,128)(2,1)S(1)}, u32[]{:S(2)}, u32[]{:S(2)}) collective-permute-start(bf16[64,896]{1,0:T(8,128)(2,1)S(1)} %get-tuple-element.300.refs_0_), channel_id=1, source_target_pairs={{0,6},{1,7},{2,4},{3,5},{4,2},{5,3},{6,0},{7,1},{8,14},{9,15},{10,... | collective-permute-start | bytes 344072 | tf_op jit(solution)/shard_map/ppermute | solution.py:25
  73.1 5.9 %collective-permute-start.26 = (bf16[64,896]{1,0:T(8,128)(2,1)S(1)}, bf16[64,896]{1,0:T(8,128)(2,1)S(1)}, u32[]{:S(2)}, u32[]{:S(2)}) collective-permute-start(bf16[64,896]{1,0:T(8,128)(2,1)S(1)} %get-tuple-element.302.refs_0_), channel_id=1, source_target_pairs={{0,1},{1,0},{2,3},{3,2},{4,5},{5,4},{6,7},{7,6},{8,9},{9,8},{10,11... | collective-permute-start | bytes 344072 | tf_op jit(solution)/shard_map/ppermute | solution.py:25
  74.9 6.1 %collective-permute-start.27 = (bf16[64,896]{1,0:T(8,128)(2,1)S(1)}, bf16[64,896]{1,0:T(8,128)(2,1)S(1)}, u32[]{:S(2)}, u32[]{:S(2)}) collective-permute-start(bf16[64,896]{1,0:T(8,128)(2,1)S(1)} %get-tuple-element.307.refs_0_), channel_id=1, source_target_pairs={{0,6},{1,7},{2,4},{3,5},{4,2},{5,3},{6,0},{7,1},{8,14},{9,15},{10,... | collective-permute-start | bytes 344072 | tf_op jit(solution)/shard_map/ppermute | solution.py:25
  76.2 5.9 %collective-permute-start.28 = (bf16[64,896]{1,0:T(8,128)(2,1)S(1)}, bf16[64,896]{1,0:T(8,128)(2,1)S(1)}, u32[]{:S(2)}, u32[]{:S(2)}) collective-permute-start(bf16[64,896]{1,0:T(8,128)(2,1)S(1)} %get-tuple-element.309.refs_0_), channel_id=1, source_target_pairs={{0,2},{1,3},{2,0},{3,1},{4,6},{5,7},{6,4},{7,5},{8,10},{9,11},{10,... | collective-permute-start | bytes 344072 | tf_op jit(solution)/shard_map/ppermute | solution.py:25
  77.2 8.6 %collective-permute-start.29 = (bf16[128,896]{1,0:T(8,128)(2,1)S(1)}, bf16[128,896]{1,0:T(8,128)(2,1)S(1)}, u32[]{:S(2)}, u32[]{:S(2)}) collective-permute-start(bf16[128,896]{1,0:T(8,128)(2,1)S(1)} %shard_map.117.refs_0_), channel_id=1, source_target_pairs={{0,1},{1,0},{2,3},{3,2},{4,5},{5,4},{6,7},{7,6},{8,9},{9,8},{10,11... | collective-permute-start | bytes 688136 | tf_op jit(solution)/shard_map/ppermute | solution.py:25
  79.0 8.2 %collective-permute-start.30 = (bf16[128,896]{1,0:T(8,128)(2,1)S(1)}, bf16[128,896]{1,0:T(8,128)(2,1)S(1)}, u32[]{:S(2)}, u32[]{:S(2)}) collective-permute-start(bf16[128,896]{1,0:T(8,128)(2,1)S(1)} %shard_map.118.refs_0_), channel_id=1, source_target_pairs={{0,2},{1,3},{2,0},{3,1},{4,6},{5,7},{6,4},{7,5},{8,10},{9,11},{10,... | collective-permute-start | bytes 688136 | tf_op jit(solution)/shard_map/ppermute | solution.py:25
  81.0 9.1 %collective-permute-start.31 = (bf16[128,896]{1,0:T(8,128)(2,1)S(1)}, bf16[128,896]{1,0:T(8,128)(2,1)S(1)}, u32[]{:S(2)}, u32[]{:S(2)}) collective-permute-start(bf16[128,896]{1,0:T(8,128)(2,1)S(1)} %shard_map.120.refs_0_), channel_id=1, source_target_pairs={{0,1},{1,0},{2,3},{3,2},{4,5},{5,4},{6,7},{7,6},{8,9},{9,8},{10,11... | collective-permute-start | bytes 688136 | tf_op jit(solution)/shard_map/ppermute | solution.py:25
  82.1 10.5 %collective-permute-start.32 = (bf16[128,896]{1,0:T(8,128)(2,1)S(1)}, bf16[128,896]{1,0:T(8,128)(2,1)S(1)}, u32[]{:S(2)}, u32[]{:S(2)}) collective-permute-start(bf16[128,896]{1,0:T(8,128)(2,1)S(1)} %shard_map.121.refs_0_), channel_id=1, source_target_pairs={{0,1},{1,0},{2,3},{3,2},{4,5},{5,4},{6,7},{7,6},{8,9},{9,8},{10,11... | collective-permute-start | bytes 688136 | tf_op jit(solution)/shard_map/ppermute | solution.py:25
  85.9 14.3 %collective-permute-start.34 = (bf16[256,896]{1,0:T(8,128)(2,1)S(1)}, bf16[256,896]{1,0:T(8,128)(2,1)S(1)}, u32[]{:S(2)}, u32[]{:S(2)}) collective-permute-start(bf16[256,896]{1,0:T(8,128)(2,1)S(1)} %shard_map.122.refs_0_), channel_id=1, source_target_pairs={{0,2},{1,3},{2,0},{3,1},{4,6},{5,7},{6,4},{7,5},{8,10},{9,11},{10,... | collective-permute-start | bytes 1376264 | tf_op jit(solution)/shard_map/ppermute | solution.py:25
  87.2 13.2 %collective-permute-start.35 = (bf16[256,896]{1,0:T(8,128)(2,1)S(1)}, bf16[256,896]{1,0:T(8,128)(2,1)S(1)}, u32[]{:S(2)}, u32[]{:S(2)}) collective-permute-start(bf16[256,896]{1,0:T(8,128)(2,1)S(1)} %shard_map.123.refs_0_), channel_id=1, source_target_pairs={{0,6},{1,7},{2,4},{3,5},{4,2},{5,3},{6,0},{7,1},{8,14},{9,15},{10,... | collective-permute-start | bytes 1376264 | tf_op jit(solution)/shard_map/ppermute | solution.py:25
  90.2 14.6 %collective-permute-start.36 = (bf16[256,896]{1,0:T(8,128)(2,1)S(1)}, bf16[256,896]{1,0:T(8,128)(2,1)S(1)}, u32[]{:S(2)}, u32[]{:S(2)}) collective-permute-start(bf16[256,896]{1,0:T(8,128)(2,1)S(1)} %shard_map.124.refs_0_), channel_id=1, source_target_pairs={{0,2},{1,3},{2,0},{3,1},{4,6},{5,7},{6,4},{7,5},{8,10},{9,11},{10,... | collective-permute-start | bytes 1376264 | tf_op jit(solution)/shard_map/ppermute | solution.py:25
  92.6 14.2 %collective-permute-start.37 = (bf16[256,896]{1,0:T(8,128)(2,1)S(1)}, bf16[256,896]{1,0:T(8,128)(2,1)S(1)}, u32[]{:S(2)}, u32[]{:S(2)}) collective-permute-start(bf16[256,896]{1,0:T(8,128)(2,1)S(1)} %shard_map.125.refs_0_), channel_id=1, source_target_pairs={{0,6},{1,7},{2,4},{3,5},{4,2},{5,3},{6,0},{7,1},{8,14},{9,15},{10,... | collective-permute-start | bytes 1376264 | tf_op jit(solution)/shard_map/ppermute | solution.py:25
  94.1 6.0 %collective-permute-start.33 = (bf16[64,1792]{1,0:T(8,128)(2,1)S(1)}, bf16[64,1792]{1,0:T(8,128)(2,1)S(1)}, u32[]{:S(2)}, u32[]{:S(2)}) collective-permute-start(bf16[64,1792]{1,0:T(8,128)(2,1)S(1)} %shard_map.119.refs_0_), channel_id=1, source_target_pairs={{0,1},{1,0},{2,3},{3,2},{4,5},{5,4},{6,7},{7,6},{8,9},{9,8},{10,11... | collective-permute-start | bytes 688136 | tf_op jit(solution)/shard_map/ppermute | solution.py:25
  108.2 3.7 %collective-permute-start.38 = (f32[256,1024]{1,0:T(8,128)S(1)}, f32[256,1024]{1,0:T(8,128)S(1)}, u32[]{:S(2)}, u32[]{:S(2)}) collective-permute-start(f32[256,1024]{1,0:T(8,128)S(1)} %shard_map.133), channel_id=1, source_target_pairs={{0,8},{8,0},{16,24},{24,16},{32,40},{40,32},{48,56},{56,48},{64,72... | collective-permute-start | bytes 3145736 | tf_op jit(solution)/shard_map/ppermute | solution.py:25
  108.3 8.0 %collective-permute-start.39 = (bf16[128,896]{1,0:T(8,128)(2,1)S(1)}, bf16[128,896]{1,0:T(8,128)(2,1)S(1)}, u32[]{:S(2)}, u32[]{:S(2)}) collective-permute-start(bf16[128,896]{1,0:T(8,128)(2,1)S(1)} %get-tuple-element.348.refs_0_), channel_id=1, source_target_pairs={{0,2},{1,3},{2,0},{3,1},{4,6},{5,7},{6,4},{7,5},{8,10},{9,11},{10,... | collective-permute-start | bytes 688136 | tf_op jit(solution)/shard_map/ppermute | solution.py:25
  108.4 9.9 %collective-permute-start.40 = (bf16[128,896]{1,0:T(8,128)(2,1)S(1)}, bf16[128,896]{1,0:T(8,128)(2,1)S(1)}, u32[]{:S(2)}, u32[]{:S(2)}) collective-permute-start(bf16[128,896]{1,0:T(8,128)(2,1)S(1)} %get-tuple-element.350.refs_0_), channel_id=1, source_target_pairs={{0,6},{1,7},{2,4},{3,5},{4,2},{5,3},{6,0},{7,1},{8,14},{9,15},{10,... | collective-permute-start | bytes 688136 | tf_op jit(solution)/shard_map/ppermute | solution.py:25
  112.0 9.8 %collective-permute-start.41 = (bf16[64,1024]{1,0:T(8,128)(2,1)S(1)}, bf16[64,1024]{1,0:T(8,128)(2,1)S(1)}, u32[]{:S(2)}, u32[]{:S(2)}) collective-permute-start(bf16[64,1024]{1,0:T(8,128)(2,1)S(1)} %get-tuple-element.356), channel_id=1, source_target_pairs={{0,32},{8,40},{16,48},{24,56},{32,0},{40,8},{48,16},{56,24},{64,96... | collective-permute-start | bytes 393224 | tf_op jit(solution)/shard_map/ppermute | solution.py:25
  112.1 9.7 %collective-permute-start.42 = (bf16[64,1024]{1,0:T(8,128)(2,1)S(1)}, bf16[64,1024]{1,0:T(8,128)(2,1)S(1)}, u32[]{:S(2)}, u32[]{:S(2)}) collective-permute-start(bf16[64,1024]{1,0:T(8,128)(2,1)S(1)} %get-tuple-element.357), channel_id=1, source_target_pairs={{0,96},{8,104},{16,112},{24,120},{32,64},{40,72},{48,80},{56,88},{... | collective-permute-start | bytes 393224 | tf_op jit(solution)/shard_map/ppermute | solution.py:25
  114.2 7.6 %collective-permute-start.43 = (bf16[64,1024]{1,0:T(8,128)(2,1)S(1)}, bf16[64,1024]{1,0:T(8,128)(2,1)S(1)}, u32[]{:S(2)}, u32[]{:S(2)}) collective-permute-start(bf16[64,1024]{1,0:T(8,128)(2,1)S(1)} %get-tuple-element.358), channel_id=1, source_target_pairs={{0,64},{8,72},{16,80},{24,88},{32,96},{40,104},{48,112},{56,120},{... | collective-permute-start | bytes 393224 | tf_op jit(solution)/shard_map/ppermute | solution.py:25
  116.4 13.4 %collective-permute-start.45 = (bf16[256,896]{1,0:T(8,128)(2,1)S(1)}, bf16[256,896]{1,0:T(8,128)(2,1)S(1)}, u32[]{:S(2)}, u32[]{:S(2)}) collective-permute-start(bf16[256,896]{1,0:T(8,128)(2,1)S(1)} %shard_map.136.refs_0_), channel_id=1, source_target_pairs={{0,6},{1,7},{2,4},{3,5},{4,2},{5,3},{6,0},{7,1},{8,14},{9,15},{10,... | collective-permute-start | bytes 1376264 | tf_op jit(solution)/shard_map/ppermute | solution.py:25
  118.3 11.9 %collective-permute-start.46 = (bf16[256,896]{1,0:T(8,128)(2,1)S(1)}, bf16[256,896]{1,0:T(8,128)(2,1)S(1)}, u32[]{:S(2)}, u32[]{:S(2)}) collective-permute-start(bf16[256,896]{1,0:T(8,128)(2,1)S(1)} %shard_map.137.refs_0_), channel_id=1, source_target_pairs={{0,2},{1,3},{2,0},{3,1},{4,6},{5,7},{6,4},{7,5},{8,10},{9,11},{10,... | collective-permute-start | bytes 1376264 | tf_op jit(solution)/shard_map/ppermute | solution.py:25
  121.9 6.6 %collective-permute-start.44 = (f32[32,1024]{1,0:T(8,128)S(1)}, f32[32,1024]{1,0:T(8,128)S(1)}, u32[]{:S(2)}, u32[]{:S(2)}) collective-permute-start(f32[32,1024]{1,0:T(8,128)S(1)} %get-tuple-element.362), channel_id=1, source_target_pairs={{0,16},{8,24},{16,0},{24,8},{32,48},{40,56},{48,32},{56,40},{64,80... | collective-permute-start | bytes 393224 | tf_op jit(solution)/shard_map/ppermute | solution.py:25

commit v4 on v3

--- a/solution.py
+++ b/solution.py
@@ -408,11 +408,11 @@
     send_step(5)
     halve_step(1, 0)
     halve_step(1, 1)
+    keep_step(4)
     halve_step(1, 2)
+    keep_step(5)
     halve_step(1, 3)
-    keep_step(4)
     halve_step(1, 4)
-    keep_step(5)
     halve_step(1, 5)
     halve_step(2, 0)
     halve_step(2, 1)
@@ -424,20 +424,20 @@
     swiglu_step(1)
     grow(0, 1)
     grow(1, 1)
+    grow(3, 1)
+    grow(4, 1)
     both = beside(order, grads[2], grads[5])
     far = swap(both, "col", COL[GATHER_DIMS[2][0]])
-    grow(3, 1)
-    grow(4, 1)
     grow(0, 2)
     grow(1, 2)
     grow(3, 2)
     grow(4, 2)
+    grow(0, 3)
+    grow(1, 3)
+    send, keep = input_step(0, 4, None), input_step(0, 0, None)
     grads[2], grads[5] = split(order, both, far, CHUNKS)
     for i in (2, 5):
         fars[i] = swap(grads[i], "col", COL[GATHER_DIMS[i][1]])
-    grow(0, 3)
-    grow(1, 3)
-    send, keep = input_step(0, 4, None), input_step(0, 0, None)
     grow(3, 3)
     grow(4, 3)
     send = input_step(1, 4, send)

time: 134 us -> 133 us (level)
  transfers between devices with their start and end apart: 47 -> 47, of which waited for: 29 -> 30; matrix products, arithmetic and copies ran while one was open for 0% -> 0% of each run, Pallas kernels for 16% -> 17%
where the time goes in v4:
time: 133 us
  starting transfers between devices  56.5 us (42%)
  waiting for transfers between devices  45.7 us (34%)
  Pallas kernels  26.5 us (20%)
  local copies, waits for them, and re-layouts  2.06 us (2%)
    ppermute x47, starting transfers between devices, swap(): return lax.ppermute(value, axis, [(i, i ^ mask) for i in range(size)])  56.5 us
    ppermute x47, waiting for transfers between devices, swap(): return lax.ppermute(value, axis, [(i, i ^ mask) for i in range(size)])  45.7 us
    pallas_call x60, Pallas kernels, run(): out = call(self.mine, *args)  26.5 us
  transfers between devices with their start and end apart: 47, of which 30 were waited for; matrix products, arithmetic and copies ran while one was open for 0% of the time, Pallas kernels for 17%

profile of v4, /device:TPU:0, one launch (start us, length us, event | category | flops | bytes accessed | tf_op | source)
XLA Modules:
  0.0 132.8 jit_solution(17783360043333112945)
XLA Ops:
  0.6 4.0 %collective-permute-start = (bf16[32,1024]{1,0:T(8,128)(2,1)}, bf16[32,1024]{1,0:T(8,128)(2,1)S(1)}, u32[]{:S(2)}, u32[]{:S(2)}) collective-permute-start(bf16[32,1024]{1,0:T(8,128)(2,1)} %refs_0_.1), channel_id=1, source_target_pairs={{0,16},{8,24},{16,0},{24,8},{32,48},{40,56},{48,32},{56,40},{64,80... | collective-permute-start | bytes 196616 | tf_op jit(solution)/shard_map/ppermute | solution.py:25
  4.8 2.0 %copy-done = bf16[1024,1792]{1,0:T(8,128)(2,1)S(1)} copy-done((bf16[1024,1792]{1,0:T(8,128)(2,1)S(1)}, bf16[1024,1792]{1,0:T(8,128)(2,1)}, u32[]{:S(2)}) %copy-start) | copy-done | bytes 3670040
  7.1 3.5 %collective-permute-done.1.refs_3_ = bf16[32,1024]{1,0:T(8,128)(2,1)S(1)} collective-permute-done((bf16[32,1024]{1,0:T(8,128)(2,1)}, bf16[32,1024]{1,0:T(8,128)(2,1)S(1)}, u32[]{:S(2)}, u32[]{:S(2)}) %collective-permute-start.1) | collective-permute-done | bytes 65568 | tf_op jit(solution)/shard_map/ppermute | solution.py:25
  10.7 1.6 %collective-permute-start.2 = (bf16[128,1024]{1,0:T(8,128)(2,1)S(1)}, bf16[128,1024]{1,0:T(8,128)(2,1)S(1)}, u32[]{:S(2)}, u32[]{:S(2)}) collective-permute-start(bf16[128,1024]{1,0:T(8,128)(2,1)S(1)} %shard_map.85.refs_0_), channel_id=1, source_target_pairs={{0,32},{8,40},{16,48},{24,56},{32,0},{40,8},{48,16},{56,24},{64,96... | collective-permute-start | bytes 786440 | tf_op jit(solution)/shard_map/ppermute | solution.py:25
  12.3 2.1 %collective-permute-start.3 = (bf16[128,1024]{1,0:T(8,128)(2,1)S(1)}, bf16[128,1024]{1,0:T(8,128)(2,1)S(1)}, u32[]{:S(2)}, u32[]{:S(2)}) collective-permute-start(bf16[128,1024]{1,0:T(8,128)(2,1)S(1)} %shard_map.85.refs_0_), channel_id=1, source_target_pairs={{0,96},{8,104},{16,112},{24,120},{32,64},{40,72},{48,80},{56,88},{... | collective-permute-start | bytes 786440 | tf_op jit(solution)/shard_map/ppermute | solution.py:25
  15.3 4.7 %collective-permute-done.2.refs_1_ = bf16[128,1024]{1,0:T(8,128)(2,1)S(1)} collective-permute-done((bf16[128,1024]{1,0:T(8,128)(2,1)S(1)}, bf16[128,1024]{1,0:T(8,128)(2,1)S(1)}, u32[]{:S(2)}, u32[]{:S(2)}) %collective-permute-start.2) | collective-permute-done | bytes 262176 | tf_op jit(solution)/shard_map/ppermute | solution.py:25
  20.0 5.4 %collective-permute-done.3.refs_2_ = bf16[128,1024]{1,0:T(8,128)(2,1)S(1)} collective-permute-done((bf16[128,1024]{1,0:T(8,128)(2,1)S(1)}, bf16[128,1024]{1,0:T(8,128)(2,1)S(1)}, u32[]{:S(2)}, u32[]{:S(2)}) %collective-permute-start.3) | collective-permute-done | bytes 262176 | tf_op jit(solution)/shard_map/ppermute | solution.py:25
  26.4 1.1 collective-permute-done.5.refs_1_
  28.3 1.7 %collective-permute-start.7 = (bf16[256,896]{1,0:T(8,128)(2,1)S(1)}, bf16[256,896]{1,0:T(8,128)(2,1)S(1)}, u32[]{:S(2)}, u32[]{:S(2)}) collective-permute-start(bf16[256,896]{1,0:T(8,128)(2,1)S(1)} %shard_map.90), channel_id=1, source_target_pairs={{0,2},{1,3},{2,0},{3,1},{4,6},{5,7},{6,4},{7,5},{8,10},{9,11},{10,... | collective-permute-start | bytes 1376264 | tf_op jit(solution)/shard_map/ppermute | solution.py:25
  30.7 2.3 %collective-permute-start.8 = (bf16[256,896]{1,0:T(8,128)(2,1)S(1)}, bf16[256,896]{1,0:T(8,128)(2,1)S(1)}, u32[]{:S(2)}, u32[]{:S(2)}) collective-permute-start(bf16[256,896]{1,0:T(8,128)(2,1)S(1)} %shard_map.91), channel_id=1, source_target_pairs={{0,6},{1,7},{2,4},{3,5},{4,2},{5,3},{6,0},{7,1},{8,14},{9,15},{10,... | collective-permute-start | bytes 1376264 | tf_op jit(solution)/shard_map/ppermute | solution.py:25
  33.0 0.7 shard_map.93
  33.8 1.1 collective-permute-start.9
  35.6 0.8 collective-permute-start.10
  38.5 0.7 shard_map.98.refs_0_
  40.7 0.7 shard_map.100
  41.7 1.0 collective-permute-start.12
  42.8 2.5 %collective-permute-done.8.refs_1_ = bf16[256,896]{1,0:T(8,128)(2,1)S(1)} collective-permute-done((bf16[256,896]{1,0:T(8,128)(2,1)S(1)}, bf16[256,896]{1,0:T(8,128)(2,1)S(1)}, u32[]{:S(2)}, u32[]{:S(2)}) %collective-permute-start.8) | collective-permute-done | bytes 458784 | tf_op jit(solution)/shard_map/ppermute | solution.py:25
  45.4 2.2 %collective-permute-start.13 = (bf16[128,896]{1,0:T(8,128)(2,1)S(1)}, bf16[128,896]{1,0:T(8,128)(2,1)S(1)}, u32[]{:S(2)}, u32[]{:S(2)}) collective-permute-start(bf16[128,896]{1,0:T(8,128)(2,1)S(1)} %get-tuple-element.251), channel_id=1, source_target_pairs={{0,6},{1,7},{2,4},{3,5},{4,2},{5,3},{6,0},{7,1},{8,14},{9,15},{10,... | collective-permute-start | bytes 688136 | tf_op jit(solution)/shard_map/ppermute | solution.py:25
  48.3 1.1 collective-permute-start.14
  49.5 1.2 collective-permute-done.10.refs_1_
  50.8 1.6 %collective-permute-start.15 = (bf16[128,896]{1,0:T(8,128)(2,1)S(1)}, bf16[128,896]{1,0:T(8,128)(2,1)S(1)}, u32[]{:S(2)}, u32[]{:S(2)}) collective-permute-start(bf16[128,896]{1,0:T(8,128)(2,1)S(1)} %get-tuple-element.261), channel_id=1, source_target_pairs={{0,2},{1,3},{2,0},{3,1},{4,6},{5,7},{6,4},{7,5},{8,10},{9,11},{10,... | collective-permute-start | bytes 688136 | tf_op jit(solution)/shard_map/ppermute | solution.py:25
  52.3 0.7 shard_map.105.refs_0_
  53.2 2.0 %collective-permute-done.11.refs_1_ = bf16[256,896]{1,0:T(8,128)(2,1)S(1)} collective-permute-done((bf16[256,896]{1,0:T(8,128)(2,1)S(1)}, bf16[256,896]{1,0:T(8,128)(2,1)S(1)}, u32[]{:S(2)}, u32[]{:S(2)}) %collective-permute-start.11) | collective-permute-done | bytes 458784 | tf_op jit(solution)/shard_map/ppermute | solution.py:25
  55.2 2.2 %collective-permute-start.16 = (bf16[128,896]{1,0:T(8,128)(2,1)S(1)}, bf16[128,896]{1,0:T(8,128)(2,1)S(1)}, u32[]{:S(2)}, u32[]{:S(2)}) collective-permute-start(bf16[128,896]{1,0:T(8,128)(2,1)S(1)} %get-tuple-element.266), channel_id=1, source_target_pairs={{0,6},{1,7},{2,4},{3,5},{4,2},{5,3},{6,0},{7,1},{8,14},{9,15},{10,... | collective-permute-start | bytes 688136 | tf_op jit(solution)/shard_map/ppermute | solution.py:25
  57.5 1.1 collective-permute-start.17
  58.6 1.5 %collective-permute-done.13.refs_1_ = bf16[128,896]{1,0:T(8,128)(2,1)S(1)} collective-permute-done((bf16[128,896]{1,0:T(8,128)(2,1)S(1)}, bf16[128,896]{1,0:T(8,128)(2,1)S(1)}, u32[]{:S(2)}, u32[]{:S(2)}) %collective-permute-start.13) | collective-permute-done | bytes 229408 | tf_op jit(solution)/shard_map/ppermute | solution.py:25
  60.2 1.9 %collective-permute-done.14.refs_1_ = bf16[128,896]{1,0:T(8,128)(2,1)S(1)} collective-permute-done((bf16[128,896]{1,0:T(8,128)(2,1)S(1)}, bf16[128,896]{1,0:T(8,128)(2,1)S(1)}, u32[]{:S(2)}, u32[]{:S(2)}) %collective-permute-start.14) | collective-permute-done | bytes 229408 | tf_op jit(solution)/shard_map/ppermute | solution.py:25
  62.1 1.2 collective-permute-start.21
  64.5 1.0 collective-permute-start.19
  65.6 1.1 collective-permute-done.18.refs_1_
  66.7 2.3 %collective-permute-start.24 = (bf16[64,896]{1,0:T(8,128)(2,1)S(1)}, bf16[64,896]{1,0:T(8,128)(2,1)S(1)}, u32[]{:S(2)}, u32[]{:S(2)}) collective-permute-start(bf16[64,896]{1,0:T(8,128)(2,1)S(1)} %get-tuple-element.295), channel_id=1, source_target_pairs={{0,6},{1,7},{2,4},{3,5},{4,2},{5,3},{6,0},{7,1},{8,14},{9,15},{10,... | collective-permute-start | bytes 344072 | tf_op jit(solution)/shard_map/ppermute | solution.py:25
  69.0 1.0 collective-permute-start.22
  70.4 2.2 %collective-permute-start.25 = (bf16[64,896]{1,0:T(8,128)(2,1)S(1)}, bf16[64,896]{1,0:T(8,128)(2,1)S(1)}, u32[]{:S(2)}, u32[]{:S(2)}) collective-permute-start(bf16[64,896]{1,0:T(8,128)(2,1)S(1)} %get-tuple-element.300.refs_0_), channel_id=1, source_target_pairs={{0,6},{1,7},{2,4},{3,5},{4,2},{5,3},{6,0},{7,1},{8,14},{9,15},{10,... | collective-permute-start | bytes 344072 | tf_op jit(solution)/shard_map/ppermute | solution.py:25
  72.6 1.0 collective-permute-start.26
  74.2 1.6 %collective-permute-start.27 = (bf16[64,896]{1,0:T(8,128)(2,1)S(1)}, bf16[64,896]{1,0:T(8,128)(2,1)S(1)}, u32[]{:S(2)}, u32[]{:S(2)}) collective-permute-start(bf16[64,896]{1,0:T(8,128)(2,1)S(1)} %get-tuple-element.304.refs_0_), channel_id=1, source_target_pairs={{0,6},{1,7},{2,4},{3,5},{4,2},{5,3},{6,0},{7,1},{8,14},{9,15},{10,... | collective-permute-start | bytes 344072 | tf_op jit(solution)/shard_map/ppermute | solution.py:25
  75.8 0.7 collective-permute-start.28
  76.9 1.1 collective-permute-start.29
  79.1 1.3 collective-permute-done.27.refs_1_
  80.3 1.1 collective-permute-start.31
  81.4 1.1 collective-permute-start.32
  82.6 2.9 %collective-permute-done.29.refs_1_ = bf16[128,896]{1,0:T(8,128)(2,1)S(1)} collective-permute-done((bf16[128,896]{1,0:T(8,128)(2,1)S(1)}, bf16[128,896]{1,0:T(8,128)(2,1)S(1)}, u32[]{:S(2)}, u32[]{:S(2)}) %collective-permute-start.29) | collective-permute-done | bytes 229408 | tf_op jit(solution)/shard_map/ppermute | solution.py:25
  85.5 1.1 collective-permute-start.33
  87.2 1.2 collective-permute-start.34
  89.0 0.9 collective-permute-start.36
  90.0 1.5 %collective-permute-done.32.refs_1_ = bf16[128,896]{1,0:T(8,128)(2,1)S(1)} collective-permute-done((bf16[128,896]{1,0:T(8,128)(2,1)S(1)}, bf16[128,896]{1,0:T(8,128)(2,1)S(1)}, u32[]{:S(2)}, u32[]{:S(2)}) %collective-permute-start.32) | collective-permute-done | bytes 229408 | tf_op jit(solution)/shard_map/ppermute | solution.py:25
  91.5 1.9 %collective-permute-start.37 = (bf16[256,896]{1,0:T(8,128)(2,1)S(1)}, bf16[256,896]{1,0:T(8,128)(2,1)S(1)}, u32[]{:S(2)}, u32[]{:S(2)}) collective-permute-start(bf16[256,896]{1,0:T(8,128)(2,1)S(1)} %shard_map.125.refs_0_), channel_id=1, source_target_pairs={{0,6},{1,7},{2,4},{3,5},{4,2},{5,3},{6,0},{7,1},{8,14},{9,15},{10,... | collective-permute-start | bytes 1376264 | tf_op jit(solution)/shard_map/ppermute | solution.py:25
  93.4 1.0 collective-permute-start.35
  94.4 4.7 %collective-permute-done.33.refs_1_ = bf16[256,896]{1,0:T(8,128)(2,1)S(1)} collective-permute-done((bf16[256,896]{1,0:T(8,128)(2,1)S(1)}, bf16[256,896]{1,0:T(8,128)(2,1)S(1)}, u32[]{:S(2)}, u32[]{:S(2)}) %collective-permute-start.33) | collective-permute-done | bytes 458784 | tf_op jit(solution)/shard_map/ppermute | solution.py:25
  99.2 2.3 %collective-permute-done.34.refs_1_ = bf16[256,896]{1,0:T(8,128)(2,1)S(1)} collective-permute-done((bf16[256,896]{1,0:T(8,128)(2,1)S(1)}, bf16[256,896]{1,0:T(8,128)(2,1)S(1)}, u32[]{:S(2)}, u32[]{:S(2)}) %collective-permute-start.34) | collective-permute-done | bytes 458784 | tf_op jit(solution)/shard_map/ppermute | solution.py:25
  101.5 1.3 shard_map.128.rest_0_
  102.8 1.3 shard_map.129.rest_0_
  104.3 2.1 %collective-permute-done.37.refs_1_ = bf16[256,896]{1,0:T(8,128)(2,1)S(1)} collective-permute-done((bf16[256,896]{1,0:T(8,128)(2,1)S(1)}, bf16[256,896]{1,0:T(8,128)(2,1)S(1)}, u32[]{:S(2)}, u32[]{:S(2)}) %collective-permute-start.37) | collective-permute-done | bytes 458784 | tf_op jit(solution)/shard_map/ppermute | solution.py:25
  106.4 1.3 shard_map.133
  107.9 1.9 %collective-permute-start.40 = (bf16[128,896]{1,0:T(8,128)(2,1)S(1)}, bf16[128,896]{1,0:T(8,128)(2,1)S(1)}, u32[]{:S(2)}, u32[]{:S(2)}) collective-permute-start(bf16[128,896]{1,0:T(8,128)(2,1)S(1)} %get-tuple-element.350.refs_0_), channel_id=1, source_target_pairs={{0,6},{1,7},{2,4},{3,5},{4,2},{5,3},{6,0},{7,1},{8,14},{9,15},{10,... | collective-permute-start | bytes 688136 | tf_op jit(solution)/shard_map/ppermute | solution.py:25
  109.9 1.3 shard_map.134.refs_0_
  111.4 2.2 %collective-permute-start.42 = (bf16[64,1024]{1,0:T(8,128)(2,1)S(1)}, bf16[64,1024]{1,0:T(8,128)(2,1)S(1)}, u32[]{:S(2)}, u32[]{:S(2)}) collective-permute-start(bf16[64,1024]{1,0:T(8,128)(2,1)S(1)} %get-tuple-element.357), channel_id=1, source_target_pairs={{0,96},{8,104},{16,112},{24,120},{32,64},{40,72},{48,80},{56,88},{... | collective-permute-start | bytes 393224 | tf_op jit(solution)/shard_map/ppermute | solution.py:25
  113.5 1.9 %collective-permute-start.43 = (bf16[64,1024]{1,0:T(8,128)(2,1)S(1)}, bf16[64,1024]{1,0:T(8,128)(2,1)S(1)}, u32[]{:S(2)}, u32[]{:S(2)}) collective-permute-start(bf16[64,1024]{1,0:T(8,128)(2,1)S(1)} %get-tuple-element.358), channel_id=1, source_target_pairs={{0,64},{8,72},{16,80},{24,88},{32,96},{40,104},{48,112},{56,120},{... | collective-permute-start | bytes 393224 | tf_op jit(solution)/shard_map/ppermute | solution.py:25
  115.9 1.7 %collective-permute-start.45 = (bf16[256,896]{1,0:T(8,128)(2,1)S(1)}, bf16[256,896]{1,0:T(8,128)(2,1)S(1)}, u32[]{:S(2)}, u32[]{:S(2)}) collective-permute-start(bf16[256,896]{1,0:T(8,128)(2,1)S(1)} %shard_map.136.refs_0_), channel_id=1, source_target_pairs={{0,6},{1,7},{2,4},{3,5},{4,2},{5,3},{6,0},{7,1},{8,14},{9,15},{10,... | collective-permute-start | bytes 1376264 | tf_op jit(solution)/shard_map/ppermute | solution.py:25
  117.8 3.3 %shard_map.138 = (bf16[1024,1792]{1,0:T(8,128)(2,1)}, bf16[1024,1792]{1,0:T(8,128)(2,1)}) custom-call(s32[1]{0:T(128)} %bitcast.mine_ref.mine, bf16[8,64,1024]{2,1,0:T(8,128)(2,1)S(1)} %bitcast.15, bf16[8,64,1024]{2,1,0:T(8,128)(2,1)S(1)} %bitcast.16, bf16[512,896]{1,0:T(8,128)(2,1)S(1)} %shard_map.126.refs_2_, bf16[512,896]{1,0:T(8,128)(2,1)S(1)} %shard_map.127.refs_3_), custom_call_target="tpu_custom_call" | custom-call | flops 1 | bytes 1 | tf_op jit(solution)/shard_map/pallas_call | solution.py:50
  121.3 2.2 %collective-permute-start.44 = (f32[32,1024]{1,0:T(8,128)S(1)}, f32[32,1024]{1,0:T(8,128)S(1)}, u32[]{:S(2)}, u32[]{:S(2)}) collective-permute-start(f32[32,1024]{1,0:T(8,128)S(1)} %get-tuple-element.362), channel_id=1, source_target_pairs={{0,16},{8,24},{16,0},{24,8},{32,48},{40,56},{48,32},{56,40},{64,80... | collective-permute-start | bytes 393224 | tf_op jit(solution)/shard_map/ppermute | solution.py:25
  123.5 3.3 %shard_map.140 = (bf16[1024,1792]{1,0:T(8,128)(2,1)}, bf16[1024,1792]{1,0:T(8,128)(2,1)}) custom-call(s32[1]{0:T(128)} %bitcast.mine_ref.mine, bf16[8,64,1024]{2,1,0:T(8,128)(2,1)S(1)} %bitcast.17, bf16[8,64,1024]{2,1,0:T(8,128)(2,1)S(1)} %bitcast.18, bf16[512,896]{1,0:T(8,128)(2,1)S(1)} %shard_map.131.refs_2_, ...), custom_call_target="tpu_custom_call", output_to_operand_aliasing={{0}: (5, {}), {1}: (6, {})} | custom-call | flops 1 | bytes 1 | tf_op jit(solution)/shard_map/pallas_call | solution.py:50
  126.8 1.0 collective-permute-done.44
  128.5 0.8 collective-permute-done.45.refs_1_
  129.6 3.0 %shard_map.143 = bf16[1792,1024]{1,0:T(8,128)(2,1)} custom-call(s32[1]{0:T(128)} %bitcast.mine_ref.mine, bf16[8,64,1024]{2,1,0:T(8,128)(2,1)S(1)} %bitcast.23, bf16[8,64,1024]{2,1,0:T(8,128)(2,1)S(1)} %bitcast.24, bf16[512,896]{1,0:T(8,128)(2,1)S(1)} %shard_map.141.refs_2_, bf16[512,896]{1,0:T(8,128)(2,1)S(1)} %shard_map.142.refs_3_), custom_call_target="tpu_custom_call" | custom-call | flops 1 | bytes 1 | tf_op jit(solution)/shard_map/pallas_call | solution.py:50
  (101 shorter events, 17.0 us)
Async XLA Ops:
  0.6 6.5 %collective-permute-start = (bf16[32,1024]{1,0:T(8,128)(2,1)}, bf16[32,1024]{1,0:T(8,128)(2,1)S(1)}, u32[]{:S(2)}, u32[]{:S(2)}) collective-permute-start(bf16[32,1024]{1,0:T(8,128)(2,1)} %refs_0_.1), channel_id=1, source_target_pairs={{0,16},{8,24},{16,0},{24,8},{32,48},{40,56},{48,32},{56,40},{64,80... | collective-permute-start | bytes 196616 | tf_op jit(solution)/shard_map/ppermute | solution.py:25
  4.7 6.0 %collective-permute-start.1 = (bf16[32,1024]{1,0:T(8,128)(2,1)}, bf16[32,1024]{1,0:T(8,128)(2,1)S(1)}, u32[]{:S(2)}, u32[]{:S(2)}) collective-permute-start(bf16[32,1024]{1,0:T(8,128)(2,1)} %refs_2_.1), channel_id=1, source_target_pairs={{0,16},{8,24},{16,0},{24,8},{32,48},{40,56},{48,32},{56,40},{64,80... | collective-permute-start | bytes 196616 | tf_op jit(solution)/shard_map/ppermute | solution.py:25
  4.8 2.0 %copy-start = (bf16[1024,1792]{1,0:T(8,128)(2,1)S(1)}, bf16[1024,1792]{1,0:T(8,128)(2,1)}, u32[]{:S(2)}) copy-start(bf16[1024,1792]{1,0:T(8,128)(2,1)} %w_ref.3) | copy-start | bytes 11010052
  6.8 3.9 %copy-start.3 = (bf16[32,1024]{1,0:T(8,128)(2,1)S(1)}, bf16[32,1024]{1,0:T(8,128)(2,1)}, u32[]{:S(2)}) copy-start(bf16[32,1024]{1,0:T(8,128)(2,1)} %refs_0_.1) | copy-start | bytes 196612
  6.8 3.9 %copy-start.4 = (bf16[32,1024]{1,0:T(8,128)(2,1)S(1)}, bf16[32,1024]{1,0:T(8,128)(2,1)}, u32[]{:S(2)}) copy-start(bf16[32,1024]{1,0:T(8,128)(2,1)} %refs_2_.1) | copy-start | bytes 196612
  6.8 8.2 %copy-start.1 = (bf16[1024,1792]{1,0:T(8,128)(2,1)S(1)}, bf16[1024,1792]{1,0:T(8,128)(2,1)}, u32[]{:S(2)}) copy-start(bf16[1024,1792]{1,0:T(8,128)(2,1)} %w_ref.4) | copy-start | bytes 11010052
  10.7 15.4 %copy-start.2 = (bf16[1792,1024]{1,0:T(8,128)(2,1)S(1)}, bf16[1792,1024]{1,0:T(8,128)(2,1)}, u32[]{:S(2)}) copy-start(bf16[1792,1024]{1,0:T(8,128)(2,1)} %w_ref.5) | copy-start | bytes 11010052
  10.7 9.3 %collective-permute-start.2 = (bf16[128,1024]{1,0:T(8,128)(2,1)S(1)}, bf16[128,1024]{1,0:T(8,128)(2,1)S(1)}, u32[]{:S(2)}, u32[]{:S(2)}) collective-permute-start(bf16[128,1024]{1,0:T(8,128)(2,1)S(1)} %shard_map.85.refs_0_), channel_id=1, source_target_pairs={{0,32},{8,40},{16,48},{24,56},{32,0},{40,8},{48,16},{56,24},{64,96... | collective-permute-start | bytes 786440 | tf_op jit(solution)/shard_map/ppermute | solution.py:25
  12.3 13.2 %collective-permute-start.3 = (bf16[128,1024]{1,0:T(8,128)(2,1)S(1)}, bf16[128,1024]{1,0:T(8,128)(2,1)S(1)}, u32[]{:S(2)}, u32[]{:S(2)}) collective-permute-start(bf16[128,1024]{1,0:T(8,128)(2,1)S(1)} %shard_map.85.refs_0_), channel_id=1, source_target_pairs={{0,96},{8,104},{16,112},{24,120},{32,64},{40,72},{48,80},{56,88},{... | collective-permute-start | bytes 786440 | tf_op jit(solution)/shard_map/ppermute | solution.py:25
  14.4 11.1 %collective-permute-start.4 = (bf16[128,1024]{1,0:T(8,128)(2,1)S(1)}, bf16[128,1024]{1,0:T(8,128)(2,1)S(1)}, u32[]{:S(2)}, u32[]{:S(2)}) collective-permute-start(bf16[128,1024]{1,0:T(8,128)(2,1)S(1)} %shard_map.85.refs_0_), channel_id=1, source_target_pairs={{0,64},{8,72},{16,80},{24,88},{32,96},{40,104},{48,112},{56,120},{... | collective-permute-start | bytes 786440 | tf_op jit(solution)/shard_map/ppermute | solution.py:25
  25.5 2.0 %collective-permute-start.5 = (bf16[256,1024]{1,0:T(8,128)(2,1)S(1)}, bf16[256,1024]{1,0:T(8,128)(2,1)S(1)}, u32[]{:S(2)}, u32[]{:S(2)}) collective-permute-start(bf16[256,1024]{1,0:T(8,128)(2,1)S(1)} %get-tuple-element.199.refs_0_), channel_id=1, source_target_pairs={{0,8},{8,0},{16,24},{24,16},{32,40},{40,32},{48,56},{56,48},{64,72... | collective-permute-start | bytes 1572872 | tf_op jit(solution)/shard_map/ppermute | solution.py:25
  25.6 7.3 %collective-permute-start.6 = (bf16[256,1024]{1,0:T(8,128)(2,1)S(1)}, bf16[256,1024]{1,0:T(8,128)(2,1)S(1)}, u32[]{:S(2)}, u32[]{:S(2)}) collective-permute-start(bf16[256,1024]{1,0:T(8,128)(2,1)S(1)} %get-tuple-element.206.refs_0_), channel_id=1, source_target_pairs={{0,8},{8,0},{16,24},{24,16},{32,40},{40,32},{48,56},{56,48},{64,72... | collective-permute-start | bytes 1572872 | tf_op jit(solution)/shard_map/ppermute | solution.py:25
  28.3 13.4 %collective-permute-start.7 = (bf16[256,896]{1,0:T(8,128)(2,1)S(1)}, bf16[256,896]{1,0:T(8,128)(2,1)S(1)}, u32[]{:S(2)}, u32[]{:S(2)}) collective-permute-start(bf16[256,896]{1,0:T(8,128)(2,1)S(1)} %shard_map.90), channel_id=1, source_target_pairs={{0,2},{1,3},{2,0},{3,1},{4,6},{5,7},{6,4},{7,5},{8,10},{9,11},{10,... | collective-permute-start | bytes 1376264 | tf_op jit(solution)/shard_map/ppermute | solution.py:25
  30.7 14.7 %collective-permute-start.8 = (bf16[256,896]{1,0:T(8,128)(2,1)S(1)}, bf16[256,896]{1,0:T(8,128)(2,1)S(1)}, u32[]{:S(2)}, u32[]{:S(2)}) collective-permute-start(bf16[256,896]{1,0:T(8,128)(2,1)S(1)} %shard_map.91), channel_id=1, source_target_pairs={{0,6},{1,7},{2,4},{3,5},{4,2},{5,3},{6,0},{7,1},{8,14},{9,15},{10,... | collective-permute-start | bytes 1376264 | tf_op jit(solution)/shard_map/ppermute | solution.py:25
  33.8 14.6 %collective-permute-start.9 = (bf16[256,896]{1,0:T(8,128)(2,1)S(1)}, bf16[256,896]{1,0:T(8,128)(2,1)S(1)}, u32[]{:S(2)}, u32[]{:S(2)}) collective-permute-start(bf16[256,896]{1,0:T(8,128)(2,1)S(1)} %shard_map.93), channel_id=1, source_target_pairs={{0,1},{1,0},{2,3},{3,2},{4,5},{5,4},{6,7},{7,6},{8,9},{9,8},{10,11... | collective-permute-start | bytes 1376264 | tf_op jit(solution)/shard_map/ppermute | solution.py:25
  35.6 15.2 %collective-permute-start.10 = (bf16[256,896]{1,0:T(8,128)(2,1)S(1)}, bf16[256,896]{1,0:T(8,128)(2,1)S(1)}, u32[]{:S(2)}, u32[]{:S(2)}) collective-permute-start(bf16[256,896]{1,0:T(8,128)(2,1)S(1)} %shard_map.94), channel_id=1, source_target_pairs={{0,2},{1,3},{2,0},{3,1},{4,6},{5,7},{6,4},{7,5},{8,10},{9,11},{10,... | collective-permute-start | bytes 1376264 | tf_op jit(solution)/shard_map/ppermute | solution.py:25
  39.2 16.0 %collective-permute-start.11 = (bf16[256,896]{1,0:T(8,128)(2,1)S(1)}, bf16[256,896]{1,0:T(8,128)(2,1)S(1)}, u32[]{:S(2)}, u32[]{:S(2)}) collective-permute-start(bf16[256,896]{1,0:T(8,128)(2,1)S(1)} %shard_map.95), channel_id=1, source_target_pairs={{0,6},{1,7},{2,4},{3,5},{4,2},{5,3},{6,0},{7,1},{8,14},{9,15},{10,... | collective-permute-start | bytes 1376264 | tf_op jit(solution)/shard_map/ppermute | solution.py:25
  41.7 15.7 %collective-permute-start.12 = (bf16[256,896]{1,0:T(8,128)(2,1)S(1)}, bf16[256,896]{1,0:T(8,128)(2,1)S(1)}, u32[]{:S(2)}, u32[]{:S(2)}) collective-permute-start(bf16[256,896]{1,0:T(8,128)(2,1)S(1)} %shard_map.100), channel_id=1, source_target_pairs={{0,1},{1,0},{2,3},{3,2},{4,5},{5,4},{6,7},{7,6},{8,9},{9,8},{10,11... | collective-permute-start | bytes 1376264 | tf_op jit(solution)/shard_map/ppermute | solution.py:25
  45.4 14.7 %collective-permute-start.13 = (bf16[128,896]{1,0:T(8,128)(2,1)S(1)}, bf16[128,896]{1,0:T(8,128)(2,1)S(1)}, u32[]{:S(2)}, u32[]{:S(2)}) collective-permute-start(bf16[128,896]{1,0:T(8,128)(2,1)S(1)} %get-tuple-element.251), channel_id=1, source_target_pairs={{0,6},{1,7},{2,4},{3,5},{4,2},{5,3},{6,0},{7,1},{8,14},{9,15},{10,... | collective-permute-start | bytes 688136 | tf_op jit(solution)/shard_map/ppermute | solution.py:25
  48.3 13.7 %collective-permute-start.14 = (bf16[128,896]{1,0:T(8,128)(2,1)S(1)}, bf16[128,896]{1,0:T(8,128)(2,1)S(1)}, u32[]{:S(2)}, u32[]{:S(2)}) collective-permute-start(bf16[128,896]{1,0:T(8,128)(2,1)S(1)} %get-tuple-element.256), channel_id=1, source_target_pairs={{0,1},{1,0},{2,3},{3,2},{4,5},{5,4},{6,7},{7,6},{8,9},{9,8},{10,11... | collective-permute-start | bytes 688136 | tf_op jit(solution)/shard_map/ppermute | solution.py:25
  50.8 11.3 %collective-permute-start.15 = (bf16[128,896]{1,0:T(8,128)(2,1)S(1)}, bf16[128,896]{1,0:T(8,128)(2,1)S(1)}, u32[]{:S(2)}, u32[]{:S(2)}) collective-permute-start(bf16[128,896]{1,0:T(8,128)(2,1)S(1)} %get-tuple-element.261), channel_id=1, source_target_pairs={{0,2},{1,3},{2,0},{3,1},{4,6},{5,7},{6,4},{7,5},{8,10},{9,11},{10,... | collective-permute-start | bytes 688136 | tf_op jit(solution)/shard_map/ppermute | solution.py:25
  55.2 9.3 %collective-permute-start.16 = (bf16[128,896]{1,0:T(8,128)(2,1)S(1)}, bf16[128,896]{1,0:T(8,128)(2,1)S(1)}, u32[]{:S(2)}, u32[]{:S(2)}) collective-permute-start(bf16[128,896]{1,0:T(8,128)(2,1)S(1)} %get-tuple-element.266), channel_id=1, source_target_pairs={{0,6},{1,7},{2,4},{3,5},{4,2},{5,3},{6,0},{7,1},{8,14},{9,15},{10,... | collective-permute-start | bytes 688136 | tf_op jit(solution)/shard_map/ppermute | solution.py:25
  57.5 8.1 %collective-permute-start.17 = (bf16[128,896]{1,0:T(8,128)(2,1)S(1)}, bf16[128,896]{1,0:T(8,128)(2,1)S(1)}, u32[]{:S(2)}, u32[]{:S(2)}) collective-permute-start(bf16[128,896]{1,0:T(8,128)(2,1)S(1)} %get-tuple-element.271), channel_id=1, source_target_pairs={{0,1},{1,0},{2,3},{3,2},{4,5},{5,4},{6,7},{7,6},{8,9},{9,8},{10,11... | collective-permute-start | bytes 688136 | tf_op jit(solution)/shard_map/ppermute | solution.py:25
  60.1 6.6 %collective-permute-start.18 = (bf16[128,896]{1,0:T(8,128)(2,1)S(1)}, bf16[128,896]{1,0:T(8,128)(2,1)S(1)}, u32[]{:S(2)}, u32[]{:S(2)}) collective-permute-start(bf16[128,896]{1,0:T(8,128)(2,1)S(1)} %get-tuple-element.276), channel_id=1, source_target_pairs={{0,2},{1,3},{2,0},{3,1},{4,6},{5,7},{6,4},{7,5},{8,10},{9,11},{10,... | collective-permute-start | bytes 688136 | tf_op jit(solution)/shard_map/ppermute | solution.py:25
  62.1 6.9 %collective-permute-start.21 = (bf16[64,896]{1,0:T(8,128)(2,1)S(1)}, bf16[64,896]{1,0:T(8,128)(2,1)S(1)}, u32[]{:S(2)}, u32[]{:S(2)}) collective-permute-start(bf16[64,896]{1,0:T(8,128)(2,1)S(1)} %get-tuple-element.285), channel_id=1, source_target_pairs={{0,6},{1,7},{2,4},{3,5},{4,2},{5,3},{6,0},{7,1},{8,14},{9,15},{10,... | collective-permute-start | bytes 344072 | tf_op jit(solution)/shard_map/ppermute | solution.py:25
  63.3 6.7 %collective-permute-start.20 = (bf16[64,896]{1,0:T(8,128)(2,1)S(1)}, bf16[64,896]{1,0:T(8,128)(2,1)S(1)}, u32[]{:S(2)}, u32[]{:S(2)}) collective-permute-start(bf16[64,896]{1,0:T(8,128)(2,1)S(1)} %get-tuple-element.283), channel_id=1, source_target_pairs={{0,2},{1,3},{2,0},{3,1},{4,6},{5,7},{6,4},{7,5},{8,10},{9,11},{10,... | collective-permute-start | bytes 344072 | tf_op jit(solution)/shard_map/ppermute | solution.py:25
  64.5 5.7 %collective-permute-start.19 = (bf16[64,896]{1,0:T(8,128)(2,1)S(1)}, bf16[64,896]{1,0:T(8,128)(2,1)S(1)}, u32[]{:S(2)}, u32[]{:S(2)}) collective-permute-start(bf16[64,896]{1,0:T(8,128)(2,1)S(1)} %get-tuple-element.281), channel_id=1, source_target_pairs={{0,1},{1,0},{2,3},{3,2},{4,5},{5,4},{6,7},{7,6},{8,9},{9,8},{10,11... | collective-permute-start | bytes 344072 | tf_op jit(solution)/shard_map/ppermute | solution.py:25
  66.7 6.9 %collective-permute-start.24 = (bf16[64,896]{1,0:T(8,128)(2,1)S(1)}, bf16[64,896]{1,0:T(8,128)(2,1)S(1)}, u32[]{:S(2)}, u32[]{:S(2)}) collective-permute-start(bf16[64,896]{1,0:T(8,128)(2,1)S(1)} %get-tuple-element.295), channel_id=1, source_target_pairs={{0,6},{1,7},{2,4},{3,5},{4,2},{5,3},{6,0},{7,1},{8,14},{9,15},{10,... | collective-permute-start | bytes 344072 | tf_op jit(solution)/shard_map/ppermute | solution.py:25
  69.0 4.8 %collective-permute-start.23 = (bf16[64,896]{1,0:T(8,128)(2,1)S(1)}, bf16[64,896]{1,0:T(8,128)(2,1)S(1)}, u32[]{:S(2)}, u32[]{:S(2)}) collective-permute-start(bf16[64,896]{1,0:T(8,128)(2,1)S(1)} %get-tuple-element.293), channel_id=1, source_target_pairs={{0,2},{1,3},{2,0},{3,1},{4,6},{5,7},{6,4},{7,5},{8,10},{9,11},{10,... | collective-permute-start | bytes 344072 | tf_op jit(solution)/shard_map/ppermute | solution.py:25
  69.0 5.0 %collective-permute-start.22 = (bf16[64,896]{1,0:T(8,128)(2,1)S(1)}, bf16[64,896]{1,0:T(8,128)(2,1)S(1)}, u32[]{:S(2)}, u32[]{:S(2)}) collective-permute-start(bf16[64,896]{1,0:T(8,128)(2,1)S(1)} %get-tuple-element.291), channel_id=1, source_target_pairs={{0,1},{1,0},{2,3},{3,2},{4,5},{5,4},{6,7},{7,6},{8,9},{9,8},{10,11... | collective-permute-start | bytes 344072 | tf_op jit(solution)/shard_map/ppermute | solution.py:25
  70.4 6.5 %collective-permute-start.25 = (bf16[64,896]{1,0:T(8,128)(2,1)S(1)}, bf16[64,896]{1,0:T(8,128)(2,1)S(1)}, u32[]{:S(2)}, u32[]{:S(2)}) collective-permute-start(bf16[64,896]{1,0:T(8,128)(2,1)S(1)} %get-tuple-element.300.refs_0_), channel_id=1, source_target_pairs={{0,6},{1,7},{2,4},{3,5},{4,2},{5,3},{6,0},{7,1},{8,14},{9,15},{10,... | collective-permute-start | bytes 344072 | tf_op jit(solution)/shard_map/ppermute | solution.py:25
  72.6 6.0 %collective-permute-start.26 = (bf16[64,896]{1,0:T(8,128)(2,1)S(1)}, bf16[64,896]{1,0:T(8,128)(2,1)S(1)}, u32[]{:S(2)}, u32[]{:S(2)}) collective-permute-start(bf16[64,896]{1,0:T(8,128)(2,1)S(1)} %get-tuple-element.302.refs_0_), channel_id=1, source_target_pairs={{0,1},{1,0},{2,3},{3,2},{4,5},{5,4},{6,7},{7,6},{8,9},{9,8},{10,11... | collective-permute-start | bytes 344072 | tf_op jit(solution)/shard_map/ppermute | solution.py:25
  74.2 6.1 %collective-permute-start.27 = (bf16[64,896]{1,0:T(8,128)(2,1)S(1)}, bf16[64,896]{1,0:T(8,128)(2,1)S(1)}, u32[]{:S(2)}, u32[]{:S(2)}) collective-permute-start(bf16[64,896]{1,0:T(8,128)(2,1)S(1)} %get-tuple-element.304.refs_0_), channel_id=1, source_target_pairs={{0,6},{1,7},{2,4},{3,5},{4,2},{5,3},{6,0},{7,1},{8,14},{9,15},{10,... | collective-permute-start | bytes 344072 | tf_op jit(solution)/shard_map/ppermute | solution.py:25
  75.8 5.6 %collective-permute-start.28 = (bf16[64,896]{1,0:T(8,128)(2,1)S(1)}, bf16[64,896]{1,0:T(8,128)(2,1)S(1)}, u32[]{:S(2)}, u32[]{:S(2)}) collective-permute-start(bf16[64,896]{1,0:T(8,128)(2,1)S(1)} %get-tuple-element.306.refs_0_), channel_id=1, source_target_pairs={{0,2},{1,3},{2,0},{3,1},{4,6},{5,7},{6,4},{7,5},{8,10},{9,11},{10,... | collective-permute-start | bytes 344072 | tf_op jit(solution)/shard_map/ppermute | solution.py:25
  76.9 8.6 %collective-permute-start.29 = (bf16[128,896]{1,0:T(8,128)(2,1)S(1)}, bf16[128,896]{1,0:T(8,128)(2,1)S(1)}, u32[]{:S(2)}, u32[]{:S(2)}) collective-permute-start(bf16[128,896]{1,0:T(8,128)(2,1)S(1)} %shard_map.117.refs_0_), channel_id=1, source_target_pairs={{0,1},{1,0},{2,3},{3,2},{4,5},{5,4},{6,7},{7,6},{8,9},{9,8},{10,11... | collective-permute-start | bytes 688136 | tf_op jit(solution)/shard_map/ppermute | solution.py:25
  78.6 8.6 %collective-permute-start.30 = (bf16[128,896]{1,0:T(8,128)(2,1)S(1)}, bf16[128,896]{1,0:T(8,128)(2,1)S(1)}, u32[]{:S(2)}, u32[]{:S(2)}) collective-permute-start(bf16[128,896]{1,0:T(8,128)(2,1)S(1)} %shard_map.118.refs_0_), channel_id=1, source_target_pairs={{0,2},{1,3},{2,0},{3,1},{4,6},{5,7},{6,4},{7,5},{8,10},{9,11},{10,... | collective-permute-start | bytes 688136 | tf_op jit(solution)/shard_map/ppermute | solution.py:25
  80.3 8.7 %collective-permute-start.31 = (bf16[128,896]{1,0:T(8,128)(2,1)S(1)}, bf16[128,896]{1,0:T(8,128)(2,1)S(1)}, u32[]{:S(2)}, u32[]{:S(2)}) collective-permute-start(bf16[128,896]{1,0:T(8,128)(2,1)S(1)} %shard_map.119.refs_0_), channel_id=1, source_target_pairs={{0,1},{1,0},{2,3},{3,2},{4,5},{5,4},{6,7},{7,6},{8,9},{9,8},{10,11... | collective-permute-start | bytes 688136 | tf_op jit(solution)/shard_map/ppermute | solution.py:25
  81.4 10.0 %collective-permute-start.32 = (bf16[128,896]{1,0:T(8,128)(2,1)S(1)}, bf16[128,896]{1,0:T(8,128)(2,1)S(1)}, u32[]{:S(2)}, u32[]{:S(2)}) collective-permute-start(bf16[128,896]{1,0:T(8,128)(2,1)S(1)} %shard_map.120.refs_0_), channel_id=1, source_target_pairs={{0,1},{1,0},{2,3},{3,2},{4,5},{5,4},{6,7},{7,6},{8,9},{9,8},{10,11... | collective-permute-start | bytes 688136 | tf_op jit(solution)/shard_map/ppermute | solution.py:25
  85.5 13.5 %collective-permute-start.33 = (bf16[256,896]{1,0:T(8,128)(2,1)S(1)}, bf16[256,896]{1,0:T(8,128)(2,1)S(1)}, u32[]{:S(2)}, u32[]{:S(2)}) collective-permute-start(bf16[256,896]{1,0:T(8,128)(2,1)S(1)} %shard_map.122.refs_0_), channel_id=1, source_target_pairs={{0,2},{1,3},{2,0},{3,1},{4,6},{5,7},{6,4},{7,5},{8,10},{9,11},{10,... | collective-permute-start | bytes 1376264 | tf_op jit(solution)/shard_map/ppermute | solution.py:25
  87.2 14.2 %collective-permute-start.34 = (bf16[256,896]{1,0:T(8,128)(2,1)S(1)}, bf16[256,896]{1,0:T(8,128)(2,1)S(1)}, u32[]{:S(2)}, u32[]{:S(2)}) collective-permute-start(bf16[256,896]{1,0:T(8,128)(2,1)S(1)} %shard_map.123.refs_0_), channel_id=1, source_target_pairs={{0,6},{1,7},{2,4},{3,5},{4,2},{5,3},{6,0},{7,1},{8,14},{9,15},{10,... | collective-permute-start | bytes 1376264 | tf_op jit(solution)/shard_map/ppermute | solution.py:25
  89.0 15.1 %collective-permute-start.36 = (bf16[256,896]{1,0:T(8,128)(2,1)S(1)}, bf16[256,896]{1,0:T(8,128)(2,1)S(1)}, u32[]{:S(2)}, u32[]{:S(2)}) collective-permute-start(bf16[256,896]{1,0:T(8,128)(2,1)S(1)} %shard_map.124.refs_0_), channel_id=1, source_target_pairs={{0,2},{1,3},{2,0},{3,1},{4,6},{5,7},{6,4},{7,5},{8,10},{9,11},{10,... | collective-permute-start | bytes 1376264 | tf_op jit(solution)/shard_map/ppermute | solution.py:25
  91.5 14.9 %collective-permute-start.37 = (bf16[256,896]{1,0:T(8,128)(2,1)S(1)}, bf16[256,896]{1,0:T(8,128)(2,1)S(1)}, u32[]{:S(2)}, u32[]{:S(2)}) collective-permute-start(bf16[256,896]{1,0:T(8,128)(2,1)S(1)} %shard_map.125.refs_0_), channel_id=1, source_target_pairs={{0,6},{1,7},{2,4},{3,5},{4,2},{5,3},{6,0},{7,1},{8,14},{9,15},{10,... | collective-permute-start | bytes 1376264 | tf_op jit(solution)/shard_map/ppermute | solution.py:25
  93.4 10.8 %collective-permute-start.35 = (bf16[64,1792]{1,0:T(8,128)(2,1)S(1)}, bf16[64,1792]{1,0:T(8,128)(2,1)S(1)}, u32[]{:S(2)}, u32[]{:S(2)}) collective-permute-start(bf16[64,1792]{1,0:T(8,128)(2,1)S(1)} %shard_map.121.refs_0_), channel_id=1, source_target_pairs={{0,1},{1,0},{2,3},{3,2},{4,5},{5,4},{6,7},{7,6},{8,9},{9,8},{10,11... | collective-permute-start | bytes 688136 | tf_op jit(solution)/shard_map/ppermute | solution.py:25
  107.7 3.4 %collective-permute-start.38 = (f32[256,1024]{1,0:T(8,128)S(1)}, f32[256,1024]{1,0:T(8,128)S(1)}, u32[]{:S(2)}, u32[]{:S(2)}) collective-permute-start(f32[256,1024]{1,0:T(8,128)S(1)} %shard_map.133), channel_id=1, source_target_pairs={{0,8},{8,0},{16,24},{24,16},{32,40},{40,32},{48,56},{56,48},{64,72... | collective-permute-start | bytes 3145736 | tf_op jit(solution)/shard_map/ppermute | solution.py:25
  107.8 8.0 %collective-permute-start.39 = (bf16[128,896]{1,0:T(8,128)(2,1)S(1)}, bf16[128,896]{1,0:T(8,128)(2,1)S(1)}, u32[]{:S(2)}, u32[]{:S(2)}) collective-permute-start(bf16[128,896]{1,0:T(8,128)(2,1)S(1)} %get-tuple-element.348.refs_0_), channel_id=1, source_target_pairs={{0,2},{1,3},{2,0},{3,1},{4,6},{5,7},{6,4},{7,5},{8,10},{9,11},{10,... | collective-permute-start | bytes 688136 | tf_op jit(solution)/shard_map/ppermute | solution.py:25
  107.9 9.7 %collective-permute-start.40 = (bf16[128,896]{1,0:T(8,128)(2,1)S(1)}, bf16[128,896]{1,0:T(8,128)(2,1)S(1)}, u32[]{:S(2)}, u32[]{:S(2)}) collective-permute-start(bf16[128,896]{1,0:T(8,128)(2,1)S(1)} %get-tuple-element.350.refs_0_), channel_id=1, source_target_pairs={{0,6},{1,7},{2,4},{3,5},{4,2},{5,3},{6,0},{7,1},{8,14},{9,15},{10,... | collective-permute-start | bytes 688136 | tf_op jit(solution)/shard_map/ppermute | solution.py:25
  111.3 9.9 %collective-permute-start.41 = (bf16[64,1024]{1,0:T(8,128)(2,1)S(1)}, bf16[64,1024]{1,0:T(8,128)(2,1)S(1)}, u32[]{:S(2)}, u32[]{:S(2)}) collective-permute-start(bf16[64,1024]{1,0:T(8,128)(2,1)S(1)} %get-tuple-element.356), channel_id=1, source_target_pairs={{0,32},{8,40},{16,48},{24,56},{32,0},{40,8},{48,16},{56,24},{64,96... | collective-permute-start | bytes 393224 | tf_op jit(solution)/shard_map/ppermute | solution.py:25
  111.4 9.8 %collective-permute-start.42 = (bf16[64,1024]{1,0:T(8,128)(2,1)S(1)}, bf16[64,1024]{1,0:T(8,128)(2,1)S(1)}, u32[]{:S(2)}, u32[]{:S(2)}) collective-permute-start(bf16[64,1024]{1,0:T(8,128)(2,1)S(1)} %get-tuple-element.357), channel_id=1, source_target_pairs={{0,96},{8,104},{16,112},{24,120},{32,64},{40,72},{48,80},{56,88},{... | collective-permute-start | bytes 393224 | tf_op jit(solution)/shard_map/ppermute | solution.py:25
  113.5 7.7 %collective-permute-start.43 = (bf16[64,1024]{1,0:T(8,128)(2,1)S(1)}, bf16[64,1024]{1,0:T(8,128)(2,1)S(1)}, u32[]{:S(2)}, u32[]{:S(2)}) collective-permute-start(bf16[64,1024]{1,0:T(8,128)(2,1)S(1)} %get-tuple-element.358), channel_id=1, source_target_pairs={{0,64},{8,72},{16,80},{24,88},{32,96},{40,104},{48,112},{56,120},{... | collective-permute-start | bytes 393224 | tf_op jit(solution)/shard_map/ppermute | solution.py:25
  115.9 13.4 %collective-permute-start.45 = (bf16[256,896]{1,0:T(8,128)(2,1)S(1)}, bf16[256,896]{1,0:T(8,128)(2,1)S(1)}, u32[]{:S(2)}, u32[]{:S(2)}) collective-permute-start(bf16[256,896]{1,0:T(8,128)(2,1)S(1)} %shard_map.136.refs_0_), channel_id=1, source_target_pairs={{0,6},{1,7},{2,4},{3,5},{4,2},{5,3},{6,0},{7,1},{8,14},{9,15},{10,... | collective-permute-start | bytes 1376264 | tf_op jit(solution)/shard_map/ppermute | solution.py:25
  117.6 11.9 %collective-permute-start.46 = (bf16[256,896]{1,0:T(8,128)(2,1)S(1)}, bf16[256,896]{1,0:T(8,128)(2,1)S(1)}, u32[]{:S(2)}, u32[]{:S(2)}) collective-permute-start(bf16[256,896]{1,0:T(8,128)(2,1)S(1)} %shard_map.137.refs_0_), channel_id=1, source_target_pairs={{0,2},{1,3},{2,0},{3,1},{4,6},{5,7},{6,4},{7,5},{8,10},{9,11},{10,... | collective-permute-start | bytes 1376264 | tf_op jit(solution)/shard_map/ppermute | solution.py:25
  121.3 6.6 %collective-permute-start.44 = (f32[32,1024]{1,0:T(8,128)S(1)}, f32[32,1024]{1,0:T(8,128)S(1)}, u32[]{:S(2)}, u32[]{:S(2)}) collective-permute-start(f32[32,1024]{1,0:T(8,128)S(1)} %get-tuple-element.362), channel_id=1, source_target_pairs={{0,16},{8,24},{16,0},{24,8},{32,48},{40,56},{48,32},{56,40},{64,80... | collective-permute-start | bytes 393224 | tf_op jit(solution)/shard_map/ppermute | solution.py:25

commit v5 on v4

--- a/solution.py
+++ b/solution.py
@@ -322,7 +322,8 @@
     weights = [fetch(order, gate_weight)]
     both = join(order, (inputs, far_x, out_grad, far_g), tuple((k, 0, n) for k in range(4)))
     n = 2 * n
-    fars = [swap(both, "row", mask) for mask in (XA, XB, XAB)]
+    far = swap(both, "row", XAB)
+    fars = [swap(both, "row", mask) for mask in (XA, XB)] + [far]
     weights.append(fetch(order, up_weight))
     x, g = join(
         order,
@@ -455,7 +456,8 @@
         keep,
         far,
     )
-    rings = [swap(v, "row", mask) for v, mask in zip(sends, (XA, XB, XAB))]
+    ring = swap(sends[2], "row", XAB)
+    rings = [swap(v, "row", mask) for v, mask in zip(sends, (XA, XB))] + [ring]
     grow(2, 2)
     grow(5, 2)
     weight_step(0, 1)

time: 133 us -> 133 us (level)
  no operation moved by 1% of the time
where the time goes in v5:
time: 133 us
  starting transfers between devices  56.5 us (42%)
  waiting for transfers between devices  45.7 us (34%)
  Pallas kernels  26.5 us (20%)
  local copies, waits for them, and re-layouts  2.06 us (2%)
    ppermute x47, starting transfers between devices, swap(): return lax.ppermute(value, axis, [(i, i ^ mask) for i in range(size)])  56.5 us
    ppermute x47, waiting for transfers between devices, swap(): return lax.ppermute(value, axis, [(i, i ^ mask) for i in range(size)])  45.7 us
    pallas_call x60, Pallas kernels, run(): out = call(self.mine, *args)  26.5 us
  transfers between devices with their start and end apart: 47, of which 30 were waited for; matrix products, arithmetic and copies ran while one was open for 0% of the time, Pallas kernels for 17%

profile of v5, /device:TPU:0, one launch (start us, length us, event | category | flops | bytes accessed | tf_op | source)
XLA Modules:
  0.0 132.8 jit_solution(17783360043333112945)
XLA Ops:
  0.6 4.0 %collective-permute-start = (bf16[32,1024]{1,0:T(8,128)(2,1)}, bf16[32,1024]{1,0:T(8,128)(2,1)S(1)}, u32[]{:S(2)}, u32[]{:S(2)}) collective-permute-start(bf16[32,1024]{1,0:T(8,128)(2,1)} %refs_0_.1), channel_id=1, source_target_pairs={{0,16},{8,24},{16,0},{24,8},{32,48},{40,56},{48,32},{56,40},{64,80... | collective-permute-start | bytes 196616 | tf_op jit(solution)/shard_map/ppermute | solution.py:25
  4.8 2.0 %copy-done = bf16[1024,1792]{1,0:T(8,128)(2,1)S(1)} copy-done((bf16[1024,1792]{1,0:T(8,128)(2,1)S(1)}, bf16[1024,1792]{1,0:T(8,128)(2,1)}, u32[]{:S(2)}) %copy-start) | copy-done | bytes 3670040
  7.1 3.5 %collective-permute-done.1.refs_3_ = bf16[32,1024]{1,0:T(8,128)(2,1)S(1)} collective-permute-done((bf16[32,1024]{1,0:T(8,128)(2,1)}, bf16[32,1024]{1,0:T(8,128)(2,1)S(1)}, u32[]{:S(2)}, u32[]{:S(2)}) %collective-permute-start.1) | collective-permute-done | bytes 65568 | tf_op jit(solution)/shard_map/ppermute | solution.py:25
  10.7 1.6 %collective-permute-start.2 = (bf16[128,1024]{1,0:T(8,128)(2,1)S(1)}, bf16[128,1024]{1,0:T(8,128)(2,1)S(1)}, u32[]{:S(2)}, u32[]{:S(2)}) collective-permute-start(bf16[128,1024]{1,0:T(8,128)(2,1)S(1)} %shard_map.85.refs_0_), channel_id=1, source_target_pairs={{0,32},{8,40},{16,48},{24,56},{32,0},{40,8},{48,16},{56,24},{64,96... | collective-permute-start | bytes 786440 | tf_op jit(solution)/shard_map/ppermute | solution.py:25
  12.3 2.1 %collective-permute-start.3 = (bf16[128,1024]{1,0:T(8,128)(2,1)S(1)}, bf16[128,1024]{1,0:T(8,128)(2,1)S(1)}, u32[]{:S(2)}, u32[]{:S(2)}) collective-permute-start(bf16[128,1024]{1,0:T(8,128)(2,1)S(1)} %shard_map.85.refs_0_), channel_id=1, source_target_pairs={{0,96},{8,104},{16,112},{24,120},{32,64},{40,72},{48,80},{56,88},{... | collective-permute-start | bytes 786440 | tf_op jit(solution)/shard_map/ppermute | solution.py:25
  15.3 4.7 %collective-permute-done.2.refs_1_ = bf16[128,1024]{1,0:T(8,128)(2,1)S(1)} collective-permute-done((bf16[128,1024]{1,0:T(8,128)(2,1)S(1)}, bf16[128,1024]{1,0:T(8,128)(2,1)S(1)}, u32[]{:S(2)}, u32[]{:S(2)}) %collective-permute-start.2) | collective-permute-done | bytes 262176 | tf_op jit(solution)/shard_map/ppermute | solution.py:25
  20.0 5.4 %collective-permute-done.3.refs_2_ = bf16[128,1024]{1,0:T(8,128)(2,1)S(1)} collective-permute-done((bf16[128,1024]{1,0:T(8,128)(2,1)S(1)}, bf16[128,1024]{1,0:T(8,128)(2,1)S(1)}, u32[]{:S(2)}, u32[]{:S(2)}) %collective-permute-start.3) | collective-permute-done | bytes 262176 | tf_op jit(solution)/shard_map/ppermute | solution.py:25
  26.4 1.1 collective-permute-done.5.refs_1_
  28.3 1.7 %collective-permute-start.7 = (bf16[256,896]{1,0:T(8,128)(2,1)S(1)}, bf16[256,896]{1,0:T(8,128)(2,1)S(1)}, u32[]{:S(2)}, u32[]{:S(2)}) collective-permute-start(bf16[256,896]{1,0:T(8,128)(2,1)S(1)} %shard_map.90), channel_id=1, source_target_pairs={{0,2},{1,3},{2,0},{3,1},{4,6},{5,7},{6,4},{7,5},{8,10},{9,11},{10,... | collective-permute-start | bytes 1376264 | tf_op jit(solution)/shard_map/ppermute | solution.py:25
  30.7 2.3 %collective-permute-start.8 = (bf16[256,896]{1,0:T(8,128)(2,1)S(1)}, bf16[256,896]{1,0:T(8,128)(2,1)S(1)}, u32[]{:S(2)}, u32[]{:S(2)}) collective-permute-start(bf16[256,896]{1,0:T(8,128)(2,1)S(1)} %shard_map.91), channel_id=1, source_target_pairs={{0,6},{1,7},{2,4},{3,5},{4,2},{5,3},{6,0},{7,1},{8,14},{9,15},{10,... | collective-permute-start | bytes 1376264 | tf_op jit(solution)/shard_map/ppermute | solution.py:25
  33.0 0.7 shard_map.93
  33.8 1.1 collective-permute-start.9
  35.6 0.8 collective-permute-start.10
  38.5 0.7 shard_map.98.refs_0_
  40.7 0.7 shard_map.100
  41.7 1.0 collective-permute-start.12
  42.8 2.5 %collective-permute-done.8.refs_1_ = bf16[256,896]{1,0:T(8,128)(2,1)S(1)} collective-permute-done((bf16[256,896]{1,0:T(8,128)(2,1)S(1)}, bf16[256,896]{1,0:T(8,128)(2,1)S(1)}, u32[]{:S(2)}, u32[]{:S(2)}) %collective-permute-start.8) | collective-permute-done | bytes 458784 | tf_op jit(solution)/shard_map/ppermute | solution.py:25
  45.4 2.2 %collective-permute-start.13 = (bf16[128,896]{1,0:T(8,128)(2,1)S(1)}, bf16[128,896]{1,0:T(8,128)(2,1)S(1)}, u32[]{:S(2)}, u32[]{:S(2)}) collective-permute-start(bf16[128,896]{1,0:T(8,128)(2,1)S(1)} %get-tuple-element.251), channel_id=1, source_target_pairs={{0,6},{1,7},{2,4},{3,5},{4,2},{5,3},{6,0},{7,1},{8,14},{9,15},{10,... | collective-permute-start | bytes 688136 | tf_op jit(solution)/shard_map/ppermute | solution.py:25
  48.3 1.1 collective-permute-start.14
  49.5 1.2 collective-permute-done.10.refs_1_
  50.8 1.6 %collective-permute-start.15 = (bf16[128,896]{1,0:T(8,128)(2,1)S(1)}, bf16[128,896]{1,0:T(8,128)(2,1)S(1)}, u32[]{:S(2)}, u32[]{:S(2)}) collective-permute-start(bf16[128,896]{1,0:T(8,128)(2,1)S(1)} %get-tuple-element.261), channel_id=1, source_target_pairs={{0,2},{1,3},{2,0},{3,1},{4,6},{5,7},{6,4},{7,5},{8,10},{9,11},{10,... | collective-permute-start | bytes 688136 | tf_op jit(solution)/shard_map/ppermute | solution.py:25
  52.3 0.7 shard_map.105.refs_0_
  53.2 2.0 %collective-permute-done.11.refs_1_ = bf16[256,896]{1,0:T(8,128)(2,1)S(1)} collective-permute-done((bf16[256,896]{1,0:T(8,128)(2,1)S(1)}, bf16[256,896]{1,0:T(8,128)(2,1)S(1)}, u32[]{:S(2)}, u32[]{:S(2)}) %collective-permute-start.11) | collective-permute-done | bytes 458784 | tf_op jit(solution)/shard_map/ppermute | solution.py:25
  55.2 2.2 %collective-permute-start.16 = (bf16[128,896]{1,0:T(8,128)(2,1)S(1)}, bf16[128,896]{1,0:T(8,128)(2,1)S(1)}, u32[]{:S(2)}, u32[]{:S(2)}) collective-permute-start(bf16[128,896]{1,0:T(8,128)(2,1)S(1)} %get-tuple-element.266), channel_id=1, source_target_pairs={{0,6},{1,7},{2,4},{3,5},{4,2},{5,3},{6,0},{7,1},{8,14},{9,15},{10,... | collective-permute-start | bytes 688136 | tf_op jit(solution)/shard_map/ppermute | solution.py:25
  57.5 1.1 collective-permute-start.17
  58.6 1.5 %collective-permute-done.13.refs_1_ = bf16[128,896]{1,0:T(8,128)(2,1)S(1)} collective-permute-done((bf16[128,896]{1,0:T(8,128)(2,1)S(1)}, bf16[128,896]{1,0:T(8,128)(2,1)S(1)}, u32[]{:S(2)}, u32[]{:S(2)}) %collective-permute-start.13) | collective-permute-done | bytes 229408 | tf_op jit(solution)/shard_map/ppermute | solution.py:25
  60.2 1.9 %collective-permute-done.14.refs_1_ = bf16[128,896]{1,0:T(8,128)(2,1)S(1)} collective-permute-done((bf16[128,896]{1,0:T(8,128)(2,1)S(1)}, bf16[128,896]{1,0:T(8,128)(2,1)S(1)}, u32[]{:S(2)}, u32[]{:S(2)}) %collective-permute-start.14) | collective-permute-done | bytes 229408 | tf_op jit(solution)/shard_map/ppermute | solution.py:25
  62.1 1.2 collective-permute-start.21
  64.5 1.0 collective-permute-start.19
  65.6 1.1 collective-permute-done.18.refs_1_
  66.7 2.3 %collective-permute-start.24 = (bf16[64,896]{1,0:T(8,128)(2,1)S(1)}, bf16[64,896]{1,0:T(8,128)(2,1)S(1)}, u32[]{:S(2)}, u32[]{:S(2)}) collective-permute-start(bf16[64,896]{1,0:T(8,128)(2,1)S(1)} %get-tuple-element.295), channel_id=1, source_target_pairs={{0,6},{1,7},{2,4},{3,5},{4,2},{5,3},{6,0},{7,1},{8,14},{9,15},{10,... | collective-permute-start | bytes 344072 | tf_op jit(solution)/shard_map/ppermute | solution.py:25
  69.0 1.0 collective-permute-start.22
  70.4 2.2 %collective-permute-start.25 = (bf16[64,896]{1,0:T(8,128)(2,1)S(1)}, bf16[64,896]{1,0:T(8,128)(2,1)S(1)}, u32[]{:S(2)}, u32[]{:S(2)}) collective-permute-start(bf16[64,896]{1,0:T(8,128)(2,1)S(1)} %get-tuple-element.300.refs_0_), channel_id=1, source_target_pairs={{0,6},{1,7},{2,4},{3,5},{4,2},{5,3},{6,0},{7,1},{8,14},{9,15},{10,... | collective-permute-start | bytes 344072 | tf_op jit(solution)/shard_map/ppermute | solution.py:25
  72.6 1.0 collective-permute-start.26
  74.2 1.6 %collective-permute-start.27 = (bf16[64,896]{1,0:T(8,128)(2,1)S(1)}, bf16[64,896]{1,0:T(8,128)(2,1)S(1)}, u32[]{:S(2)}, u32[]{:S(2)}) collective-permute-start(bf16[64,896]{1,0:T(8,128)(2,1)S(1)} %get-tuple-element.304.refs_0_), channel_id=1, source_target_pairs={{0,6},{1,7},{2,4},{3,5},{4,2},{5,3},{6,0},{7,1},{8,14},{9,15},{10,... | collective-permute-start | bytes 344072 | tf_op jit(solution)/shard_map/ppermute | solution.py:25
  75.8 0.7 collective-permute-start.28
  76.9 1.1 collective-permute-start.29
  79.1 1.3 collective-permute-done.27.refs_1_
  80.3 1.1 collective-permute-start.31
  81.4 1.1 collective-permute-start.32
  82.6 2.9 %collective-permute-done.29.refs_1_ = bf16[128,896]{1,0:T(8,128)(2,1)S(1)} collective-permute-done((bf16[128,896]{1,0:T(8,128)(2,1)S(1)}, bf16[128,896]{1,0:T(8,128)(2,1)S(1)}, u32[]{:S(2)}, u32[]{:S(2)}) %collective-permute-start.29) | collective-permute-done | bytes 229408 | tf_op jit(solution)/shard_map/ppermute | solution.py:25
  85.5 1.1 collective-permute-start.33
  87.2 1.2 collective-permute-start.34
  89.0 0.9 collective-permute-start.36
  90.0 1.5 %collective-permute-done.32.refs_1_ = bf16[128,896]{1,0:T(8,128)(2,1)S(1)} collective-permute-done((bf16[128,896]{1,0:T(8,128)(2,1)S(1)}, bf16[128,896]{1,0:T(8,128)(2,1)S(1)}, u32[]{:S(2)}, u32[]{:S(2)}) %collective-permute-start.32) | collective-permute-done | bytes 229408 | tf_op jit(solution)/shard_map/ppermute | solution.py:25
  91.5 1.9 %collective-permute-start.37 = (bf16[256,896]{1,0:T(8,128)(2,1)S(1)}, bf16[256,896]{1,0:T(8,128)(2,1)S(1)}, u32[]{:S(2)}, u32[]{:S(2)}) collective-permute-start(bf16[256,896]{1,0:T(8,128)(2,1)S(1)} %shard_map.125.refs_0_), channel_id=1, source_target_pairs={{0,6},{1,7},{2,4},{3,5},{4,2},{5,3},{6,0},{7,1},{8,14},{9,15},{10,... | collective-permute-start | bytes 1376264 | tf_op jit(solution)/shard_map/ppermute | solution.py:25
  93.4 1.0 collective-permute-start.35
  94.4 4.7 %collective-permute-done.33.refs_1_ = bf16[256,896]{1,0:T(8,128)(2,1)S(1)} collective-permute-done((bf16[256,896]{1,0:T(8,128)(2,1)S(1)}, bf16[256,896]{1,0:T(8,128)(2,1)S(1)}, u32[]{:S(2)}, u32[]{:S(2)}) %collective-permute-start.33) | collective-permute-done | bytes 458784 | tf_op jit(solution)/shard_map/ppermute | solution.py:25
  99.2 2.3 %collective-permute-done.34.refs_1_ = bf16[256,896]{1,0:T(8,128)(2,1)S(1)} collective-permute-done((bf16[256,896]{1,0:T(8,128)(2,1)S(1)}, bf16[256,896]{1,0:T(8,128)(2,1)S(1)}, u32[]{:S(2)}, u32[]{:S(2)}) %collective-permute-start.34) | collective-permute-done | bytes 458784 | tf_op jit(solution)/shard_map/ppermute | solution.py:25
  101.5 1.3 shard_map.128.rest_0_
  102.8 1.3 shard_map.129.rest_0_
  104.3 2.1 %collective-permute-done.37.refs_1_ = bf16[256,896]{1,0:T(8,128)(2,1)S(1)} collective-permute-done((bf16[256,896]{1,0:T(8,128)(2,1)S(1)}, bf16[256,896]{1,0:T(8,128)(2,1)S(1)}, u32[]{:S(2)}, u32[]{:S(2)}) %collective-permute-start.37) | collective-permute-done | bytes 458784 | tf_op jit(solution)/shard_map/ppermute | solution.py:25
  106.4 1.3 shard_map.133
  107.9 1.9 %collective-permute-start.40 = (bf16[128,896]{1,0:T(8,128)(2,1)S(1)}, bf16[128,896]{1,0:T(8,128)(2,1)S(1)}, u32[]{:S(2)}, u32[]{:S(2)}) collective-permute-start(bf16[128,896]{1,0:T(8,128)(2,1)S(1)} %get-tuple-element.350.refs_0_), channel_id=1, source_target_pairs={{0,6},{1,7},{2,4},{3,5},{4,2},{5,3},{6,0},{7,1},{8,14},{9,15},{10,... | collective-permute-start | bytes 688136 | tf_op jit(solution)/shard_map/ppermute | solution.py:25
  109.9 1.3 shard_map.134.refs_0_
  111.4 2.2 %collective-permute-start.42 = (bf16[64,1024]{1,0:T(8,128)(2,1)S(1)}, bf16[64,1024]{1,0:T(8,128)(2,1)S(1)}, u32[]{:S(2)}, u32[]{:S(2)}) collective-permute-start(bf16[64,1024]{1,0:T(8,128)(2,1)S(1)} %get-tuple-element.357), channel_id=1, source_target_pairs={{0,96},{8,104},{16,112},{24,120},{32,64},{40,72},{48,80},{56,88},{... | collective-permute-start | bytes 393224 | tf_op jit(solution)/shard_map/ppermute | solution.py:25
  113.5 1.9 %collective-permute-start.43 = (bf16[64,1024]{1,0:T(8,128)(2,1)S(1)}, bf16[64,1024]{1,0:T(8,128)(2,1)S(1)}, u32[]{:S(2)}, u32[]{:S(2)}) collective-permute-start(bf16[64,1024]{1,0:T(8,128)(2,1)S(1)} %get-tuple-element.358), channel_id=1, source_target_pairs={{0,64},{8,72},{16,80},{24,88},{32,96},{40,104},{48,112},{56,120},{... | collective-permute-start | bytes 393224 | tf_op jit(solution)/shard_map/ppermute | solution.py:25
  115.9 1.7 %collective-permute-start.45 = (bf16[256,896]{1,0:T(8,128)(2,1)S(1)}, bf16[256,896]{1,0:T(8,128)(2,1)S(1)}, u32[]{:S(2)}, u32[]{:S(2)}) collective-permute-start(bf16[256,896]{1,0:T(8,128)(2,1)S(1)} %shard_map.136.refs_0_), channel_id=1, source_target_pairs={{0,6},{1,7},{2,4},{3,5},{4,2},{5,3},{6,0},{7,1},{8,14},{9,15},{10,... | collective-permute-start | bytes 1376264 | tf_op jit(solution)/shard_map/ppermute | solution.py:25
  117.8 3.3 %shard_map.138 = (bf16[1024,1792]{1,0:T(8,128)(2,1)}, bf16[1024,1792]{1,0:T(8,128)(2,1)}) custom-call(s32[1]{0:T(128)} %bitcast.mine_ref.mine, bf16[8,64,1024]{2,1,0:T(8,128)(2,1)S(1)} %bitcast.15, bf16[8,64,1024]{2,1,0:T(8,128)(2,1)S(1)} %bitcast.16, bf16[512,896]{1,0:T(8,128)(2,1)S(1)} %shard_map.126.refs_2_, bf16[512,896]{1,0:T(8,128)(2,1)S(1)} %shard_map.127.refs_3_), custom_call_target="tpu_custom_call" | custom-call | flops 1 | bytes 1 | tf_op jit(solution)/shard_map/pallas_call | solution.py:50
  121.3 2.2 %collective-permute-start.44 = (f32[32,1024]{1,0:T(8,128)S(1)}, f32[32,1024]{1,0:T(8,128)S(1)}, u32[]{:S(2)}, u32[]{:S(2)}) collective-permute-start(f32[32,1024]{1,0:T(8,128)S(1)} %get-tuple-element.362), channel_id=1, source_target_pairs={{0,16},{8,24},{16,0},{24,8},{32,48},{40,56},{48,32},{56,40},{64,80... | collective-permute-start | bytes 393224 | tf_op jit(solution)/shard_map/ppermute | solution.py:25
  123.5 3.3 %shard_map.140 = (bf16[1024,1792]{1,0:T(8,128)(2,1)}, bf16[1024,1792]{1,0:T(8,128)(2,1)}) custom-call(s32[1]{0:T(128)} %bitcast.mine_ref.mine, bf16[8,64,1024]{2,1,0:T(8,128)(2,1)S(1)} %bitcast.17, bf16[8,64,1024]{2,1,0:T(8,128)(2,1)S(1)} %bitcast.18, bf16[512,896]{1,0:T(8,128)(2,1)S(1)} %shard_map.131.refs_2_, ...), custom_call_target="tpu_custom_call", output_to_operand_aliasing={{0}: (5, {}), {1}: (6, {})} | custom-call | flops 1 | bytes 1 | tf_op jit(solution)/shard_map/pallas_call | solution.py:50
  126.8 1.0 collective-permute-done.44
  128.5 0.8 collective-permute-done.45.refs_1_
  129.6 3.0 %shard_map.143 = bf16[1792,1024]{1,0:T(8,128)(2,1)} custom-call(s32[1]{0:T(128)} %bitcast.mine_ref.mine, bf16[8,64,1024]{2,1,0:T(8,128)(2,1)S(1)} %bitcast.23, bf16[8,64,1024]{2,1,0:T(8,128)(2,1)S(1)} %bitcast.24, bf16[512,896]{1,0:T(8,128)(2,1)S(1)} %shard_map.141.refs_2_, bf16[512,896]{1,0:T(8,128)(2,1)S(1)} %shard_map.142.refs_3_), custom_call_target="tpu_custom_call" | custom-call | flops 1 | bytes 1 | tf_op jit(solution)/shard_map/pallas_call | solution.py:50
  (101 shorter events, 17.0 us)
Async XLA Ops:
  0.6 6.5 %collective-permute-start = (bf16[32,1024]{1,0:T(8,128)(2,1)}, bf16[32,1024]{1,0:T(8,128)(2,1)S(1)}, u32[]{:S(2)}, u32[]{:S(2)}) collective-permute-start(bf16[32,1024]{1,0:T(8,128)(2,1)} %refs_0_.1), channel_id=1, source_target_pairs={{0,16},{8,24},{16,0},{24,8},{32,48},{40,56},{48,32},{56,40},{64,80... | collective-permute-start | bytes 196616 | tf_op jit(solution)/shard_map/ppermute | solution.py:25
  4.7 6.0 %collective-permute-start.1 = (bf16[32,1024]{1,0:T(8,128)(2,1)}, bf16[32,1024]{1,0:T(8,128)(2,1)S(1)}, u32[]{:S(2)}, u32[]{:S(2)}) collective-permute-start(bf16[32,1024]{1,0:T(8,128)(2,1)} %refs_2_.1), channel_id=1, source_target_pairs={{0,16},{8,24},{16,0},{24,8},{32,48},{40,56},{48,32},{56,40},{64,80... | collective-permute-start | bytes 196616 | tf_op jit(solution)/shard_map/ppermute | solution.py:25
  4.8 2.0 %copy-start = (bf16[1024,1792]{1,0:T(8,128)(2,1)S(1)}, bf16[1024,1792]{1,0:T(8,128)(2,1)}, u32[]{:S(2)}) copy-start(bf16[1024,1792]{1,0:T(8,128)(2,1)} %w_ref.3) | copy-start | bytes 11010052
  6.8 3.9 %copy-start.3 = (bf16[32,1024]{1,0:T(8,128)(2,1)S(1)}, bf16[32,1024]{1,0:T(8,128)(2,1)}, u32[]{:S(2)}) copy-start(bf16[32,1024]{1,0:T(8,128)(2,1)} %refs_0_.1) | copy-start | bytes 196612
  6.8 3.9 %copy-start.4 = (bf16[32,1024]{1,0:T(8,128)(2,1)S(1)}, bf16[32,1024]{1,0:T(8,128)(2,1)}, u32[]{:S(2)}) copy-start(bf16[32,1024]{1,0:T(8,128)(2,1)} %refs_2_.1) | copy-start | bytes 196612
  6.8 8.2 %copy-start.1 = (bf16[1024,1792]{1,0:T(8,128)(2,1)S(1)}, bf16[1024,1792]{1,0:T(8,128)(2,1)}, u32[]{:S(2)}) copy-start(bf16[1024,1792]{1,0:T(8,128)(2,1)} %w_ref.4) | copy-start | bytes 11010052
  10.7 15.4 %copy-start.2 = (bf16[1792,1024]{1,0:T(8,128)(2,1)S(1)}, bf16[1792,1024]{1,0:T(8,128)(2,1)}, u32[]{:S(2)}) copy-start(bf16[1792,1024]{1,0:T(8,128)(2,1)} %w_ref.5) | copy-start | bytes 11010052
  10.7 9.3 %collective-permute-start.2 = (bf16[128,1024]{1,0:T(8,128)(2,1)S(1)}, bf16[128,1024]{1,0:T(8,128)(2,1)S(1)}, u32[]{:S(2)}, u32[]{:S(2)}) collective-permute-start(bf16[128,1024]{1,0:T(8,128)(2,1)S(1)} %shard_map.85.refs_0_), channel_id=1, source_target_pairs={{0,32},{8,40},{16,48},{24,56},{32,0},{40,8},{48,16},{56,24},{64,96... | collective-permute-start | bytes 786440 | tf_op jit(solution)/shard_map/ppermute | solution.py:25
  12.3 13.2 %collective-permute-start.3 = (bf16[128,1024]{1,0:T(8,128)(2,1)S(1)}, bf16[128,1024]{1,0:T(8,128)(2,1)S(1)}, u32[]{:S(2)}, u32[]{:S(2)}) collective-permute-start(bf16[128,1024]{1,0:T(8,128)(2,1)S(1)} %shard_map.85.refs_0_), channel_id=1, source_target_pairs={{0,96},{8,104},{16,112},{24,120},{32,64},{40,72},{48,80},{56,88},{... | collective-permute-start | bytes 786440 | tf_op jit(solution)/shard_map/ppermute | solution.py:25
  14.4 11.1 %collective-permute-start.4 = (bf16[128,1024]{1,0:T(8,128)(2,1)S(1)}, bf16[128,1024]{1,0:T(8,128)(2,1)S(1)}, u32[]{:S(2)}, u32[]{:S(2)}) collective-permute-start(bf16[128,1024]{1,0:T(8,128)(2,1)S(1)} %shard_map.85.refs_0_), channel_id=1, source_target_pairs={{0,64},{8,72},{16,80},{24,88},{32,96},{40,104},{48,112},{56,120},{... | collective-permute-start | bytes 786440 | tf_op jit(solution)/shard_map/ppermute | solution.py:25
  25.5 2.0 %collective-permute-start.5 = (bf16[256,1024]{1,0:T(8,128)(2,1)S(1)}, bf16[256,1024]{1,0:T(8,128)(2,1)S(1)}, u32[]{:S(2)}, u32[]{:S(2)}) collective-permute-start(bf16[256,1024]{1,0:T(8,128)(2,1)S(1)} %get-tuple-element.199.refs_0_), channel_id=1, source_target_pairs={{0,8},{8,0},{16,24},{24,16},{32,40},{40,32},{48,56},{56,48},{64,72... | collective-permute-start | bytes 1572872 | tf_op jit(solution)/shard_map/ppermute | solution.py:25
  25.6 7.3 %collective-permute-start.6 = (bf16[256,1024]{1,0:T(8,128)(2,1)S(1)}, bf16[256,1024]{1,0:T(8,128)(2,1)S(1)}, u32[]{:S(2)}, u32[]{:S(2)}) collective-permute-start(bf16[256,1024]{1,0:T(8,128)(2,1)S(1)} %get-tuple-element.206.refs_0_), channel_id=1, source_target_pairs={{0,8},{8,0},{16,24},{24,16},{32,40},{40,32},{48,56},{56,48},{64,72... | collective-permute-start | bytes 1572872 | tf_op jit(solution)/shard_map/ppermute | solution.py:25
  28.3 13.4 %collective-permute-start.7 = (bf16[256,896]{1,0:T(8,128)(2,1)S(1)}, bf16[256,896]{1,0:T(8,128)(2,1)S(1)}, u32[]{:S(2)}, u32[]{:S(2)}) collective-permute-start(bf16[256,896]{1,0:T(8,128)(2,1)S(1)} %shard_map.90), channel_id=1, source_target_pairs={{0,2},{1,3},{2,0},{3,1},{4,6},{5,7},{6,4},{7,5},{8,10},{9,11},{10,... | collective-permute-start | bytes 1376264 | tf_op jit(solution)/shard_map/ppermute | solution.py:25
  30.7 14.7 %collective-permute-start.8 = (bf16[256,896]{1,0:T(8,128)(2,1)S(1)}, bf16[256,896]{1,0:T(8,128)(2,1)S(1)}, u32[]{:S(2)}, u32[]{:S(2)}) collective-permute-start(bf16[256,896]{1,0:T(8,128)(2,1)S(1)} %shard_map.91), channel_id=1, source_target_pairs={{0,6},{1,7},{2,4},{3,5},{4,2},{5,3},{6,0},{7,1},{8,14},{9,15},{10,... | collective-permute-start | bytes 1376264 | tf_op jit(solution)/shard_map/ppermute | solution.py:25
  33.8 14.6 %collective-permute-start.9 = (bf16[256,896]{1,0:T(8,128)(2,1)S(1)}, bf16[256,896]{1,0:T(8,128)(2,1)S(1)}, u32[]{:S(2)}, u32[]{:S(2)}) collective-permute-start(bf16[256,896]{1,0:T(8,128)(2,1)S(1)} %shard_map.93), channel_id=1, source_target_pairs={{0,1},{1,0},{2,3},{3,2},{4,5},{5,4},{6,7},{7,6},{8,9},{9,8},{10,11... | collective-permute-start | bytes 1376264 | tf_op jit(solution)/shard_map/ppermute | solution.py:25
  35.6 15.2 %collective-permute-start.10 = (bf16[256,896]{1,0:T(8,128)(2,1)S(1)}, bf16[256,896]{1,0:T(8,128)(2,1)S(1)}, u32[]{:S(2)}, u32[]{:S(2)}) collective-permute-start(bf16[256,896]{1,0:T(8,128)(2,1)S(1)} %shard_map.94), channel_id=1, source_target_pairs={{0,2},{1,3},{2,0},{3,1},{4,6},{5,7},{6,4},{7,5},{8,10},{9,11},{10,... | collective-permute-start | bytes 1376264 | tf_op jit(solution)/shard_map/ppermute | solution.py:25
  39.2 16.0 %collective-permute-start.11 = (bf16[256,896]{1,0:T(8,128)(2,1)S(1)}, bf16[256,896]{1,0:T(8,128)(2,1)S(1)}, u32[]{:S(2)}, u32[]{:S(2)}) collective-permute-start(bf16[256,896]{1,0:T(8,128)(2,1)S(1)} %shard_map.95), channel_id=1, source_target_pairs={{0,6},{1,7},{2,4},{3,5},{4,2},{5,3},{6,0},{7,1},{8,14},{9,15},{10,... | collective-permute-start | bytes 1376264 | tf_op jit(solution)/shard_map/ppermute | solution.py:25
  41.7 15.7 %collective-permute-start.12 = (bf16[256,896]{1,0:T(8,128)(2,1)S(1)}, bf16[256,896]{1,0:T(8,128)(2,1)S(1)}, u32[]{:S(2)}, u32[]{:S(2)}) collective-permute-start(bf16[256,896]{1,0:T(8,128)(2,1)S(1)} %shard_map.100), channel_id=1, source_target_pairs={{0,1},{1,0},{2,3},{3,2},{4,5},{5,4},{6,7},{7,6},{8,9},{9,8},{10,11... | collective-permute-start | bytes 1376264 | tf_op jit(solution)/shard_map/ppermute | solution.py:25
  45.4 14.7 %collective-permute-start.13 = (bf16[128,896]{1,0:T(8,128)(2,1)S(1)}, bf16[128,896]{1,0:T(8,128)(2,1)S(1)}, u32[]{:S(2)}, u32[]{:S(2)}) collective-permute-start(bf16[128,896]{1,0:T(8,128)(2,1)S(1)} %get-tuple-element.251), channel_id=1, source_target_pairs={{0,6},{1,7},{2,4},{3,5},{4,2},{5,3},{6,0},{7,1},{8,14},{9,15},{10,... | collective-permute-start | bytes 688136 | tf_op jit(solution)/shard_map/ppermute | solution.py:25
  48.3 13.7 %collective-permute-start.14 = (bf16[128,896]{1,0:T(8,128)(2,1)S(1)}, bf16[128,896]{1,0:T(8,128)(2,1)S(1)}, u32[]{:S(2)}, u32[]{:S(2)}) collective-permute-start(bf16[128,896]{1,0:T(8,128)(2,1)S(1)} %get-tuple-element.256), channel_id=1, source_target_pairs={{0,1},{1,0},{2,3},{3,2},{4,5},{5,4},{6,7},{7,6},{8,9},{9,8},{10,11... | collective-permute-start | bytes 688136 | tf_op jit(solution)/shard_map/ppermute | solution.py:25
  50.8 11.3 %collective-permute-start.15 = (bf16[128,896]{1,0:T(8,128)(2,1)S(1)}, bf16[128,896]{1,0:T(8,128)(2,1)S(1)}, u32[]{:S(2)}, u32[]{:S(2)}) collective-permute-start(bf16[128,896]{1,0:T(8,128)(2,1)S(1)} %get-tuple-element.261), channel_id=1, source_target_pairs={{0,2},{1,3},{2,0},{3,1},{4,6},{5,7},{6,4},{7,5},{8,10},{9,11},{10,... | collective-permute-start | bytes 688136 | tf_op jit(solution)/shard_map/ppermute | solution.py:25
  55.2 9.3 %collective-permute-start.16 = (bf16[128,896]{1,0:T(8,128)(2,1)S(1)}, bf16[128,896]{1,0:T(8,128)(2,1)S(1)}, u32[]{:S(2)}, u32[]{:S(2)}) collective-permute-start(bf16[128,896]{1,0:T(8,128)(2,1)S(1)} %get-tuple-element.266), channel_id=1, source_target_pairs={{0,6},{1,7},{2,4},{3,5},{4,2},{5,3},{6,0},{7,1},{8,14},{9,15},{10,... | collective-permute-start | bytes 688136 | tf_op jit(solution)/shard_map/ppermute | solution.py:25
  57.5 8.1 %collective-permute-start.17 = (bf16[128,896]{1,0:T(8,128)(2,1)S(1)}, bf16[128,896]{1,0:T(8,128)(2,1)S(1)}, u32[]{:S(2)}, u32[]{:S(2)}) collective-permute-start(bf16[128,896]{1,0:T(8,128)(2,1)S(1)} %get-tuple-element.271), channel_id=1, source_target_pairs={{0,1},{1,0},{2,3},{3,2},{4,5},{5,4},{6,7},{7,6},{8,9},{9,8},{10,11... | collective-permute-start | bytes 688136 | tf_op jit(solution)/shard_map/ppermute | solution.py:25
  60.1 6.6 %collective-permute-start.18 = (bf16[128,896]{1,0:T(8,128)(2,1)S(1)}, bf16[128,896]{1,0:T(8,128)(2,1)S(1)}, u32[]{:S(2)}, u32[]{:S(2)}) collective-permute-start(bf16[128,896]{1,0:T(8,128)(2,1)S(1)} %get-tuple-element.276), channel_id=1, source_target_pairs={{0,2},{1,3},{2,0},{3,1},{4,6},{5,7},{6,4},{7,5},{8,10},{9,11},{10,... | collective-permute-start | bytes 688136 | tf_op jit(solution)/shard_map/ppermute | solution.py:25
  62.1 6.9 %collective-permute-start.21 = (bf16[64,896]{1,0:T(8,128)(2,1)S(1)}, bf16[64,896]{1,0:T(8,128)(2,1)S(1)}, u32[]{:S(2)}, u32[]{:S(2)}) collective-permute-start(bf16[64,896]{1,0:T(8,128)(2,1)S(1)} %get-tuple-element.285), channel_id=1, source_target_pairs={{0,6},{1,7},{2,4},{3,5},{4,2},{5,3},{6,0},{7,1},{8,14},{9,15},{10,... | collective-permute-start | bytes 344072 | tf_op jit(solution)/shard_map/ppermute | solution.py:25
  63.3 6.7 %collective-permute-start.20 = (bf16[64,896]{1,0:T(8,128)(2,1)S(1)}, bf16[64,896]{1,0:T(8,128)(2,1)S(1)}, u32[]{:S(2)}, u32[]{:S(2)}) collective-permute-start(bf16[64,896]{1,0:T(8,128)(2,1)S(1)} %get-tuple-element.283), channel_id=1, source_target_pairs={{0,2},{1,3},{2,0},{3,1},{4,6},{5,7},{6,4},{7,5},{8,10},{9,11},{10,... | collective-permute-start | bytes 344072 | tf_op jit(solution)/shard_map/ppermute | solution.py:25
  64.5 5.7 %collective-permute-start.19 = (bf16[64,896]{1,0:T(8,128)(2,1)S(1)}, bf16[64,896]{1,0:T(8,128)(2,1)S(1)}, u32[]{:S(2)}, u32[]{:S(2)}) collective-permute-start(bf16[64,896]{1,0:T(8,128)(2,1)S(1)} %get-tuple-element.281), channel_id=1, source_target_pairs={{0,1},{1,0},{2,3},{3,2},{4,5},{5,4},{6,7},{7,6},{8,9},{9,8},{10,11... | collective-permute-start | bytes 344072 | tf_op jit(solution)/shard_map/ppermute | solution.py:25
  66.7 6.9 %collective-permute-start.24 = (bf16[64,896]{1,0:T(8,128)(2,1)S(1)}, bf16[64,896]{1,0:T(8,128)(2,1)S(1)}, u32[]{:S(2)}, u32[]{:S(2)}) collective-permute-start(bf16[64,896]{1,0:T(8,128)(2,1)S(1)} %get-tuple-element.295), channel_id=1, source_target_pairs={{0,6},{1,7},{2,4},{3,5},{4,2},{5,3},{6,0},{7,1},{8,14},{9,15},{10,... | collective-permute-start | bytes 344072 | tf_op jit(solution)/shard_map/ppermute | solution.py:25
  69.0 4.8 %collective-permute-start.23 = (bf16[64,896]{1,0:T(8,128)(2,1)S(1)}, bf16[64,896]{1,0:T(8,128)(2,1)S(1)}, u32[]{:S(2)}, u32[]{:S(2)}) collective-permute-start(bf16[64,896]{1,0:T(8,128)(2,1)S(1)} %get-tuple-element.293), channel_id=1, source_target_pairs={{0,2},{1,3},{2,0},{3,1},{4,6},{5,7},{6,4},{7,5},{8,10},{9,11},{10,... | collective-permute-start | bytes 344072 | tf_op jit(solution)/shard_map/ppermute | solution.py:25
  69.0 5.0 %collective-permute-start.22 = (bf16[64,896]{1,0:T(8,128)(2,1)S(1)}, bf16[64,896]{1,0:T(8,128)(2,1)S(1)}, u32[]{:S(2)}, u32[]{:S(2)}) collective-permute-start(bf16[64,896]{1,0:T(8,128)(2,1)S(1)} %get-tuple-element.291), channel_id=1, source_target_pairs={{0,1},{1,0},{2,3},{3,2},{4,5},{5,4},{6,7},{7,6},{8,9},{9,8},{10,11... | collective-permute-start | bytes 344072 | tf_op jit(solution)/shard_map/ppermute | solution.py:25
  70.4 6.5 %collective-permute-start.25 = (bf16[64,896]{1,0:T(8,128)(2,1)S(1)}, bf16[64,896]{1,0:T(8,128)(2,1)S(1)}, u32[]{:S(2)}, u32[]{:S(2)}) collective-permute-start(bf16[64,896]{1,0:T(8,128)(2,1)S(1)} %get-tuple-element.300.refs_0_), channel_id=1, source_target_pairs={{0,6},{1,7},{2,4},{3,5},{4,2},{5,3},{6,0},{7,1},{8,14},{9,15},{10,... | collective-permute-start | bytes 344072 | tf_op jit(solution)/shard_map/ppermute | solution.py:25
  72.6 6.0 %collective-permute-start.26 = (bf16[64,896]{1,0:T(8,128)(2,1)S(1)}, bf16[64,896]{1,0:T(8,128)(2,1)S(1)}, u32[]{:S(2)}, u32[]{:S(2)}) collective-permute-start(bf16[64,896]{1,0:T(8,128)(2,1)S(1)} %get-tuple-element.302.refs_0_), channel_id=1, source_target_pairs={{0,1},{1,0},{2,3},{3,2},{4,5},{5,4},{6,7},{7,6},{8,9},{9,8},{10,11... | collective-permute-start | bytes 344072 | tf_op jit(solution)/shard_map/ppermute | solution.py:25
  74.2 6.1 %collective-permute-start.27 = (bf16[64,896]{1,0:T(8,128)(2,1)S(1)}, bf16[64,896]{1,0:T(8,128)(2,1)S(1)}, u32[]{:S(2)}, u32[]{:S(2)}) collective-permute-start(bf16[64,896]{1,0:T(8,128)(2,1)S(1)} %get-tuple-element.304.refs_0_), channel_id=1, source_target_pairs={{0,6},{1,7},{2,4},{3,5},{4,2},{5,3},{6,0},{7,1},{8,14},{9,15},{10,... | collective-permute-start | bytes 344072 | tf_op jit(solution)/shard_map/ppermute | solution.py:25
  75.8 5.6 %collective-permute-start.28 = (bf16[64,896]{1,0:T(8,128)(2,1)S(1)}, bf16[64,896]{1,0:T(8,128)(2,1)S(1)}, u32[]{:S(2)}, u32[]{:S(2)}) collective-permute-start(bf16[64,896]{1,0:T(8,128)(2,1)S(1)} %get-tuple-element.306.refs_0_), channel_id=1, source_target_pairs={{0,2},{1,3},{2,0},{3,1},{4,6},{5,7},{6,4},{7,5},{8,10},{9,11},{10,... | collective-permute-start | bytes 344072 | tf_op jit(solution)/shard_map/ppermute | solution.py:25
  76.9 8.6 %collective-permute-start.29 = (bf16[128,896]{1,0:T(8,128)(2,1)S(1)}, bf16[128,896]{1,0:T(8,128)(2,1)S(1)}, u32[]{:S(2)}, u32[]{:S(2)}) collective-permute-start(bf16[128,896]{1,0:T(8,128)(2,1)S(1)} %shard_map.117.refs_0_), channel_id=1, source_target_pairs={{0,1},{1,0},{2,3},{3,2},{4,5},{5,4},{6,7},{7,6},{8,9},{9,8},{10,11... | collective-permute-start | bytes 688136 | tf_op jit(solution)/shard_map/ppermute | solution.py:25
  78.6 8.6 %collective-permute-start.30 = (bf16[128,896]{1,0:T(8,128)(2,1)S(1)}, bf16[128,896]{1,0:T(8,128)(2,1)S(1)}, u32[]{:S(2)}, u32[]{:S(2)}) collective-permute-start(bf16[128,896]{1,0:T(8,128)(2,1)S(1)} %shard_map.118.refs_0_), channel_id=1, source_target_pairs={{0,2},{1,3},{2,0},{3,1},{4,6},{5,7},{6,4},{7,5},{8,10},{9,11},{10,... | collective-permute-start | bytes 688136 | tf_op jit(solution)/shard_map/ppermute | solution.py:25
  80.3 8.7 %collective-permute-start.31 = (bf16[128,896]{1,0:T(8,128)(2,1)S(1)}, bf16[128,896]{1,0:T(8,128)(2,1)S(1)}, u32[]{:S(2)}, u32[]{:S(2)}) collective-permute-start(bf16[128,896]{1,0:T(8,128)(2,1)S(1)} %shard_map.119.refs_0_), channel_id=1, source_target_pairs={{0,1},{1,0},{2,3},{3,2},{4,5},{5,4},{6,7},{7,6},{8,9},{9,8},{10,11... | collective-permute-start | bytes 688136 | tf_op jit(solution)/shard_map/ppermute | solution.py:25
  81.4 10.0 %collective-permute-start.32 = (bf16[128,896]{1,0:T(8,128)(2,1)S(1)}, bf16[128,896]{1,0:T(8,128)(2,1)S(1)}, u32[]{:S(2)}, u32[]{:S(2)}) collective-permute-start(bf16[128,896]{1,0:T(8,128)(2,1)S(1)} %shard_map.120.refs_0_), channel_id=1, source_target_pairs={{0,1},{1,0},{2,3},{3,2},{4,5},{5,4},{6,7},{7,6},{8,9},{9,8},{10,11... | collective-permute-start | bytes 688136 | tf_op jit(solution)/shard_map/ppermute | solution.py:25
  85.5 13.5 %collective-permute-start.33 = (bf16[256,896]{1,0:T(8,128)(2,1)S(1)}, bf16[256,896]{1,0:T(8,128)(2,1)S(1)}, u32[]{:S(2)}, u32[]{:S(2)}) collective-permute-start(bf16[256,896]{1,0:T(8,128)(2,1)S(1)} %shard_map.122.refs_0_), channel_id=1, source_target_pairs={{0,2},{1,3},{2,0},{3,1},{4,6},{5,7},{6,4},{7,5},{8,10},{9,11},{10,... | collective-permute-start | bytes 1376264 | tf_op jit(solution)/shard_map/ppermute | solution.py:25
  87.2 14.2 %collective-permute-start.34 = (bf16[256,896]{1,0:T(8,128)(2,1)S(1)}, bf16[256,896]{1,0:T(8,128)(2,1)S(1)}, u32[]{:S(2)}, u32[]{:S(2)}) collective-permute-start(bf16[256,896]{1,0:T(8,128)(2,1)S(1)} %shard_map.123.refs_0_), channel_id=1, source_target_pairs={{0,6},{1,7},{2,4},{3,5},{4,2},{5,3},{6,0},{7,1},{8,14},{9,15},{10,... | collective-permute-start | bytes 1376264 | tf_op jit(solution)/shard_map/ppermute | solution.py:25
  89.0 15.1 %collective-permute-start.36 = (bf16[256,896]{1,0:T(8,128)(2,1)S(1)}, bf16[256,896]{1,0:T(8,128)(2,1)S(1)}, u32[]{:S(2)}, u32[]{:S(2)}) collective-permute-start(bf16[256,896]{1,0:T(8,128)(2,1)S(1)} %shard_map.124.refs_0_), channel_id=1, source_target_pairs={{0,2},{1,3},{2,0},{3,1},{4,6},{5,7},{6,4},{7,5},{8,10},{9,11},{10,... | collective-permute-start | bytes 1376264 | tf_op jit(solution)/shard_map/ppermute | solution.py:25
  91.5 14.9 %collective-permute-start.37 = (bf16[256,896]{1,0:T(8,128)(2,1)S(1)}, bf16[256,896]{1,0:T(8,128)(2,1)S(1)}, u32[]{:S(2)}, u32[]{:S(2)}) collective-permute-start(bf16[256,896]{1,0:T(8,128)(2,1)S(1)} %shard_map.125.refs_0_), channel_id=1, source_target_pairs={{0,6},{1,7},{2,4},{3,5},{4,2},{5,3},{6,0},{7,1},{8,14},{9,15},{10,... | collective-permute-start | bytes 1376264 | tf_op jit(solution)/shard_map/ppermute | solution.py:25
  93.4 10.8 %collective-permute-start.35 = (bf16[64,1792]{1,0:T(8,128)(2,1)S(1)}, bf16[64,1792]{1,0:T(8,128)(2,1)S(1)}, u32[]{:S(2)}, u32[]{:S(2)}) collective-permute-start(bf16[64,1792]{1,0:T(8,128)(2,1)S(1)} %shard_map.121.refs_0_), channel_id=1, source_target_pairs={{0,1},{1,0},{2,3},{3,2},{4,5},{5,4},{6,7},{7,6},{8,9},{9,8},{10,11... | collective-permute-start | bytes 688136 | tf_op jit(solution)/shard_map/ppermute | solution.py:25
  107.7 3.4 %collective-permute-start.38 = (f32[256,1024]{1,0:T(8,128)S(1)}, f32[256,1024]{1,0:T(8,128)S(1)}, u32[]{:S(2)}, u32[]{:S(2)}) collective-permute-start(f32[256,1024]{1,0:T(8,128)S(1)} %shard_map.133), channel_id=1, source_target_pairs={{0,8},{8,0},{16,24},{24,16},{32,40},{40,32},{48,56},{56,48},{64,72... | collective-permute-start | bytes 3145736 | tf_op jit(solution)/shard_map/ppermute | solution.py:25
  107.8 8.0 %collective-permute-start.39 = (bf16[128,896]{1,0:T(8,128)(2,1)S(1)}, bf16[128,896]{1,0:T(8,128)(2,1)S(1)}, u32[]{:S(2)}, u32[]{:S(2)}) collective-permute-start(bf16[128,896]{1,0:T(8,128)(2,1)S(1)} %get-tuple-element.348.refs_0_), channel_id=1, source_target_pairs={{0,2},{1,3},{2,0},{3,1},{4,6},{5,7},{6,4},{7,5},{8,10},{9,11},{10,... | collective-permute-start | bytes 688136 | tf_op jit(solution)/shard_map/ppermute | solution.py:25
  107.9 9.7 %collective-permute-start.40 = (bf16[128,896]{1,0:T(8,128)(2,1)S(1)}, bf16[128,896]{1,0:T(8,128)(2,1)S(1)}, u32[]{:S(2)}, u32[]{:S(2)}) collective-permute-start(bf16[128,896]{1,0:T(8,128)(2,1)S(1)} %get-tuple-element.350.refs_0_), channel_id=1, source_target_pairs={{0,6},{1,7},{2,4},{3,5},{4,2},{5,3},{6,0},{7,1},{8,14},{9,15},{10,... | collective-permute-start | bytes 688136 | tf_op jit(solution)/shard_map/ppermute | solution.py:25
  111.3 9.9 %collective-permute-start.41 = (bf16[64,1024]{1,0:T(8,128)(2,1)S(1)}, bf16[64,1024]{1,0:T(8,128)(2,1)S(1)}, u32[]{:S(2)}, u32[]{:S(2)}) collective-permute-start(bf16[64,1024]{1,0:T(8,128)(2,1)S(1)} %get-tuple-element.356), channel_id=1, source_target_pairs={{0,32},{8,40},{16,48},{24,56},{32,0},{40,8},{48,16},{56,24},{64,96... | collective-permute-start | bytes 393224 | tf_op jit(solution)/shard_map/ppermute | solution.py:25
  111.4 9.8 %collective-permute-start.42 = (bf16[64,1024]{1,0:T(8,128)(2,1)S(1)}, bf16[64,1024]{1,0:T(8,128)(2,1)S(1)}, u32[]{:S(2)}, u32[]{:S(2)}) collective-permute-start(bf16[64,1024]{1,0:T(8,128)(2,1)S(1)} %get-tuple-element.357), channel_id=1, source_target_pairs={{0,96},{8,104},{16,112},{24,120},{32,64},{40,72},{48,80},{56,88},{... | collective-permute-start | bytes 393224 | tf_op jit(solution)/shard_map/ppermute | solution.py:25
  113.5 7.7 %collective-permute-start.43 = (bf16[64,1024]{1,0:T(8,128)(2,1)S(1)}, bf16[64,1024]{1,0:T(8,128)(2,1)S(1)}, u32[]{:S(2)}, u32[]{:S(2)}) collective-permute-start(bf16[64,1024]{1,0:T(8,128)(2,1)S(1)} %get-tuple-element.358), channel_id=1, source_target_pairs={{0,64},{8,72},{16,80},{24,88},{32,96},{40,104},{48,112},{56,120},{... | collective-permute-start | bytes 393224 | tf_op jit(solution)/shard_map/ppermute | solution.py:25
  115.9 13.4 %collective-permute-start.45 = (bf16[256,896]{1,0:T(8,128)(2,1)S(1)}, bf16[256,896]{1,0:T(8,128)(2,1)S(1)}, u32[]{:S(2)}, u32[]{:S(2)}) collective-permute-start(bf16[256,896]{1,0:T(8,128)(2,1)S(1)} %shard_map.136.refs_0_), channel_id=1, source_target_pairs={{0,6},{1,7},{2,4},{3,5},{4,2},{5,3},{6,0},{7,1},{8,14},{9,15},{10,... | collective-permute-start | bytes 1376264 | tf_op jit(solution)/shard_map/ppermute | solution.py:25
  117.6 11.9 %collective-permute-start.46 = (bf16[256,896]{1,0:T(8,128)(2,1)S(1)}, bf16[256,896]{1,0:T(8,128)(2,1)S(1)}, u32[]{:S(2)}, u32[]{:S(2)}) collective-permute-start(bf16[256,896]{1,0:T(8,128)(2,1)S(1)} %shard_map.137.refs_0_), channel_id=1, source_target_pairs={{0,2},{1,3},{2,0},{3,1},{4,6},{5,7},{6,4},{7,5},{8,10},{9,11},{10,... | collective-permute-start | bytes 1376264 | tf_op jit(solution)/shard_map/ppermute | solution.py:25
  121.3 6.6 %collective-permute-start.44 = (f32[32,1024]{1,0:T(8,128)S(1)}, f32[32,1024]{1,0:T(8,128)S(1)}, u32[]{:S(2)}, u32[]{:S(2)}) collective-permute-start(f32[32,1024]{1,0:T(8,128)S(1)} %get-tuple-element.362), channel_id=1, source_target_pairs={{0,16},{8,24},{16,0},{24,8},{32,48},{40,56},{48,32},{56,40},{64,80... | collective-permute-start | bytes 393224 | tf_op jit(solution)/shard_map/ppermute | solution.py:25
